TPU v7x, 256 devices: a whole 4x4x8 slice. The times are simulated.
256 devices in a mesh: dp: 64 (over z, y, core), mp: 4 (over x).
Axes of the slice: x: 4, y: 4, z: 8, core: 2. Of those that a mesh axis runs over, the one named last changes fastest.
Arguments:
- grads: bfloat16 [64, 32, 512, 512], P('dp', None, None, 'mp'), may hold values from -600 to 600
- owner: int32 [32], replicated, may hold values from 0 to 63, as said below
Outputs:
- updates: bfloat16 [128, 512, 512], P('dp', None, 'mp')
Inputs may be any that keep to these rules, and one draw needn't show every extreme that they name: `owner`: each entry is an index of dp. Each index of dp owns at most 2 blocks, and at least one owns exactly 2.
All inputs are finite; a program needn't handle non-finite values.
Results may differ from a plain program's by a relative error of at most 0.012.
The roundings to bfloat16 on the way count: a program that leaves them out, or rounds other values in their place, can miss the bound.
Values may be sent and summed in bfloat16 or wider, within the bound.
No kernel may reach another device: no remote copies, remote signals or barrier semaphores. Data moves between devices by JAX's collectives and lax.ppermute only.
A program may use at most 192 MiB of HBM per device.

v0:
```python
import math

import jax
import jax.numpy as jnp
from jax import lax
from jax.sharding import PartitionSpec as P

ITERS = 3
MOST = 2


def selection(target, slot_rank, capacity, devices):
    slot_index = jnp.arange(capacity * devices, dtype=jnp.int32)
    want_slot = slot_index // devices
    want_device = slot_index % devices
    matches = (slot_rank[None, :] == want_slot[:, None]) & (target[None, :] == want_device[:, None])
    return matches.astype(jnp.bfloat16)


def inverse_roots(statistics):
    extent = statistics.shape[1]
    identity = jnp.eye(extent, dtype=jnp.float32)
    scaling = 2.5 / jnp.sqrt(jnp.sum(statistics * statistics, axis=(1, 2), keepdims=True) + 1e-06)
    root_now = (scaling**0.25 * identity).astype(jnp.bfloat16)
    moment = (scaling * statistics).astype(jnp.bfloat16)
    for iteration in range(ITERS):
        factor = ((5.0 * identity - moment.astype(jnp.float32)) / 4.0).astype(jnp.bfloat16)
        root_now = jnp.einsum(
            "cij,cjk->cik", root_now, factor, preferred_element_type=jnp.float32
        ).astype(jnp.bfloat16)
        square = jnp.einsum(
            "cij,cjk->cik", factor, factor, preferred_element_type=jnp.float32
        ).astype(jnp.bfloat16)
        fourth = jnp.einsum(
            "cij,cjk->cik", square, square, preferred_element_type=jnp.float32
        ).astype(jnp.bfloat16)
        moment = jnp.einsum(
            "cij,cjk->cik", fourth, moment, preferred_element_type=jnp.float32
        ).astype(jnp.bfloat16)
    return root_now


def precondition(owned_blocks):
    full_block = lax.all_gather(owned_blocks, "mp", axis=2, tiled=True)
    slot_count, extent, columns = owned_blocks.shape
    column_start = lax.axis_index("mp") * columns
    left_stat = jnp.einsum(
        "cij,ckj->cik", full_block, full_block, preferred_element_type=jnp.float32
    )
    right_stat = jnp.einsum(
        "cji,cjk->cik", full_block, full_block, preferred_element_type=jnp.float32
    )
    both_roots = inverse_roots(jnp.concatenate([left_stat, right_stat], axis=0))
    left_root = both_roots[:slot_count]
    right_root = both_roots[slot_count:]
    right_columns = lax.dynamic_slice_in_dim(right_root, column_start, columns, 2)
    right_half = jnp.einsum(
        "cij,cjk->cik", full_block, right_columns, preferred_element_type=jnp.float32
    ).astype(jnp.bfloat16)
    product = jnp.einsum("cij,cjk->cik", left_root, right_half, preferred_element_type=jnp.float32)
    return (math.sqrt(extent) * product).astype(jnp.bfloat16)


def on_device(grads, owner):
    local_grads = grads[0]
    block_count, extent, columns = local_grads.shape
    devices = lax.axis_size("dp")
    stripe = extent // devices
    positions = jnp.arange(block_count, dtype=jnp.int32)
    earlier = (owner[None, :] == owner[:, None]) & (positions[None, :] < positions[:, None])
    owner_rank = jnp.sum(earlier.astype(jnp.int32), axis=1)
    capacity = MOST
    summed = lax.psum_scatter(
        local_grads.astype(jnp.float32), "dp", scatter_dimension=1, tiled=True
    )
    mean_rows = (summed / devices).astype(jnp.bfloat16).reshape(block_count, stripe * columns)
    outgoing = jnp.dot(
        selection(owner, owner_rank, capacity, devices),
        mean_rows,
        preferred_element_type=jnp.float32,
    )
    outgoing = outgoing.astype(jnp.bfloat16).reshape(capacity, devices, stripe * columns)
    arrived = lax.all_to_all(outgoing, "dp", split_axis=1, concat_axis=1, tiled=True)
    owned_blocks = arrived.reshape(capacity, extent, columns)
    result = precondition(owned_blocks)
    return result


def solution(mesh):
    placed = (P("dp", None, None, "mp"), P())
    return jax.shard_map(
        on_device, mesh=mesh, in_specs=placed, out_specs=P("dp", None, "mp"), check_vma=False
    )
```

profile of v0, /device:TPU:1, one launch (start us, length us, event | category | flops | bytes accessed | tf_op | source)
XLA Modules:
  0.0 259.8 jit_solution(8408981134143692026)
XLA Ops:
  6.5 6.4 %bitcast_convert_fusion = f32[32,512,128]{2,1,0:T(8,128)} fusion(bf16[1,32,512,128]{3,2,1,0:T(8,128)(2,1)} %param.2), kind=kLoop, calls=%fused_computation.1 | loop fusion | flops 2097152 | bytes 12582912 | tf_op jit(solution)/shard_map/convert_element_type | solution.py:74
  13.0 0.6 copy-done.2
  13.8 150.2 %reduce-scatter.2.cloned.1.call-done = f32[32,8,128]{2,1,0:T(8,128)} async-done(((f32[32,512,128]{2,1,0:T(8,128)}), f32[32,8,128]{2,1,0:T(8,128)}) %reduce-scatter.2.cloned.1.call-update) | async-done | bytes 131088 | tf_op jit(solution)/shard_map/reduce_scatter | solution.py:73
  163.9 0.9 multiply_convert_fusion.19
  164.9 0.3 convolution_convert_fusion
  165.1 0.3 copy.7
  165.4 24.9 %all_to_all.5 = bf16[2,64,1024]{2,0,1:T(2,128)(2,1)S(1)} all-to-all(bf16[2,64,1024]{2,0,1:T(2,128)(2,1)S(1)} %copy.7), channel_id=1, replica_groups=mesh['dp'=64,'mp'=4] {'dp'}, dimensions={1} | all-to-all | bytes 524288 | tf_op jit(solution)/shard_map/all_to_all | solution.py:83
  190.4 0.8 reshape.63
  191.2 1.1 fusion.32
  192.3 1.1 fusion.33
  193.4 20.7 %all-gather.2.cloned.1.call-done = bf16[2,512,512]{2,1,0:T(8,128)(2,1)} async-done(((bf16[2,512,128]{2,1,0:T(8,128)(2,1)}), bf16[2,512,512]{2,1,0:T(8,128)(2,1)}) %all-gather.2.cloned.1.call-update) | async-done | bytes 1048592 | tf_op jit(solution)/shard_map/all_gather | solution.py:44
  214.2 2.4 fusion.54
  216.6 0.8 fusion.55
  217.3 0.5 multiply_reduce_fusion
  217.8 0.7 multiply_convert_fusion.3
  218.5 7.6 %fusion.10 = bf16[4,512,512]{2,1,0:T(8,128)(2,1)} fusion(bf16[4,512,512]{2,1,0:T(8,128)(2,1)S(1)} %multiply_convert_fusion.3, f32[512,512]{1,0:T(8,128)} %fusion.32), kind=kOutput, calls=%fused_computation.18 | convolution fusion | flops 2152726528 | bytes 5242880 | tf_op jit(solution)/shard_map/cij,cjk->cik/dot_general | solution.py:34
  226.1 2.9 %fusion.18 = bf16[4,512,512]{2,1,0:T(8,128)(2,1)S(1)} fusion(bf16[4,512,512]{2,1,0:T(8,128)(2,1)S(1)} %multiply_convert_fusion.3, bf16[4,512,512]{2,1,0:T(8,128)(2,1)} %fusion.10), kind=kOutput, calls=%fused_computation.26 | convolution fusion | flops 1074790400 | bytes 6291456 | tf_op jit(solution)/shard_map/cij,cjk->cik/dot_general | solution.py:37
  229.0 1.3 copy-done.3
  230.4 2.6 %fusion.31 = bf16[4,512,512]{2,1,0:T(8,128)(2,1)} fusion(bf16[4,512,512]{2,1,0:T(8,128)(2,1)S(1)} %fusion.18, f32[512,512]{1,0:T(8,128)S(1)} %copy-done.1), kind=kOutput, calls=%fused_computation.33 | convolution fusion | flops 1077936128 | bytes 5242880 | tf_op jit(solution)/shard_map/cij,cjk->cik/dot_general | solution.py:31
  233.0 6.5 %fusion.3 = bf16[4,512,512]{2,1,0:T(8,128)(2,1)} fusion(bf16[4,512,512]{2,1,0:T(8,128)(2,1)} %copy-done.3, bf16[4,512,512]{2,1,0:T(8,128)(2,1)} %fusion.31), kind=kOutput, calls=%fused_computation.11 | convolution fusion | flops 2148532224 | bytes 6291456 | tf_op jit(solution)/shard_map/cij,cjk->cik/dot_general | solution.py:37
  239.5 6.2 %fusion.12 = bf16[4,512,512]{2,1,0:T(8,128)(2,1)} fusion(f32[512,512]{1,0:T(8,128)} %fusion.33, f32[4]{0:T(128)S(1)} %get-tuple-element.5, bf16[4,512,512]{2,1,0:T(8,128)(2,1)S(1)} %multiply_convert_fusion.3, f32[512,512]{1,0:T(8,128)} %fusion.32, bf16[4,512,512]{2,1,0:T(8,128)(2,1)} %copy-done.3), kind=kOutput, calls=%fused_computation.20 | convolution fusion | flops 2159017984 | bytes 8388624 | tf_op jit(solution)/shard_map/cij,cjk->cik/dot_general | solution.py:28
  245.7 3.8 %fusion.21 = bf16[4,512,512]{2,1,0:T(8,128)(2,1)S(1)} fusion(bf16[4,512,512]{2,1,0:T(8,128)(2,1)} %fusion.3, f32[512,512]{1,0:T(8,128)} %fusion.32, bf16[4,512,512]{2,1,0:T(8,128)(2,1)} %fusion.12), kind=kOutput, calls=%fused_computation.27 | convolution fusion | flops 1078984704 | bytes 7340032 | tf_op jit(solution)/shard_map/cij,cjk->cik/dot_general | solution.py:28
  249.5 1.0 slice.8
  250.5 2.4 fusion.30
  (14 shorter events, 0.3 us)
Async XLA Ops:
  6.5 157.4 %reduce-scatter.2.cloned.1.call-start = ((), (), s32[]{:S(2)}) async-start(), calls=%async_computation.2 | async-start | bytes 8519680 | tf_op jit(solution)/shard_map/reduce_scatter | solution.py:73
  12.9 0.7 copy-start.2
  13.0 201.2 %all-gather.2.cloned.1.call-start = ((), (), s32[]{:S(2)}) async-start(), calls=%async_computation.3 | async-start | bytes 1310720 | tf_op jit(solution)/shard_map/all_gather | solution.py:44
  214.2 2.4 copy-start
  226.1 4.3 %copy-start.1 = (f32[512,512]{1,0:T(8,128)S(1)}, f32[512,512]{1,0:T(8,128)}, u32[]{:S(2)}) copy-start(f32[512,512]{1,0:T(8,128)} %fusion.32) | copy-start | bytes 3145732
  229.0 1.3 copy-start.3
Sparse Core Ops, SparseCore 0:
  13.1 150.8 reduce-scatter.1
  191.3 22.8 all-gather.1
where the time goes:
time: 260 us
  waiting for transfers between devices  171 us (66%)
  matrix products  35.4 us (14%)
  blocking collectives  24.9 us (10%)
  between operations  13.5 us (5%)
  other arithmetic  10.9 us (4%)
  local copies, waits for them, and re-layouts  4.07 us (2%)
    reduce_scatter x1, waiting for transfers between devices, on_device(): lax.psum_scatter(local_grads.astype(jnp.float32), 'dp', scatter_dimension...  150 us
    all_to_all x1, blocking collectives, on_device(): lax.all_to_all(outgoing, 'dp', split_axis=1, concat_axis=1, tiled=True)  24.9 us
    all_gather x1, waiting for transfers between devices, precondition(): full_block = lax.all_gather(owned_blocks, 'mp', axis=2, tiled=True)  20.7 us
    dot_general x2, matrix products, inverse_roots(): jnp.einsum('cij,cjk->cik', root_now, factor, preferred_element_type=jnp.f...  9.97 us
    dot_general x2, matrix products, inverse_roots(): jnp.einsum('cij,cjk->cik', fourth, moment, preferred_element_type=jnp.flo...  9.44 us
    dot_general x1, matrix products, inverse_roots(): jnp.einsum('cij,cjk->cik', square, square, preferred_element_type=jnp.flo...  7.56 us
    convert_element_type x1, other arithmetic, on_device(): local_grads.astype(jnp.float32)  6.4 us
  transfers between devices with their start and end apart: 2, of which 2 were waited for; matrix products, arithmetic and copies ran while one was open for 1% of the time, Pallas kernels for 0%

commit v1 on v0

v1 whole, which is shorter than its diff:
```python
import math

import jax
import jax.numpy as jnp
from jax import lax
from jax.experimental import pallas as pl
from jax.experimental.pallas import tpu as pltpu
from jax.sharding import Mesh, PartitionSpec as P

ITERS = 3
MOST = 2
Z, Y, CORE = 8, 4, 2
DP = ("z", "y", "core")


def selection(target, slot_rank, capacity, devices):
    slot_index = jnp.arange(capacity * devices, dtype=jnp.int32)
    want_slot = slot_index // devices
    want_device = slot_index % devices
    matches = (slot_rank[None, :] == want_slot[:, None]) & (target[None, :] == want_device[:, None])
    return matches.astype(jnp.bfloat16)


def dot(a, b):
    return jnp.dot(a, b, preferred_element_type=jnp.float32)


def dot16(a, b):
    return dot(a, b).astype(jnp.bfloat16)


def precondition_kernel(p0, p1, p2, p3, out_ref):
    slots, extent, columns = out_ref.shape
    rows = lax.broadcasted_iota(jnp.int32, (extent, extent), 0)
    cols = lax.broadcasted_iota(jnp.int32, (extent, extent), 1)
    five = jnp.where(rows == cols, jnp.float32(5.0), jnp.float32(0.0))
    blocks, moments, scales = [], [], []
    for slot in range(slots):
        block = jnp.concatenate([p[slot] for p in (p0, p1, p2, p3)], axis=1)
        left = lax.dot_general(block, block, (((1,), (1,)), ((), ())), preferred_element_type=jnp.float32)
        right = lax.dot_general(block, block, (((0,), (0,)), ((), ())), preferred_element_type=jnp.float32)
        blocks.append(block)
        for stat in (left, right):
            total = jnp.sum(stat * stat, keepdims=True)
            scaling = 2.5 / jnp.sqrt(total + 1e-06)
            moments.append((scaling * stat).astype(jnp.bfloat16))
            scales.append(jnp.sqrt(jnp.sqrt(scaling)).astype(jnp.bfloat16).astype(jnp.float32))
    chains = range(2 * slots)
    roots = [None] * (2 * slots)
    for iteration in range(ITERS):
        factors = [((five - m.astype(jnp.float32)) * 0.25).astype(jnp.bfloat16) for m in moments]
        for c in chains:
            if iteration == 0:
                roots[c] = (scales[c] * factors[c].astype(jnp.float32)).astype(jnp.bfloat16)
            elif iteration == ITERS - 1 and c % 2 == 1:
                roots[c] = dot16(roots[c], factors[c][:, :columns])
            else:
                roots[c] = dot16(roots[c], factors[c])
        if iteration < ITERS - 1:
            squares = [dot16(f, f) for f in factors]
            fourths = [dot16(s, s) for s in squares]
            moments = [dot16(f, m) for f, m in zip(fourths, moments)]
    for slot in range(slots):
        right_half = dot16(blocks[slot], roots[2 * slot + 1])
        product = dot(roots[2 * slot], right_half)
        out_ref[slot] = (math.sqrt(extent) * product).astype(jnp.bfloat16)


def on_device(grads, owner):
    local_grads = grads[0]
    block_count, extent, columns = local_grads.shape
    devices = Z * Y * CORE
    half = extent // CORE
    positions = jnp.arange(block_count, dtype=jnp.int32)
    earlier = (owner[None, :] == owner[:, None]) & (positions[None, :] < positions[:, None])
    owner_rank = jnp.sum(earlier.astype(jnp.int32), axis=1)
    core = lax.axis_index("core")
    kept = lax.dynamic_slice_in_dim(local_grads, core * half, half, 1)
    sent = lax.dynamic_slice_in_dim(local_grads, (1 - core) * half, half, 1)
    arrived = lax.ppermute(sent, "core", [(0, 1), (1, 0)])
    pair = (kept.astype(jnp.float32) + arrived.astype(jnp.float32)).astype(jnp.bfloat16)
    pair = pair.reshape(block_count, Y, half // Y, columns)
    pieces = lax.all_to_all(pair, "y", split_axis=1, concat_axis=1, tiled=True)
    plane = jnp.sum(pieces.astype(jnp.float32), axis=1).astype(jnp.bfloat16)
    plane = plane.reshape(block_count, Z, half // (Y * Z), columns)
    pieces = lax.all_to_all(plane, "z", split_axis=1, concat_axis=1, tiled=True)
    summed = jnp.sum(pieces.astype(jnp.float32), axis=1)
    stripe = extent // devices
    mean_rows = (summed / devices).astype(jnp.bfloat16).reshape(block_count, stripe * columns)
    outgoing = jnp.dot(
        selection(owner, owner_rank, MOST, devices),
        mean_rows,
        preferred_element_type=jnp.float32,
    )
    outgoing = outgoing.astype(jnp.bfloat16).reshape(MOST, devices, stripe * columns)
    arrived = lax.all_to_all(outgoing, DP, split_axis=1, concat_axis=1, tiled=True)
    arrived = arrived.reshape(MOST, Z, Y, CORE, stripe, columns)
    owned = arrived.transpose(0, 3, 2, 1, 4, 5).reshape(MOST, extent, columns)
    bands = [owned]
    for shift in range(1, 4):
        bands.append(lax.ppermute(owned, "mp", [(i, (i + shift) % 4) for i in range(4)]))
    return pl.pallas_call(
        precondition_kernel,
        out_shape=jax.ShapeDtypeStruct(owned.shape, jnp.bfloat16),
        in_specs=[pl.BlockSpec(memory_space=pltpu.VMEM)] * 4,
        out_specs=pl.BlockSpec(memory_space=pltpu.VMEM),
        compiler_params=pltpu.CompilerParams(vmem_limit_bytes=48 * 1024 * 1024),
        name="precondition",
    )(*bands)


def solution(mesh):
    split = Mesh(mesh.devices.reshape(Z, Y, CORE, 4), ("z", "y", "core", "mp"))
    placed = (P(DP, None, None, "mp"), P())
    return jax.shard_map(
        on_device, mesh=split, in_specs=placed, out_specs=P(DP, None, "mp"), check_vma=False
    )
```

time: 260 us -> 113 us (0.43)
  waiting for transfers between devices: 171 us -> 30.1 us
  matrix products: 35.4 us -> 0.27 us
  blocking collectives: 24.9 us -> 47.7 us
  starting transfers between devices: 0.04 us -> 15.6 us
  between operations: 13.5 us -> 0.08 us
  Pallas kernels: 0 us -> 11.7 us
  other arithmetic: 10.9 us -> 3.01 us
    reduce_scatter x1 -> x0, waiting for transfers between devices: 150 us -> none  [on_device(): lax.psum_scatter(local_grads.astype(jnp.float32), 'dp', scatter_dimension...]
    dot_general x10 -> x1, matrix products: 35.4 us -> 0.27 us  [on_device(): jnp.dot(selection(owner, owner_rank, MOST, devices), mean_rows, preferred...]
    all_to_all x1 -> x2, blocking collectives: 24.9 us -> 47.7 us  [the longest x1 28.5 us: on_device(): pieces = lax.all_to_all(pair, 'y', split_axis=1, concat_axis=1, tiled=True)]
    all_gather x1 -> x0, waiting for transfers between devices: 20.7 us -> none  [precondition(): full_block = lax.all_gather(owned_blocks, 'mp', axis=2, tiled=True)]
    all_to_all x0 -> x1, waiting for transfers between devices: none -> 15.5 us  [on_device(): pieces = lax.all_to_all(plane, 'z', split_axis=1, concat_axis=1, tiled=True)]
    ppermute x0 -> x4, waiting for transfers between devices: none -> 14.6 us  [the longest x3 10.6 us: on_device(): lax.ppermute(owned, 'mp', [(i, (i + shift) % 4) for i in range(4)])]
    pallas_call x0 -> x1, Pallas kernels: none -> 11.7 us  [on_device(): pl.pallas_call(precondition_kernel, out_shape=jax.ShapeDtypeStruct(owned....]
    ppermute x0 -> x4, starting transfers between devices: none -> 8.13 us  [the longest x3 4.89 us: on_device(): lax.ppermute(owned, 'mp', [(i, (i + shift) % 4) for i in range(4)])]
  transfers between devices with their start and end apart: 2 -> 5, of which waited for: 2 -> 4; matrix products, arithmetic and copies ran while one was open for 1% -> 0% of each run, Pallas kernels for 0% -> 0%
where the time goes in v1:
time: 113 us
  blocking collectives  47.7 us (42%)
  waiting for transfers between devices  30.1 us (27%)
  starting transfers between devices  15.6 us (14%)
  Pallas kernels  11.7 us (10%)
  local copies, waits for them, and re-layouts  4.73 us (4%)
  other arithmetic  3.01 us (3%)
    all_to_all x1, blocking collectives, on_device(): pieces = lax.all_to_all(pair, 'y', split_axis=1, concat_axis=1, tiled=True)  28.5 us
    all_to_all x1, blocking collectives, on_device(): lax.all_to_all(outgoing, DP, split_axis=1, concat_axis=1, tiled=True)  19.3 us
    all_to_all x1, waiting for transfers between devices, on_device(): pieces = lax.all_to_all(plane, 'z', split_axis=1, concat_axis=1, tiled=True)  15.5 us
    pallas_call x1, Pallas kernels, on_device(): pl.pallas_call(precondition_kernel, out_shape=jax.ShapeDtypeStruct(owned....  11.7 us
    ppermute x3, waiting for transfers between devices, on_device(): lax.ppermute(owned, 'mp', [(i, (i + shift) % 4) for i in range(4)])  10.6 us
    all_to_all x1, starting transfers between devices, on_device(): pieces = lax.all_to_all(plane, 'z', split_axis=1, concat_axis=1, tiled=True)  7.43 us
    ppermute x3, starting transfers between devices, on_device(): lax.ppermute(owned, 'mp', [(i, (i + shift) % 4) for i in range(4)])  4.89 us
    ppermute x1, waiting for transfers between devices, on_device(): arrived = lax.ppermute(sent, 'core', [(0, 1), (1, 0)])  4 us
  transfers between devices with their start and end apart: 5, of which 4 were waited for; matrix products, arithmetic and copies ran while one was open for 0% of the time, Pallas kernels for 0%

profile of v1, /device:TPU:1, one launch (start us, length us, event | category | flops | bytes accessed | tf_op | source)
XLA Modules:
  0.0 113.1 jit_solution(16137938772290913128)
XLA Ops:
  0.0 3.2 %dynamic-slice_bitcast_fusion = bf16[32,256,128]{2,1,0:T(8,128)(2,1)} fusion(bf16[1,32,512,128]{3,2,1,0:T(8,128)(2,1)} %param.2, s32[]{:T(128)S(6)} %select_n.29), kind=kLoop, calls=%fused_computation.2 | loop fusion | bytes 4194308 | tf_op jit(solution)/shard_map/dynamic_slice | solution.py:79
  3.2 3.2 %collective-permute-start = (bf16[32,256,128]{2,1,0:T(8,128)(2,1)}, bf16[32,256,128]{2,1,0:T(8,128)(2,1)S(1)}, u32[]{:S(2)}, u32[]{:S(2)}) collective-permute-start(bf16[32,256,128]{2,1,0:T(8,128)(2,1)} %dynamic-slice_bitcast_fusion), channel_id=1, source_target_pairs={{0,4},{4,0},{1,5},{5,1},{2,6},{6,2},{3,7},{7,3},{8,12},{12,8},{9,1... | collective-permute-start | bytes 6291464 | tf_op jit(solution)/shard_map/ppermute | solution.py:80
  6.4 4.0 %collective-permute-done = bf16[32,256,128]{2,1,0:T(8,128)(2,1)S(1)} collective-permute-done((bf16[32,256,128]{2,1,0:T(8,128)(2,1)}, bf16[32,256,128]{2,1,0:T(8,128)(2,1)S(1)}, u32[]{:S(2)}, u32[]{:S(2)}) %collective-permute-start) | collective-permute-done | bytes 2097184 | tf_op jit(solution)/shard_map/ppermute | solution.py:80
  10.4 2.3 %fusion = bf16[32,256,128]{2,1,0:T(8,128)(2,1)S(1)} fusion(bf16[32,256,128]{2,1,0:T(8,128)(2,1)S(1)} %collective-permute-done, bf16[1,32,512,128]{3,2,1,0:T(8,128)(2,1)} %param.2, s32[]{:T(128)S(6)} %select_n.28), kind=kLoop, calls=%fused_computation.1 | loop fusion | flops 4194304 | bytes 6291460 | tf_op jit(solution)/shard_map/convert_element_type | solution.py:81
  12.7 0.2 copy.12
  12.9 28.5 %all_to_all.15 = bf16[32,4,64,128]{3,2,0,1:T(8,128)(2,1)S(1)} all-to-all(bf16[32,4,64,128]{3,2,0,1:T(8,128)(2,1)S(1)} %copy.12), channel_id=1, replica_groups=mesh['z'=8,'y'=4,'core'=2,'mp'=4] {'y'}, dimensions={1} | all-to-all | bytes 4194304 | tf_op jit(solution)/shard_map/all_to_all | solution.py:83
  41.4 0.4 reduce_sum.31
  41.8 0.9 copy.13
  42.7 7.4 %all-to-all-start.1 = ((bf16[32,8,8,128]{3,2,0,1:T(8,128)(2,1)}), bf16[32,8,8,128]{3,2,0,1:T(8,128)(2,1)S(1)}, u32[]{:S(2)}, u32[]{:S(2)}) async-start(bf16[32,8,8,128]{3,2,0,1:T(8,128)(2,1)} %copy.13), calls=%async_computation.1 | async-start | bytes 1048576 | tf_op jit(solution)/shard_map/all_to_all | solution.py:86
  50.2 0.2 convert_reduce_fusion.1
  50.3 15.5 %all-to-all-done.1 = bf16[32,8,8,128]{3,2,0,1:T(8,128)(2,1)S(1)} async-done(((bf16[32,8,8,128]{3,2,0,1:T(8,128)(2,1)}), bf16[32,8,8,128]{3,2,0,1:T(8,128)(2,1)S(1)}, u32[]{:S(2)}, u32[]{:S(2)}) %all-to-all-start.1) | async-done | bytes 524320 | tf_op jit(solution)/shard_map/all_to_all | solution.py:86
  65.8 0.1 convert_reduce_fusion
  65.9 0.3 convolution_convert_fusion
  66.2 0.3 copy.14
  66.5 19.3 %all_to_all.16 = bf16[2,64,1024]{2,0,1:T(2,128)(2,1)S(1)} all-to-all(bf16[2,64,1024]{2,0,1:T(2,128)(2,1)S(1)} %copy.14), channel_id=1, replica_groups=mesh['z'=8,'y'=4,'core'=2,'mp'=4] {'z','y','core'}, dimensions={1} | all-to-all | bytes 524288 | tf_op jit(solution)/shard_map/all_to_all | solution.py:96
  85.7 0.2 reshape.55
  85.9 0.1 copy.16
  86.0 1.3 %collective-permute-start.1 = (bf16[2,512,128]{2,1,0:T(8,128)(2,1)S(1)}, bf16[2,512,128]{2,1,0:T(8,128)(2,1)S(1)}, u32[]{:S(2)}, u32[]{:S(2)}) collective-permute-start(bf16[2,512,128]{2,1,0:T(8,128)(2,1)S(1)} %bitcast.17), channel_id=1, source_target_pairs={{0,1},{1,2},{2,3},{3,0},{4,5},{5,6},{6,7},{7,4},{8,9},{9,10},{10,1... | collective-permute-start | bytes 786440 | tf_op jit(solution)/shard_map/ppermute | solution.py:101
  87.3 2.5 %collective-permute-start.2 = (bf16[2,512,128]{2,1,0:T(8,128)(2,1)S(1)}, bf16[2,512,128]{2,1,0:T(8,128)(2,1)S(1)}, u32[]{:S(2)}, u32[]{:S(2)}) collective-permute-start(bf16[2,512,128]{2,1,0:T(8,128)(2,1)S(1)} %bitcast.18), channel_id=1, source_target_pairs={{0,2},{1,3},{2,0},{3,1},{4,6},{5,7},{6,4},{7,5},{8,10},{9,11},{10,... | collective-permute-start | bytes 786440 | tf_op jit(solution)/shard_map/ppermute | solution.py:101
  89.7 1.2 %collective-permute-start.3 = (bf16[2,512,128]{2,1,0:T(8,128)(2,1)S(1)}, bf16[2,512,128]{2,1,0:T(8,128)(2,1)S(1)}, u32[]{:S(2)}, u32[]{:S(2)}) collective-permute-start(bf16[2,512,128]{2,1,0:T(8,128)(2,1)S(1)} %bitcast.19), channel_id=1, source_target_pairs={{0,3},{1,0},{2,1},{3,2},{4,7},{5,4},{6,5},{7,6},{8,11},{9,8},{10,9... | collective-permute-start | bytes 786440 | tf_op jit(solution)/shard_map/ppermute | solution.py:101
  90.9 4.0 %collective-permute-done.1.p1 = bf16[2,512,128]{2,1,0:T(8,128)(2,1)S(1)} collective-permute-done((bf16[2,512,128]{2,1,0:T(8,128)(2,1)S(1)}, bf16[2,512,128]{2,1,0:T(8,128)(2,1)S(1)}, u32[]{:S(2)}, u32[]{:S(2)}) %collective-permute-start.1) | collective-permute-done | bytes 262176 | tf_op jit(solution)/shard_map/ppermute | solution.py:101
  94.9 6.6 %collective-permute-done.2.p2 = bf16[2,512,128]{2,1,0:T(8,128)(2,1)S(1)} collective-permute-done((bf16[2,512,128]{2,1,0:T(8,128)(2,1)S(1)}, bf16[2,512,128]{2,1,0:T(8,128)(2,1)S(1)}, u32[]{:S(2)}, u32[]{:S(2)}) %collective-permute-start.2) | collective-permute-done | bytes 262176 | tf_op jit(solution)/shard_map/ppermute | solution.py:101
  101.5 0.0 collective-permute-done.3.p3
  101.5 11.7 %precondition.1 = bf16[2,512,128]{2,1,0:T(8,128)(2,1)} custom-call(bf16[2,512,128]{2,1,0:T(8,128)(2,1)S(1)} %bitcast.20, bf16[2,512,128]{2,1,0:T(8,128)(2,1)S(1)} %collective-permute-done.1.p1, bf16[2,512,128]{2,1,0:T(8,128)(2,1)S(1)} %collective-permute-done.2.p2, bf16[2,512,128]{2,1,0:T(8,128)(2,1)S(1)} %collective-permute-done.3.p3), custom_call_target="tpu_custom_call" | custom-call | tf_op jit(solution)/shard_map/precondition/pallas_call | solution.py:102
  (4 shorter events, 0.0 us)
Async XLA Ops:
  3.2 7.2 %collective-permute-start = (bf16[32,256,128]{2,1,0:T(8,128)(2,1)}, bf16[32,256,128]{2,1,0:T(8,128)(2,1)S(1)}, u32[]{:S(2)}, u32[]{:S(2)}) collective-permute-start(bf16[32,256,128]{2,1,0:T(8,128)(2,1)} %dynamic-slice_bitcast_fusion), channel_id=1, source_target_pairs={{0,4},{4,0},{1,5},{5,1},{2,6},{6,2},{3,7},{7,3},{8,12},{12,8},{9,1... | collective-permute-start | bytes 6291464 | tf_op jit(solution)/shard_map/ppermute | solution.py:80
  41.4 8.7 %copy-start = (s32[32]{0:T(128)S(1)}, s32[32]{0:T(128)}, u32[]{:S(2)}) copy-start(s32[32]{0:T(128)} %param.3) | copy-start | bytes 388
  42.7 23.1 %all-to-all-start.1 = ((bf16[32,8,8,128]{3,2,0,1:T(8,128)(2,1)}), bf16[32,8,8,128]{3,2,0,1:T(8,128)(2,1)S(1)}, u32[]{:S(2)}, u32[]{:S(2)}) async-start(bf16[32,8,8,128]{3,2,0,1:T(8,128)(2,1)} %copy.13), calls=%async_computation.1 | async-start | bytes 1048576 | tf_op jit(solution)/shard_map/all_to_all | solution.py:86
  86.0 8.9 %collective-permute-start.1 = (bf16[2,512,128]{2,1,0:T(8,128)(2,1)S(1)}, bf16[2,512,128]{2,1,0:T(8,128)(2,1)S(1)}, u32[]{:S(2)}, u32[]{:S(2)}) collective-permute-start(bf16[2,512,128]{2,1,0:T(8,128)(2,1)S(1)} %bitcast.17), channel_id=1, source_target_pairs={{0,1},{1,2},{2,3},{3,0},{4,5},{5,6},{6,7},{7,4},{8,9},{9,10},{10,1... | collective-permute-start | bytes 786440 | tf_op jit(solution)/shard_map/ppermute | solution.py:101
  87.3 14.2 %collective-permute-start.2 = (bf16[2,512,128]{2,1,0:T(8,128)(2,1)S(1)}, bf16[2,512,128]{2,1,0:T(8,128)(2,1)S(1)}, u32[]{:S(2)}, u32[]{:S(2)}) collective-permute-start(bf16[2,512,128]{2,1,0:T(8,128)(2,1)S(1)} %bitcast.18), channel_id=1, source_target_pairs={{0,2},{1,3},{2,0},{3,1},{4,6},{5,7},{6,4},{7,5},{8,10},{9,11},{10,... | collective-permute-start | bytes 786440 | tf_op jit(solution)/shard_map/ppermute | solution.py:101
  89.7 11.8 %collective-permute-start.3 = (bf16[2,512,128]{2,1,0:T(8,128)(2,1)S(1)}, bf16[2,512,128]{2,1,0:T(8,128)(2,1)S(1)}, u32[]{:S(2)}, u32[]{:S(2)}) collective-permute-start(bf16[2,512,128]{2,1,0:T(8,128)(2,1)S(1)} %bitcast.19), channel_id=1, source_target_pairs={{0,3},{1,0},{2,1},{3,2},{4,7},{5,4},{6,5},{7,6},{8,11},{9,8},{10,9... | collective-permute-start | bytes 786440 | tf_op jit(solution)/shard_map/ppermute | solution.py:101

commit v2 on v1

v2 whole, which is shorter than its diff:
```python
import math

import jax
import jax.numpy as jnp
from jax import lax
from jax.experimental import pallas as pl
from jax.experimental.pallas import tpu as pltpu
from jax.sharding import Mesh, PartitionSpec as P

ITERS = 3
MOST = 2
Z, Y, CORE, MP = 8, 4, 2, 4
DP = ("z", "y", "core")
IN_VMEM = pl.BlockSpec(memory_space=pltpu.VMEM)
IN_SMEM = pl.BlockSpec(memory_space=pltpu.SMEM)
IN_HBM = pl.BlockSpec(memory_space=pltpu.HBM)
PARAMS = pltpu.CompilerParams(vmem_limit_bytes=12 * 1024 * 1024)
LARGE = pltpu.CompilerParams(vmem_limit_bytes=24 * 1024 * 1024)


def selection(owner, devices, stripe):
    blocks = owner.shape[0]
    positions = jnp.arange(blocks, dtype=jnp.int32)
    earlier = (owner[None, :] == owner[:, None]) & (positions[None, :] < positions[:, None])
    slot_of = owner * MOST + jnp.sum(earlier.astype(jnp.int32), axis=1)
    wanted = slot_of[:, None] * stripe + jnp.arange(stripe, dtype=jnp.int32)[None, :]
    row = jnp.arange(MOST * devices * stripe, dtype=jnp.int32)
    return (wanted.reshape(1, blocks * stripe) == row[:, None]).astype(jnp.bfloat16)


def dot(a, b):
    return jnp.dot(a, b, preferred_element_type=jnp.float32)


def dot16(a, b):
    return dot(a, b).astype(jnp.bfloat16)


def pieces_of(grads, core, y, shifts, name):
    blocks, extent, columns = grads.shape
    half = extent // CORE
    rows = half // Y
    cuts = 4
    group = blocks // cuts

    def kernel(core_ref, y_ref, in_ref, sent_ref, kept_ref, sems):
        copies = []
        for out_ref, which in ((sent_ref, 1 - core_ref[0]), (kept_ref, core_ref[0])):
            for i, shift in enumerate(shifts):
                first = pl.multiple_of(which * half + (y_ref[0] + shift) % Y * rows, rows)
                for cut in range(cuts):
                    some = pl.ds(cut * group, group)
                    source = in_ref.at[some, pl.ds(first, rows)]
                    copies.append(
                        pltpu.make_async_copy(source, out_ref.at[i, some], sems.at[len(copies)])
                    )
        for copy in copies:
            copy.start()
        for copy in copies:
            copy.wait()

    shape = pltpu.VMEM((len(shifts), blocks, rows, columns), grads.dtype)
    return pl.pallas_call(
        kernel,
        out_shape=(shape, shape),
        in_specs=[IN_SMEM, IN_SMEM, IN_HBM],
        out_specs=[IN_VMEM] * 2,
        scratch_shapes=[pltpu.SemaphoreType.DMA((2 * cuts * len(shifts),))],
        compiler_params=PARAMS,
        name=name,
    )(core, y, pltpu.with_memory_space_constraint(grads, pltpu.HBM))


def add_parts(parts, arrays, dtype, name):
    count = [entry[0][3] for entry in parts]
    rows, columns = arrays[0].shape[-2:]

    def kernel(*refs):
        ins, outs = refs[: len(arrays)], refs[len(arrays) :]
        for entry, out in zip(parts, outs):

            def add(b, carry):
                total = None
                for which, index, first, _ in entry:
                    value = ins[which][index, first + b].astype(jnp.float32)
                    total = value if total is None else total + value
                out[0, b] = total.astype(dtype)
                return carry

            lax.fori_loop(0, entry[0][3], add, 0, unroll=4)

    return pl.pallas_call(
        kernel,
        out_shape=[pltpu.VMEM((1, n, rows, columns), dtype) for n in count],
        in_specs=[IN_VMEM] * len(arrays),
        out_specs=[IN_VMEM] * len(parts),
        compiler_params=PARAMS,
        name=name,
    )(*arrays)


def plane_kernel(own_a_ref, own_b_ref, w_up_ref, w_down_ref, out_ref):
    half, rows = own_a_ref.shape[1:3]
    stripe = rows // Z
    for first, one, two in ((0, own_a_ref, w_up_ref), (half, own_b_ref, w_down_ref)):

        def add(pair, carry):
            totals = [one[0, b] + two[0, b].astype(jnp.float32) for b in (2 * pair, 2 * pair + 1)]
            at = pl.multiple_of((first + 2 * pair) * stripe, 2 * stripe)
            for z in range(Z):
                both = [total[z * stripe : (z + 1) * stripe] for total in totals]
                out_ref[z, pl.ds(at, 2 * stripe)] = jnp.concatenate(both, axis=0).astype(jnp.bfloat16)
            return carry

        lax.fori_loop(0, half // 2, add, 0, unroll=2)


def plane_sum(own_a, own_b, w_up, w_down):
    half, rows, columns = own_a.shape[1:]
    return pl.pallas_call(
        plane_kernel,
        out_shape=pltpu.VMEM((Z, 2 * half * rows // Z, columns), jnp.bfloat16),
        in_specs=[IN_VMEM] * 4,
        out_specs=IN_VMEM,
        compiler_params=PARAMS,
        name="plane_sum",
    )(own_a, own_b, w_up, w_down)


def select_kernel(devices, chosen_ref, *refs):
    out_ref = refs[-1]
    parts = []
    for ref in refs[:-1]:
        parts.append((jnp.sum(ref[...].astype(jnp.float32), axis=0) / devices).astype(jnp.bfloat16))
    out_ref[...] = dot16(chosen_ref[...], jnp.concatenate(parts, axis=0))


def select(chosen, pieces, devices):
    columns = pieces[0].shape[-1]
    return pl.pallas_call(
        lambda *refs: select_kernel(devices, *refs),
        out_shape=pltpu.VMEM((chosen.shape[0], columns), jnp.bfloat16),
        in_specs=[IN_VMEM] * (1 + len(pieces)),
        out_specs=IN_VMEM,
        compiler_params=PARAMS,
        name="select",
    )(chosen, *pieces)


def spread_kernel(in_ref, out_ref):
    stripe = in_ref.shape[1] // (Y * CORE * MOST)
    values = in_ref[...].astype(jnp.float32)
    for y in range(Y):
        for core in range(CORE):
            for slot in range(MOST):
                first = ((y * CORE + core) * MOST + slot) * stripe
                piece = values[:, first : first + stripe].reshape(Z * stripe, -1).astype(jnp.bfloat16)
                for m in range(slot, MP, MOST):
                    out_ref[y * MP + m, core] = piece


def spread(routed):
    stripe = routed.shape[1] // (Y * CORE * MOST)
    return pl.pallas_call(
        spread_kernel,
        out_shape=pltpu.VMEM((Y * MP, CORE, Z * stripe, routed.shape[2]), routed.dtype),
        in_specs=[IN_VMEM],
        out_specs=IN_VMEM,
        compiler_params=PARAMS,
        name="spread",
    )(routed)


def other_core_kernel(core_ref, in_ref, out_ref):
    for i in range(out_ref.shape[0]):
        out_ref[i] = in_ref[i, 1 - core_ref[0]]


def for_other_core(core, pieces):
    return pl.pallas_call(
        other_core_kernel,
        out_shape=pltpu.VMEM(pieces.shape[:1] + pieces.shape[2:], pieces.dtype),
        in_specs=[IN_SMEM, IN_VMEM],
        out_specs=IN_VMEM,
        compiler_params=PARAMS,
        name="for_other_core",
    )(core, pieces)


def place_kernel(band_ref, kept_ref, taken_ref, out_ref, sems):
    slot = band_ref[0] % MOST
    one = pltpu.make_async_copy(kept_ref, out_ref.at[slot], sems.at[0])
    two = pltpu.make_async_copy(taken_ref, out_ref.at[1 - slot], sems.at[1])
    one.start()
    two.start()
    one.wait()
    two.wait()


def place(band, kept, taken):
    return pl.pallas_call(
        place_kernel,
        out_shape=jax.ShapeDtypeStruct((MOST,) + kept.shape, kept.dtype),
        in_specs=[IN_SMEM, IN_VMEM, IN_VMEM],
        out_specs=IN_HBM,
        scratch_shapes=[pltpu.SemaphoreType.DMA((2,))],
        compiler_params=PARAMS,
        name="place",
    )(band, kept, taken)


def precondition_kernel(core_ref, band_ref, own_ref, other_ref, kept_ref, sent_ref, block_ref):
    own = band_ref[0]
    extent = block_ref.shape[0]
    rows, columns = other_ref.shape[1:]
    half = extent // CORE
    for y in range(Y):
        for j in range(MP):
            at = y * MP + (own ^ j)
            band = pl.ds(j * columns, columns)
            first = pl.multiple_of(core_ref[0] * half + y * rows, rows)
            block_ref[pl.ds(first, rows), band] = own_ref[at, core_ref[0]]
            first = pl.multiple_of((1 - core_ref[0]) * half + y * rows, rows)
            block_ref[pl.ds(first, rows), band] = other_ref[at]
    block = block_ref[...]
    row = lax.broadcasted_iota(jnp.int32, (extent, extent), 0)
    col = lax.broadcasted_iota(jnp.int32, (extent, extent), 1)
    five = jnp.where(row == col, jnp.float32(5.0), jnp.float32(0.0))
    left = lax.dot_general(block, block, (((1,), (1,)), ((), ())), preferred_element_type=jnp.float32)
    right = lax.dot_general(block, block, (((0,), (0,)), ((), ())), preferred_element_type=jnp.float32)
    moments, scales = [], []
    for stat in (left, right):
        total = jnp.sum(stat * stat, keepdims=True)
        scaling = 2.5 / jnp.sqrt(total + 1e-06)
        moments.append((scaling * stat).astype(jnp.bfloat16))
        scales.append(jnp.sqrt(jnp.sqrt(scaling)).astype(jnp.bfloat16).astype(jnp.float32))
    for iteration in range(ITERS):
        factors = [((five - m.astype(jnp.float32)) * 0.25).astype(jnp.bfloat16) for m in moments]
        if iteration == 0:
            roots = [(s * f.astype(jnp.float32)).astype(jnp.bfloat16) for s, f in zip(scales, factors)]
        elif iteration < ITERS - 1:
            roots = [dot16(r, f) for r, f in zip(roots, factors)]
        else:
            roots = [dot16(roots[0], factors[0]), dot16(roots[1], factors[1][:, : 2 * columns])]
        if iteration < ITERS - 1:
            squares = [dot16(f, f) for f in factors]
            fourths = [dot16(s, s) for s in squares]
            moments = [dot16(f, m) for f, m in zip(fourths, moments)]
    right_half = dot16(block, roots[1])
    product = (math.sqrt(extent) * dot(roots[0], right_half)).astype(jnp.bfloat16)
    kept_ref[...] = product[:, :columns]
    sent_ref[...] = product[:, columns:]


def on_device(grads, owner):
    local_grads = grads[0]
    block_count, extent, columns = local_grads.shape
    devices = Z * Y * CORE
    core = lax.axis_index("core").reshape(1).astype(jnp.int32)
    y = lax.axis_index("y").reshape(1).astype(jnp.int32)
    band = lax.axis_index("mp").reshape(1).astype(jnp.int32)
    chosen = selection(owner, devices, extent // devices)

    def swap(value):
        return lax.ppermute(value, "core", [(0, 1), (1, 0)])

    def up(value):
        return lax.ppermute(value, "y", [(i, (i + 1) % Y) for i in range(Y)])

    def down(value):
        return lax.ppermute(value, "y", [(i, (i - 1) % Y) for i in range(Y)])

    n = block_count // 2
    sent_far, kept_far = pieces_of(local_grads, core, y, (2,), "far")
    far = swap(sent_far)
    local_grads, kept_far = lax.optimization_barrier((local_grads, kept_far))
    sent_near, kept_near = pieces_of(local_grads, core, y, (1, 3), "near")
    near = swap(sent_near)
    local_grads, kept_near = lax.optimization_barrier((local_grads, kept_near))
    sent_own, kept_own = pieces_of(local_grads, core, y, (0,), "own")
    own = swap(sent_own)
    v2a, v2b = add_parts(
        [[(0, 0, 0, n), (1, 0, 0, n)], [(0, 0, n, n), (1, 0, n, n)]], (kept_far, far), jnp.bfloat16, "far_sum"
    )
    from_down, from_up = up(v2a), down(v2b)
    v1b, v3a = add_parts(
        [[(0, 0, n, n), (1, 0, n, n)], [(0, 1, 0, n), (1, 1, 0, n)]], (kept_near, near), jnp.bfloat16, "near_sum"
    )
    v_up, v_down = up(v1b), down(v3a)
    kept_near, near, v1b, v3a = lax.optimization_barrier((kept_near, near, v1b, v3a))
    w1a, w3b = add_parts(
        [[(0, 0, 0, n), (1, 0, 0, n), (2, 0, 0, n)], [(0, 1, n, n), (1, 1, n, n), (3, 0, 0, n)]],
        (kept_near, near, from_down, from_up),
        jnp.bfloat16,
        "relay_sum",
    )
    w_up, w_down = up(w1a), down(w3b)
    own_a, own_b = add_parts(
        [[(0, 0, 0, n), (1, 0, 0, n), (3, 0, 0, n)], [(0, 0, n, n), (1, 0, n, n), (2, 0, 0, n)]],
        (kept_own, own, v_up, v_down),
        jnp.float32,
        "own_sum",
    )
    own_a, own_b, chosen, band = lax.optimization_barrier((own_a, own_b, chosen, band))
    plane = plane_sum(own_a, own_b, w_up, w_down)
    pieces = [lax.all_to_all(plane, "z", split_axis=0, concat_axis=0, tiled=True)]
    outgoing = select(chosen, pieces, devices).reshape(Z, -1, columns)
    routed = lax.all_to_all(outgoing, "z", split_axis=0, concat_axis=0, tiled=True)
    spread_out = spread(routed)
    mine = lax.all_to_all(spread_out, ("y", "mp"), split_axis=0, concat_axis=0, tiled=True)
    other = swap(for_other_core(core, mine))

    result = pltpu.VMEM((extent, columns), jnp.bfloat16)
    kept, given = pl.pallas_call(
        precondition_kernel,
        out_shape=(result, result),
        in_specs=[IN_SMEM, IN_SMEM, IN_VMEM, IN_VMEM],
        out_specs=[IN_VMEM] * 2,
        scratch_shapes=[pltpu.VMEM((extent, extent), jnp.bfloat16)],
        compiler_params=LARGE,
        name="precondition",
    )(core, band, mine, other)
    taken = lax.ppermute(given, "mp", [(i, i ^ 1) for i in range(MP)])
    return place(band, kept, taken)


def solution(mesh):
    split = Mesh(mesh.devices.reshape(Z, Y, CORE, MP), ("z", "y", "core", "mp"))
    placed = (P(DP, None, None, "mp"), P())
    return jax.shard_map(
        on_device, mesh=split, in_specs=placed, out_specs=P(DP, None, "mp"), check_vma=False
    )
```

time: 113 us -> 97.7 us (0.86)
  waiting for transfers between devices: 30.1 us -> 16.3 us
  local copies, waits for them, and re-layouts: 4.73 us -> 0.09 us
  starting transfers between devices: 15.6 us -> 18.2 us
  other arithmetic: 3.01 us -> 0.47 us
  Pallas kernels: 11.7 us -> 13.4 us
    all_to_all x1 -> x0, waiting for transfers between devices: 15.5 us -> none  [on_device(): pieces = lax.all_to_all(plane, 'z', split_axis=1, concat_axis=1, tiled=True)]
    ppermute x4 -> x11, starting transfers between devices: 8.13 us -> 18.2 us  [the longest x4 9.62 us: swap(): return lax.ppermute(value, 'core', [(0, 1), (1, 0)])]
    all_to_all x1 -> x0, starting transfers between devices: 7.43 us -> none  [on_device(): pieces = lax.all_to_all(plane, 'z', split_axis=1, concat_axis=1, tiled=True)]
    dynamic_slice x1 -> x0, local copies, waits for them, and re-layouts: 3.17 us -> none  [on_device(): sent = lax.dynamic_slice_in_dim(local_grads, (1 - core) * half, half, 1)]
    convert_element_type x2 -> x1, other arithmetic: 2.34 us -> 0.22 us  [selection(): (wanted.reshape(1, blocks * stripe) == row[:, None]).astype(jnp.bfloat16)]
    pallas_call x1 -> x13, Pallas kernels: 11.7 us -> 13.4 us  [the longest x1 6.28 us: on_device(): pl.pallas_call(precondition_kernel, out_shape=(result, result), in_specs=...]
    ppermute x4 -> x11, waiting for transfers between devices: 14.6 us -> 16.3 us  [the longest x3 9.58 us: up(): return lax.ppermute(value, 'y', [(i, (i + 1) % Y) for i in range(Y)])]
    reshape x4 -> x0, local copies, waits for them, and re-layouts: 1.5 us -> none  [the longest x1 0.89 us: on_device(): plane = plane.reshape(block_count, Z, half // (Y * Z), columns)]
  transfers between devices with their start and end apart: 5 -> 11, of which waited for: 4 -> 6; matrix products, arithmetic and copies ran while one was open for 0% -> 1% of each run, Pallas kernels for 0% -> 3%
where the time goes in v2:
time: 97.7 us; the launch traced here: 97.5 us
  blocking collectives  48.8 us (50%)
  starting transfers between devices  18.2 us (19%)
  waiting for transfers between devices  16.3 us (17%)
  Pallas kernels  13.4 us (14%)
    all_to_all x1, blocking collectives, on_device(): lax.all_to_all(plane, 'z', split_axis=0, concat_axis=0, tiled=True)  20.5 us
    all_to_all x1, blocking collectives, on_device(): lax.all_to_all(spread_out, ('y', 'mp'), split_axis=0, concat_axis=0, tile...  15.5 us
    all_to_all x1, blocking collectives, on_device(): lax.all_to_all(outgoing, 'z', split_axis=0, concat_axis=0, tiled=True)  12.7 us
    ppermute x4, starting transfers between devices, swap(): return lax.ppermute(value, 'core', [(0, 1), (1, 0)])  9.62 us
    ppermute x3, waiting for transfers between devices, up(): return lax.ppermute(value, 'y', [(i, (i + 1) % Y) for i in range(Y)])  9.58 us
    ppermute x3, starting transfers between devices, down(): return lax.ppermute(value, 'y', [(i, (i - 1) % Y) for i in range(Y)])  8 us
    pallas_call x1, Pallas kernels, on_device(): pl.pallas_call(precondition_kernel, out_shape=(result, result), in_specs=...  6.28 us
    pallas_call x3, Pallas kernels, pieces_of(): pl.pallas_call(kernel, out_shape=(shape, shape), in_specs=[IN_SMEM, IN_SM...  4.46 us
  transfers between devices with their start and end apart: 11, of which 6 were waited for; matrix products, arithmetic and copies ran while one was open for 1% of the time, Pallas kernels for 3%

profile of v2, /device:TPU:1, one launch (start us, length us, event | category | flops | bytes accessed | tf_op | source)
XLA Modules:
  0.0 97.5 jit_solution(5990706372474862687)
XLA Ops:
  0.0 1.4 %far.1 = (bf16[1,32,64,128]{3,2,1,0:T(8,128)(2,1)S(1)}, bf16[1,32,64,128]{3,2,1,0:T(8,128)(2,1)S(1)}) custom-call(s32[1]{0:T(128)} %bitcast.core_ref, s32[1]{0:T(128)} %bitcast.1.y_ref, bf16[32,512,128]{2,1,0:T(8,128)(2,1)} %bitcast.6), custom_call_target="tpu_custom_call" | custom-call | tf_op jit(solution)/shard_map/far/pallas_call | solution.py:63
  1.4 1.8 %near.1 = (bf16[2,32,64,128]{3,2,1,0:T(8,128)(2,1)S(1)}, bf16[2,32,64,128]{3,2,1,0:T(8,128)(2,1)S(1)}) custom-call(s32[1]{0:T(128)} %bitcast.core_ref, s32[1]{0:T(128)} %bitcast.1.y_ref, bf16[32,512,128]{2,1,0:T(8,128)(2,1)} %bitcast.7), custom_call_target="tpu_custom_call" | custom-call | tf_op jit(solution)/shard_map/near/pallas_call | solution.py:63
  3.1 3.3 %collective-permute-start.1 = (bf16[2,32,64,128]{3,2,1,0:T(8,128)(2,1)S(1)}, bf16[2,32,64,128]{3,2,1,0:T(8,128)(2,1)S(1)}, u32[]{:S(2)}, u32[]{:S(2)}) collective-permute-start(bf16[2,32,64,128]{3,2,1,0:T(8,128)(2,1)S(1)} %get-tuple-element.38), channel_id=1, source_target_pairs={{0,4},{4,0},{1,5},{5,1},{2,6},{6,2},{3,7},{7,3},{8,12},{12,8},{9,1... | collective-permute-start | bytes 3145736 | tf_op jit(solution)/shard_map/ppermute | solution.py:265
  6.6 1.4 %own.1 = (bf16[1,32,64,128]{3,2,1,0:T(8,128)(2,1)S(1)}, bf16[1,32,64,128]{3,2,1,0:T(8,128)(2,1)S(1)}) custom-call(s32[1]{0:T(128)} %bitcast.core_ref, s32[1]{0:T(128)} %bitcast.1.y_ref, bf16[32,512,128]{2,1,0:T(8,128)(2,1)} %bitcast.8), custom_call_target="tpu_custom_call" | custom-call | tf_op jit(solution)/shard_map/own/pallas_call | solution.py:63
  7.9 0.5 collective-permute-start
  8.4 1.1 %collective-permute-done.4.refs_1_ = bf16[1,32,64,128]{3,2,1,0:T(8,128)(2,1)S(1)} collective-permute-done((bf16[1,32,64,128]{3,2,1,0:T(8,128)(2,1)S(1)}, bf16[1,32,64,128]{3,2,1,0:T(8,128)(2,1)S(1)}, u32[]{:S(2)}, u32[]{:S(2)}) %collective-permute-start.4) | collective-permute-done | bytes 524320 | tf_op jit(solution)/shard_map/ppermute | solution.py:265
  9.8 2.7 %collective-permute-start.6 = (bf16[1,16,64,128]{3,2,1,0:T(8,128)(2,1)S(1)}, bf16[1,16,64,128]{3,2,1,0:T(8,128)(2,1)S(1)}, u32[]{:S(2)}, u32[]{:S(2)}) collective-permute-start(bf16[1,16,64,128]{3,2,1,0:T(8,128)(2,1)S(1)} %get-tuple-element.52), channel_id=1, source_target_pairs={{0,24},{8,0},{16,8},{24,16},{1,25},{9,1},{17,9},{25,17},{2,26},{10... | collective-permute-start | bytes 786440 | tf_op jit(solution)/shard_map/ppermute | solution.py:271
  12.9 2.7 %collective-permute-start.3 = (bf16[1,16,64,128]{3,2,1,0:T(8,128)(2,1)S(1)}, bf16[1,16,64,128]{3,2,1,0:T(8,128)(2,1)S(1)}, u32[]{:S(2)}, u32[]{:S(2)}) collective-permute-start(bf16[1,16,64,128]{3,2,1,0:T(8,128)(2,1)S(1)} %get-tuple-element.40), channel_id=1, source_target_pairs={{0,24},{8,0},{16,8},{24,16},{1,25},{9,1},{17,9},{25,17},{2,26},{10... | collective-permute-start | bytes 786440 | tf_op jit(solution)/shard_map/ppermute | solution.py:271
  15.5 2.9 %collective-permute-done.5.refs_2_ = bf16[1,16,64,128]{3,2,1,0:T(8,128)(2,1)S(1)} collective-permute-done((bf16[1,16,64,128]{3,2,1,0:T(8,128)(2,1)S(1)}, bf16[1,16,64,128]{3,2,1,0:T(8,128)(2,1)S(1)}, u32[]{:S(2)}, u32[]{:S(2)}) %collective-permute-start.5) | collective-permute-done | bytes 262176 | tf_op jit(solution)/shard_map/ppermute | solution.py:268
  18.5 0.9 relay_sum.1
  19.4 2.7 %collective-permute-start.8 = (bf16[1,16,64,128]{3,2,1,0:T(8,128)(2,1)S(1)}, bf16[1,16,64,128]{3,2,1,0:T(8,128)(2,1)S(1)}, u32[]{:S(2)}, u32[]{:S(2)}) collective-permute-start(bf16[1,16,64,128]{3,2,1,0:T(8,128)(2,1)S(1)} %get-tuple-element.54), channel_id=1, source_target_pairs={{0,24},{8,0},{16,8},{24,16},{1,25},{9,1},{17,9},{25,17},{2,26},{10... | collective-permute-start | bytes 786440 | tf_op jit(solution)/shard_map/ppermute | solution.py:271
  22.2 0.2 fusion.refs_0_
  22.5 1.6 %collective-permute-done.2.refs_2_ = bf16[1,16,64,128]{3,2,1,0:T(8,128)(2,1)S(1)} collective-permute-done((bf16[1,16,64,128]{3,2,1,0:T(8,128)(2,1)S(1)}, bf16[1,16,64,128]{3,2,1,0:T(8,128)(2,1)S(1)}, u32[]{:S(2)}, u32[]{:S(2)}) %collective-permute-start.2) | collective-permute-done | bytes 262176 | tf_op jit(solution)/shard_map/ppermute | solution.py:268
  24.3 5.0 %collective-permute-done.7.w_up_ref = bf16[1,16,64,128]{3,2,1,0:T(8,128)(2,1)S(1)} collective-permute-done((bf16[1,16,64,128]{3,2,1,0:T(8,128)(2,1)}, bf16[1,16,64,128]{3,2,1,0:T(8,128)(2,1)S(1)}, u32[]{:S(2)}, u32[]{:S(2)}) %collective-permute-start.7) | collective-permute-done | bytes 262176 | tf_op jit(solution)/shard_map/ppermute | solution.py:268
  29.4 20.5 %all_to_all.15.refs_1_ = bf16[8,256,128]{2,1,0:T(8,128)(2,1)S(1)} all-to-all(bf16[8,256,128]{2,1,0:T(8,128)(2,1)S(1)} %plane_sum.1), channel_id=1, replica_groups=mesh['z'=8,'y'=4,'core'=2,'mp'=4] {'z'}, dimensions={0} | all-to-all | bytes 1048576 | tf_op jit(solution)/shard_map/all_to_all | solution.py:306
  50.0 0.3 select.1
  50.3 12.7 %all_to_all.16.in_ref = bf16[8,128,128]{2,1,0:T(8,128)(2,1)S(1)} all-to-all(bf16[8,128,128]{2,1,0:T(8,128)(2,1)S(1)} %bitcast.5), channel_id=1, replica_groups=mesh['z'=8,'y'=4,'core'=2,'mp'=4] {'z'}, dimensions={0} | all-to-all | bytes 524288 | tf_op jit(solution)/shard_map/all_to_all | solution.py:308
  63.1 15.5 %all_to_all.17.in_ref.own_ref = bf16[16,2,64,128]{3,2,1,0:T(8,128)(2,1)S(1)} all-to-all(bf16[16,2,64,128]{3,2,1,0:T(8,128)(2,1)S(1)} %spread.1), channel_id=1, replica_groups=mesh['z'=8,'y'=4,'core'=2,'mp'=4] {'y','mp'}, dimensions={0} | all-to-all | bytes 1048576 | tf_op jit(solution)/shard_map/all_to_all | solution.py:310
  78.6 5.7 %collective-permute-start.9 = (bf16[16,64,128]{2,1,0:T(8,128)(2,1)S(1)}, bf16[16,64,128]{2,1,0:T(8,128)(2,1)S(1)}, u32[]{:S(2)}, u32[]{:S(2)}) collective-permute-start(bf16[16,64,128]{2,1,0:T(8,128)(2,1)S(1)} %for_other_core.1), channel_id=1, source_target_pairs={{0,4},{4,0},{1,5},{5,1},{2,6},{6,2},{3,7},{7,3},{8,12},{12,8},{9,1... | collective-permute-start | bytes 786440 | tf_op jit(solution)/shard_map/ppermute | solution.py:265
  84.3 1.2 %collective-permute-done.9.other_ref = bf16[16,64,128]{2,1,0:T(8,128)(2,1)S(1)} collective-permute-done((bf16[16,64,128]{2,1,0:T(8,128)(2,1)S(1)}, bf16[16,64,128]{2,1,0:T(8,128)(2,1)S(1)}, u32[]{:S(2)}, u32[]{:S(2)}) %collective-permute-start.9) | collective-permute-done | bytes 262176 | tf_op jit(solution)/shard_map/ppermute | solution.py:265
  85.5 6.3 %precondition.1 = (bf16[512,128]{1,0:T(8,128)(2,1)S(1)}, bf16[512,128]{1,0:T(8,128)(2,1)S(1)}) custom-call(s32[1]{0:T(128)} %bitcast.core_ref, s32[1]{0:T(128)} %bitcast.3.band_ref, bf16[16,2,64,128]{3,2,1,0:T(8,128)(2,1)S(1)} %all_to_all.17.in_ref.own_ref, bf16[16,64,128]{2,1,0:T(8,128)(2,1)S(1)} %collective-permute-done.9.other_ref), custom_call_target="tpu_custom_call" | custom-call | tf_op jit(solution)/shard_map/precondition/pallas_call | solution.py:314
  91.8 0.4 collective-permute-start.10
  92.1 4.4 %collective-permute-done.10.taken_ref = bf16[512,128]{1,0:T(8,128)(2,1)S(1)} collective-permute-done((bf16[512,128]{1,0:T(8,128)(2,1)S(1)}, bf16[512,128]{1,0:T(8,128)(2,1)S(1)}, u32[]{:S(2)}, u32[]{:S(2)}) %collective-permute-start.10) | collective-permute-done | bytes 131104 | tf_op jit(solution)/shard_map/ppermute | solution.py:323
  96.6 0.7 place.1
  (21 shorter events, 1.3 us)
Async XLA Ops:
  1.4 11.1 %copy-start = (s32[32]{0:T(128)S(1)}, s32[32]{0:T(128)}, u32[]{:S(2)}) copy-start(s32[32]{0:T(128)} %param.3) | copy-start | bytes 388
  3.1 9.5 %collective-permute-start.1 = (bf16[2,32,64,128]{3,2,1,0:T(8,128)(2,1)S(1)}, bf16[2,32,64,128]{3,2,1,0:T(8,128)(2,1)S(1)}, u32[]{:S(2)}, u32[]{:S(2)}) collective-permute-start(bf16[2,32,64,128]{3,2,1,0:T(8,128)(2,1)S(1)} %get-tuple-element.38), channel_id=1, source_target_pairs={{0,4},{4,0},{1,5},{5,1},{2,6},{6,2},{3,7},{7,3},{8,12},{12,8},{9,1... | collective-permute-start | bytes 3145736 | tf_op jit(solution)/shard_map/ppermute | solution.py:265
  6.5 3.0 %collective-permute-start.4 = (bf16[1,32,64,128]{3,2,1,0:T(8,128)(2,1)S(1)}, bf16[1,32,64,128]{3,2,1,0:T(8,128)(2,1)S(1)}, u32[]{:S(2)}, u32[]{:S(2)}) collective-permute-start(bf16[1,32,64,128]{3,2,1,0:T(8,128)(2,1)S(1)} %get-tuple-element.50), channel_id=1, source_target_pairs={{0,4},{4,0},{1,5},{5,1},{2,6},{6,2},{3,7},{7,3},{8,12},{12,8},{9,1... | collective-permute-start | bytes 1572872 | tf_op jit(solution)/shard_map/ppermute | solution.py:265
  7.9 14.5 %collective-permute-start = (bf16[1,32,64,128]{3,2,1,0:T(8,128)(2,1)S(1)}, bf16[1,32,64,128]{3,2,1,0:T(8,128)(2,1)S(1)}, u32[]{:S(2)}, u32[]{:S(2)}) collective-permute-start(bf16[1,32,64,128]{3,2,1,0:T(8,128)(2,1)S(1)} %get-tuple-element.36), channel_id=1, source_target_pairs={{0,4},{4,0},{1,5},{5,1},{2,6},{6,2},{3,7},{7,3},{8,12},{12,8},{9,1... | collective-permute-start | bytes 1572872 | tf_op jit(solution)/shard_map/ppermute | solution.py:265
  9.7 8.8 %collective-permute-start.5 = (bf16[1,16,64,128]{3,2,1,0:T(8,128)(2,1)S(1)}, bf16[1,16,64,128]{3,2,1,0:T(8,128)(2,1)S(1)}, u32[]{:S(2)}, u32[]{:S(2)}) collective-permute-start(bf16[1,16,64,128]{3,2,1,0:T(8,128)(2,1)S(1)} %get-tuple-element.51), channel_id=1, source_target_pairs={{0,8},{8,16},{16,24},{24,0},{1,9},{9,17},{17,25},{25,1},{2,10},{10... | collective-permute-start | bytes 786440 | tf_op jit(solution)/shard_map/ppermute | solution.py:268
  9.8 8.7 %collective-permute-start.6 = (bf16[1,16,64,128]{3,2,1,0:T(8,128)(2,1)S(1)}, bf16[1,16,64,128]{3,2,1,0:T(8,128)(2,1)S(1)}, u32[]{:S(2)}, u32[]{:S(2)}) collective-permute-start(bf16[1,16,64,128]{3,2,1,0:T(8,128)(2,1)S(1)} %get-tuple-element.52), channel_id=1, source_target_pairs={{0,24},{8,0},{16,8},{24,16},{1,25},{9,1},{17,9},{25,17},{2,26},{10... | collective-permute-start | bytes 786440 | tf_op jit(solution)/shard_map/ppermute | solution.py:271
  12.8 11.3 %collective-permute-start.2 = (bf16[1,16,64,128]{3,2,1,0:T(8,128)(2,1)S(1)}, bf16[1,16,64,128]{3,2,1,0:T(8,128)(2,1)S(1)}, u32[]{:S(2)}, u32[]{:S(2)}) collective-permute-start(bf16[1,16,64,128]{3,2,1,0:T(8,128)(2,1)S(1)} %get-tuple-element.39), channel_id=1, source_target_pairs={{0,8},{8,16},{16,24},{24,0},{1,9},{9,17},{17,25},{25,1},{2,10},{10... | collective-permute-start | bytes 786440 | tf_op jit(solution)/shard_map/ppermute | solution.py:268
  12.9 11.2 %collective-permute-start.3 = (bf16[1,16,64,128]{3,2,1,0:T(8,128)(2,1)S(1)}, bf16[1,16,64,128]{3,2,1,0:T(8,128)(2,1)S(1)}, u32[]{:S(2)}, u32[]{:S(2)}) collective-permute-start(bf16[1,16,64,128]{3,2,1,0:T(8,128)(2,1)S(1)} %get-tuple-element.40), channel_id=1, source_target_pairs={{0,24},{8,0},{16,8},{24,16},{1,25},{9,1},{17,9},{25,17},{2,26},{10... | collective-permute-start | bytes 786440 | tf_op jit(solution)/shard_map/ppermute | solution.py:271
  19.4 9.9 %collective-permute-start.7 = (bf16[1,16,64,128]{3,2,1,0:T(8,128)(2,1)}, bf16[1,16,64,128]{3,2,1,0:T(8,128)(2,1)S(1)}, u32[]{:S(2)}, u32[]{:S(2)}) collective-permute-start(bf16[1,16,64,128]{3,2,1,0:T(8,128)(2,1)} %get-tuple-element.53), channel_id=1, source_target_pairs={{0,8},{8,16},{16,24},{24,0},{1,9},{9,17},{17,25},{25,1},{2,10},{10... | collective-permute-start | bytes 786440 | tf_op jit(solution)/shard_map/ppermute | solution.py:268
  19.4 9.9 %collective-permute-start.8 = (bf16[1,16,64,128]{3,2,1,0:T(8,128)(2,1)S(1)}, bf16[1,16,64,128]{3,2,1,0:T(8,128)(2,1)S(1)}, u32[]{:S(2)}, u32[]{:S(2)}) collective-permute-start(bf16[1,16,64,128]{3,2,1,0:T(8,128)(2,1)S(1)} %get-tuple-element.54), channel_id=1, source_target_pairs={{0,24},{8,0},{16,8},{24,16},{1,25},{9,1},{17,9},{25,17},{2,26},{10... | collective-permute-start | bytes 786440 | tf_op jit(solution)/shard_map/ppermute | solution.py:271
  78.6 6.9 %collective-permute-start.9 = (bf16[16,64,128]{2,1,0:T(8,128)(2,1)S(1)}, bf16[16,64,128]{2,1,0:T(8,128)(2,1)S(1)}, u32[]{:S(2)}, u32[]{:S(2)}) collective-permute-start(bf16[16,64,128]{2,1,0:T(8,128)(2,1)S(1)} %for_other_core.1), channel_id=1, source_target_pairs={{0,4},{4,0},{1,5},{5,1},{2,6},{6,2},{3,7},{7,3},{8,12},{12,8},{9,1... | collective-permute-start | bytes 786440 | tf_op jit(solution)/shard_map/ppermute | solution.py:265
  91.8 4.8 %collective-permute-start.10 = (bf16[512,128]{1,0:T(8,128)(2,1)S(1)}, bf16[512,128]{1,0:T(8,128)(2,1)S(1)}, u32[]{:S(2)}, u32[]{:S(2)}) collective-permute-start(bf16[512,128]{1,0:T(8,128)(2,1)S(1)} %get-tuple-element.56), channel_id=1, source_target_pairs={{0,1},{1,0},{2,3},{3,2},{4,5},{5,4},{6,7},{7,6},{8,9},{9,8},{10,11... | collective-permute-start | bytes 393224 | tf_op jit(solution)/shard_map/ppermute | solution.py:323

commit v3 on v2

v3 whole, which is shorter than its diff:
```python
import math

import jax
import jax.numpy as jnp
from jax import lax
from jax.experimental import pallas as pl
from jax.experimental.pallas import tpu as pltpu
from jax.sharding import Mesh, PartitionSpec as P

ITERS = 3
MOST = 2
Z, Y, CORE, MP = 8, 4, 2, 4
DP = ("z", "y", "core")
IN_VMEM = pl.BlockSpec(memory_space=pltpu.VMEM)
IN_SMEM = pl.BlockSpec(memory_space=pltpu.SMEM)
IN_HBM = pl.BlockSpec(memory_space=pltpu.HBM)
PARAMS = pltpu.CompilerParams(vmem_limit_bytes=12 * 1024 * 1024)
LARGE = pltpu.CompilerParams(vmem_limit_bytes=24 * 1024 * 1024)


def block_of_slots(owner, core):
    blocks = owner.shape[0]
    positions = jnp.arange(blocks, dtype=jnp.int32)
    earlier = (owner[None, :] == owner[:, None]) & (positions[None, :] < positions[:, None])
    slot_of = owner * MOST + jnp.sum(earlier.astype(jnp.int32), axis=1)
    local = jnp.arange(Z * Y * MOST, dtype=jnp.int32)
    wanted = (local // MOST * CORE + core) * MOST + local % MOST
    found = slot_of[None, :] == wanted[:, None]
    return jnp.sum(jnp.where(found, positions[None, :] + 1, 0), axis=1) - 1


def dot(a, b):
    return jnp.dot(a, b, preferred_element_type=jnp.float32)


def dot16(a, b):
    return dot(a, b).astype(jnp.bfloat16)


def pieces_of(grads, which_core, y, shifts, name):
    blocks, extent, columns = grads.shape
    half = extent // CORE
    rows = half // Y
    cuts = 4
    group = blocks // cuts

    def kernel(core_ref, y_ref, in_ref, *refs):
        outs, sems = refs[:-1], refs[-1]
        copies = []
        for out_ref, entry in zip(outs, shifts):
            for i, shift in enumerate(entry):
                first = pl.multiple_of(core_ref[0] * half + (y_ref[0] + shift) % Y * rows, rows)
                for cut in range(cuts):
                    some = pl.ds(cut * group, group)
                    source = in_ref.at[some, pl.ds(first, rows)]
                    copies.append(
                        pltpu.make_async_copy(source, out_ref.at[i, some], sems.at[len(copies)])
                    )
        for copy in copies:
            copy.start()
        for copy in copies:
            copy.wait()

    return pl.pallas_call(
        kernel,
        out_shape=[pltpu.VMEM((len(entry), blocks, rows, columns), grads.dtype) for entry in shifts],
        in_specs=[IN_SMEM, IN_SMEM, IN_HBM],
        out_specs=[IN_VMEM] * len(shifts),
        scratch_shapes=[pltpu.SemaphoreType.DMA((cuts * sum(len(entry) for entry in shifts),))],
        compiler_params=PARAMS,
        name=name,
    )(which_core, y, pltpu.with_memory_space_constraint(grads, pltpu.HBM))


def add_parts(parts, arrays, dtype, name):
    count = [entry[0][3] for entry in parts]
    rows, columns = arrays[0].shape[-2:]

    def kernel(*refs):
        ins, outs = refs[: len(arrays)], refs[len(arrays) :]
        for entry, out in zip(parts, outs):

            def add(b, carry):
                total = None
                for which, index, first, _ in entry:
                    value = ins[which][index, first + b].astype(jnp.float32)
                    total = value if total is None else total + value
                out[0, b] = total.astype(dtype)
                return carry

            lax.fori_loop(0, entry[0][3], add, 0, unroll=4)

    return pl.pallas_call(
        kernel,
        out_shape=[pltpu.VMEM((1, n, rows, columns), dtype) for n in count],
        in_specs=[IN_VMEM] * len(arrays),
        out_specs=[IN_VMEM] * len(parts),
        compiler_params=PARAMS,
        name=name,
    )(*arrays)


def plane_kernel(own_a_ref, own_b_ref, w_up_ref, w_down_ref, out_ref):
    half, rows = own_a_ref.shape[1:3]
    stripe = rows // Z
    for first, one, two in ((0, own_a_ref, w_up_ref), (half, own_b_ref, w_down_ref)):

        def add(pair, carry):
            totals = [one[0, b] + two[0, b].astype(jnp.float32) for b in (2 * pair, 2 * pair + 1)]
            at = pl.multiple_of((first + 2 * pair) * stripe, 2 * stripe)
            for z in range(Z):
                both = [total[z * stripe : (z + 1) * stripe] for total in totals]
                out_ref[z, pl.ds(at, 2 * stripe)] = jnp.concatenate(both, axis=0).astype(jnp.bfloat16)
            return carry

        lax.fori_loop(0, half // 2, add, 0, unroll=2)


def plane_sum(own_a, own_b, w_up, w_down):
    half, rows, columns = own_a.shape[1:]
    return pl.pallas_call(
        plane_kernel,
        out_shape=pltpu.VMEM((Z, 2 * half * rows // Z, columns), jnp.bfloat16),
        in_specs=[IN_VMEM] * 4,
        out_specs=IN_VMEM,
        compiler_params=PARAMS,
        name="plane_sum",
    )(own_a, own_b, w_up, w_down)


def mean_rows(pieces, devices):
    def kernel(in_ref, out_ref):
        out_ref[...] = (jnp.sum(in_ref[...].astype(jnp.float32), axis=0) / devices).astype(jnp.bfloat16)

    return pl.pallas_call(
        kernel,
        out_shape=pltpu.VMEM(pieces.shape[1:], pieces.dtype),
        in_specs=[IN_VMEM],
        out_specs=IN_VMEM,
        compiler_params=PARAMS,
        name="mean_rows",
    )(pieces)


def select_kernel(core_ref, block_ref, mine_ref, other_ref, out_ref, both_ref):
    blocks, rows, columns = both_ref.shape
    mine = mine_ref[...].astype(jnp.float32).reshape(blocks, rows // CORE, columns)
    other = other_ref[...].astype(jnp.float32).reshape(blocks, rows // CORE, columns)
    first = core_ref[0] == 0
    halves = [jnp.where(first, mine, other), jnp.where(first, other, mine)]
    both_ref[...] = jnp.concatenate(halves, axis=1).astype(jnp.bfloat16)
    for device in range(Z * Y):
        for slot in range(MOST):
            block = block_ref[device * MOST + slot]
            value = both_ref[jnp.maximum(block, 0)]
            out_ref[device, slot] = jnp.where(block >= 0, value, jnp.zeros_like(value))


def select(core, block_of, mine, other, blocks):
    rows = mine.shape[0] // blocks * CORE
    columns = mine.shape[1]
    return pl.pallas_call(
        select_kernel,
        out_shape=pltpu.VMEM((Z * Y, MOST, rows, columns), mine.dtype),
        in_specs=[IN_SMEM, IN_SMEM, IN_VMEM, IN_VMEM],
        out_specs=IN_VMEM,
        scratch_shapes=[pltpu.VMEM((blocks, rows, columns), mine.dtype)],
        compiler_params=PARAMS,
        name="select",
    )(core, block_of, mine, other)


def bands_kernel(band_ref, in_ref, own_ref, next_ref):
    slot = band_ref[0] % MOST
    devices, _, rows, _ = in_ref.shape
    for device in range(devices):
        part = pl.ds(device * rows, rows)
        own_ref[part] = in_ref[device, slot]
        next_ref[part] = in_ref[device, 1 - slot]


def bands_of(band, arrived):
    devices, _, rows, columns = arrived.shape
    shape = pltpu.VMEM((devices * rows, columns), arrived.dtype)
    return pl.pallas_call(
        bands_kernel,
        out_shape=(shape, shape),
        in_specs=[IN_SMEM, IN_VMEM],
        out_specs=[IN_VMEM] * 2,
        compiler_params=PARAMS,
        name="bands",
    )(band, arrived)


def precondition_kernel(band0_ref, band1_ref, band2_ref, band3_ref, kept_ref, sent_ref):
    extent, columns = kept_ref.shape
    block = jnp.concatenate([band0_ref[...], band1_ref[...], band2_ref[...], band3_ref[...]], axis=1)
    row = lax.broadcasted_iota(jnp.int32, (extent, extent), 0)
    col = lax.broadcasted_iota(jnp.int32, (extent, extent), 1)
    five = jnp.where(row == col, jnp.float32(5.0), jnp.float32(0.0))
    right = lax.dot_general(block, block, (((0,), (0,)), ((), ())), preferred_element_type=jnp.float32)
    left = lax.dot_general(block, block, (((1,), (1,)), ((), ())), preferred_element_type=jnp.float32)
    moments, scales = [], []
    for stat in (right, left):
        total = jnp.sum(stat * stat, keepdims=True)
        scaling = 2.5 / jnp.sqrt(total + 1e-06)
        moments.append((scaling * stat).astype(jnp.bfloat16))
        scales.append(jnp.sqrt(jnp.sqrt(scaling)).astype(jnp.bfloat16).astype(jnp.float32))
    factors = [((five - m.astype(jnp.float32)) * 0.25).astype(jnp.bfloat16) for m in moments]
    roots = [(s * f.astype(jnp.float32)).astype(jnp.bfloat16) for s, f in zip(scales, factors)]
    for iteration in range(ITERS - 1):
        squares = [dot16(f, f) for f in factors]
        if iteration > 0:
            roots = [dot16(r, f) for r, f in zip(roots, factors)]
        fourths = [dot16(s, s) for s in squares]
        moments = [dot16(f, m) for f, m in zip(fourths, moments)]
        factors = [((five - m.astype(jnp.float32)) * 0.25).astype(jnp.bfloat16) for m in moments]
    right_root = dot16(roots[0], factors[0][:, : 2 * columns])
    right_half = dot16(block, right_root)
    left_root = dot16(roots[1], factors[1])
    product = math.sqrt(extent) * dot(left_root, right_half)
    stripe = extent // (Z * Y * CORE)
    pieces = []
    for core in range(CORE):
        for y in range(Y):
            for z in range(Z):
                first = ((z * Y + y) * CORE + core) * stripe
                pieces.append(product[first : first + stripe])
    product = jnp.concatenate(pieces, axis=0).astype(jnp.bfloat16)
    kept_ref[...] = product[:, :columns]
    sent_ref[...] = product[:, columns:]


def place_kernel(band_ref, kept_ref, taken_ref, out_ref, sems):
    slot = band_ref[0] % MOST
    one = pltpu.make_async_copy(kept_ref, out_ref.at[slot], sems.at[0])
    two = pltpu.make_async_copy(taken_ref, out_ref.at[1 - slot], sems.at[1])
    one.start()
    two.start()
    one.wait()
    two.wait()


def place(band, kept, taken):
    return pl.pallas_call(
        place_kernel,
        out_shape=jax.ShapeDtypeStruct((MOST,) + kept.shape, kept.dtype),
        in_specs=[IN_SMEM, IN_VMEM, IN_VMEM],
        out_specs=IN_HBM,
        scratch_shapes=[pltpu.SemaphoreType.DMA((2,))],
        compiler_params=PARAMS,
        name="place",
    )(band, kept, taken)


def on_device(grads, owner):
    local_grads = grads[0]
    block_count, extent, columns = local_grads.shape
    devices = Z * Y * CORE
    core = lax.axis_index("core").reshape(1).astype(jnp.int32)
    y = lax.axis_index("y").reshape(1).astype(jnp.int32)
    band = lax.axis_index("mp").reshape(1).astype(jnp.int32)
    block_of = block_of_slots(owner, core)

    def swap(value):
        return lax.ppermute(value, "core", [(0, 1), (1, 0)])

    def up(value):
        return lax.ppermute(value, "y", [(i, (i + 1) % Y) for i in range(Y)])

    def down(value):
        return lax.ppermute(value, "y", [(i, (i - 1) % Y) for i in range(Y)])

    def along(value, shift):
        return lax.ppermute(value, "mp", [(i, (i + shift) % MP) for i in range(MP)])

    n = block_count // 2
    shifts = ((2,), (1, 3), (0,))
    far, near, own = (swap(sent) for sent in pieces_of(local_grads, 1 - core, y, shifts, "sent"))
    kept_far, kept_near, kept_own = pieces_of(local_grads, core, y, shifts, "kept")
    v2a, v2b = add_parts(
        [[(0, 0, 0, n), (1, 0, 0, n)], [(0, 0, n, n), (1, 0, n, n)]], (kept_far, far), jnp.bfloat16, "far_sum"
    )
    from_down, from_up = up(v2a), down(v2b)
    v1b, v3a = add_parts(
        [[(0, 0, n, n), (1, 0, n, n)], [(0, 1, 0, n), (1, 1, 0, n)]], (kept_near, near), jnp.bfloat16, "near_sum"
    )
    v_up, v_down = up(v1b), down(v3a)
    kept_near, near, v1b, v3a = lax.optimization_barrier((kept_near, near, v1b, v3a))
    (w1a,) = add_parts(
        [[(0, 0, 0, n), (1, 0, 0, n), (2, 0, 0, n)]], (kept_near, near, from_down), jnp.bfloat16, "relay_up"
    )
    (w3b,) = add_parts(
        [[(0, 1, n, n), (1, 1, n, n), (2, 0, 0, n)]], (kept_near, near, from_up), jnp.bfloat16, "relay_down"
    )
    w_up, w_down = up(w1a), down(w3b)
    own_a, own_b = add_parts(
        [[(0, 0, 0, n), (1, 0, 0, n), (3, 0, 0, n)], [(0, 0, n, n), (1, 0, n, n), (2, 0, 0, n)]],
        (kept_own, own, v_up, v_down),
        jnp.float32,
        "own_sum",
    )
    own_a, own_b, block_of, band = lax.optimization_barrier((own_a, own_b, block_of, band))
    plane = plane_sum(own_a, own_b, w_up, w_down)
    mine = mean_rows(lax.all_to_all(plane, "z", split_axis=0, concat_axis=0, tiled=True), devices)

    outgoing = select(core, block_of, mine, swap(mine), block_count)
    arrived = lax.all_to_all(outgoing, ("z", "y"), split_axis=0, concat_axis=0, tiled=True)
    own_band, next_band = bands_of(band, arrived)
    bands = [own_band, along(next_band, 3), along(own_band, 2), along(next_band, 1)]

    result = pltpu.VMEM((extent, columns), jnp.bfloat16)
    kept, given = pl.pallas_call(
        precondition_kernel,
        out_shape=(result, result),
        in_specs=[IN_VMEM] * MP,
        out_specs=[IN_VMEM] * 2,
        compiler_params=LARGE,
        name="precondition",
    )(*bands)
    return place(band, kept, along(given, 1))


def solution(mesh):
    split = Mesh(mesh.devices.reshape(Z, Y, CORE, MP), ("z", "y", "core", "mp"))
    placed = (P(DP, None, None, "mp"), P())
    return jax.shard_map(
        on_device, mesh=split, in_specs=placed, out_specs=P(DP, None, "mp"), check_vma=False
    )
```

time: 97.7 us -> 93.3 us (0.955); the launches traced: 97.5 us -> 91.8 us
  blocking collectives: 48.8 us -> 37.3 us
  waiting for transfers between devices: 16.3 us -> 20.6 us
  starting transfers between devices: 18.2 us -> 20.8 us
  Pallas kernels: 13.4 us -> 12.4 us
    all_to_all x2 -> x1, blocking collectives: 28.2 us -> 15.6 us  [on_device(): lax.all_to_all(outgoing, ('z', 'y'), split_axis=0, concat_axis=0, tiled=T...]
    ppermute x1 -> x4, starting transfers between devices: 0.37 us -> 5.59 us  [along(): return lax.ppermute(value, 'mp', [(i, (i + shift) % MP) for i in range(MP)])]
    ppermute x1 -> x4, waiting for transfers between devices: 4.43 us -> 8.78 us  [along(): return lax.ppermute(value, 'mp', [(i, (i + shift) % MP) for i in range(MP)])]
    ppermute x4, starting transfers between devices: 9.62 us -> 7.01 us  [swap(): return lax.ppermute(value, 'core', [(0, 1), (1, 0)])]
    all_to_all x1, blocking collectives: 20.5 us -> 21.7 us  [on_device(): lax.all_to_all(plane, 'z', split_axis=0, concat_axis=0, tiled=True)]
    pallas_call x6 -> x5, Pallas kernels: 4.88 us -> 4.3 us  [the longest x2 3.49 us: pieces_of(): pl.pallas_call(kernel, out_shape=[pltpu.VMEM((len(entry), blocks, rows, c...]
  transfers between devices with their start and end apart: 11 -> 14, of which waited for: 6 -> 7; matrix products, arithmetic and copies ran while one was open for 1% -> 0% of each run, Pallas kernels for 3% -> 3%
where the time goes in v3:
time: 93.3 us; the launch traced here: 91.8 us
  blocking collectives  37.3 us (40%)
  starting transfers between devices  20.8 us (22%)
  waiting for transfers between devices  20.6 us (22%)
  Pallas kernels  12.4 us (13%)
    all_to_all x1, blocking collectives, on_device(): lax.all_to_all(plane, 'z', split_axis=0, concat_axis=0, tiled=True)  21.7 us
    all_to_all x1, blocking collectives, on_device(): lax.all_to_all(outgoing, ('z', 'y'), split_axis=0, concat_axis=0, tiled=T...  15.6 us
    ppermute x3, waiting for transfers between devices, up(): return lax.ppermute(value, 'y', [(i, (i + 1) % Y) for i in range(Y)])  10.4 us
    ppermute x4, waiting for transfers between devices, along(): return lax.ppermute(value, 'mp', [(i, (i + shift) % MP) for i in range(MP)])  8.78 us
    ppermute x3, starting transfers between devices, down(): return lax.ppermute(value, 'y', [(i, (i - 1) % Y) for i in range(Y)])  8.06 us
    ppermute x4, starting transfers between devices, swap(): return lax.ppermute(value, 'core', [(0, 1), (1, 0)])  7.01 us
    pallas_call x1, Pallas kernels, on_device(): pl.pallas_call(precondition_kernel, out_shape=(result, result), in_specs=...  5.89 us
    ppermute x4, starting transfers between devices, along(): return lax.ppermute(value, 'mp', [(i, (i + shift) % MP) for i in range(MP)])  5.59 us
  transfers between devices with their start and end apart: 14, of which 7 were waited for; matrix products, arithmetic and copies ran while one was open for 0% of the time, Pallas kernels for 3%

profile of v3, /device:TPU:1, one launch (start us, length us, event | category | flops | bytes accessed | tf_op | source)
XLA Modules:
  0.0 91.8 jit_solution(8838463592486488360)
XLA Ops:
  0.0 1.8 %sent.1 = (bf16[1,32,64,128]{3,2,1,0:T(8,128)(2,1)S(1)}, bf16[2,32,64,128]{3,2,1,0:T(8,128)(2,1)S(1)}, bf16[1,32,64,128]{3,2,1,0:T(8,128)(2,1)S(1)}) custom-call(s32[1]{0:T(128)S(6)} %sub.13.core_ref, s32[1]{0:T(128)} %bitcast.1.y_ref, bf16[32,512,128]{2,1,0:T(8,128)(2,1)} %bitcast.4), custom_call_target="tpu_custom_call" | custom-call | tf_op jit(solution)/shard_map/sent/pallas_call | solution.py:64
  1.8 3.3 %collective-permute-start.1 = (bf16[2,32,64,128]{3,2,1,0:T(8,128)(2,1)S(1)}, bf16[2,32,64,128]{3,2,1,0:T(8,128)(2,1)S(1)}, u32[]{:S(2)}, u32[]{:S(2)}) collective-permute-start(bf16[2,32,64,128]{3,2,1,0:T(8,128)(2,1)S(1)} %get-tuple-element.30), channel_id=1, source_target_pairs={{0,4},{4,0},{1,5},{5,1},{2,6},{6,2},{3,7},{7,3},{8,12},{12,8},{9,1... | collective-permute-start | bytes 3145736 | tf_op jit(solution)/shard_map/ppermute | solution.py:266
  5.2 0.4 collective-permute-start
  5.6 1.7 %kept.1 = (bf16[1,32,64,128]{3,2,1,0:T(8,128)(2,1)S(1)}, bf16[2,32,64,128]{3,2,1,0:T(8,128)(2,1)S(1)}, bf16[1,32,64,128]{3,2,1,0:T(8,128)(2,1)S(1)}) custom-call(s32[1]{0:T(128)} %bitcast.core_ref, s32[1]{0:T(128)} %bitcast.1.y_ref, bf16[32,512,128]{2,1,0:T(8,128)(2,1)} %bitcast.5), custom_call_target="tpu_custom_call" | custom-call | tf_op jit(solution)/shard_map/kept/pallas_call | solution.py:64
  7.5 0.6 collective-permute-done.4.refs_1_
  8.4 2.7 %collective-permute-start.7 = (bf16[1,16,64,128]{3,2,1,0:T(8,128)(2,1)S(1)}, bf16[1,16,64,128]{3,2,1,0:T(8,128)(2,1)S(1)}, u32[]{:S(2)}, u32[]{:S(2)}) collective-permute-start(bf16[1,16,64,128]{3,2,1,0:T(8,128)(2,1)S(1)} %get-tuple-element.44), channel_id=1, source_target_pairs={{0,24},{8,0},{16,8},{24,16},{1,25},{9,1},{17,9},{25,17},{2,26},{10... | collective-permute-start | bytes 786440 | tf_op jit(solution)/shard_map/ppermute | solution.py:272
  11.1 0.8 near_sum.1
  11.9 2.7 %collective-permute-start.3 = (bf16[1,16,64,128]{3,2,1,0:T(8,128)(2,1)S(1)}, bf16[1,16,64,128]{3,2,1,0:T(8,128)(2,1)S(1)}, u32[]{:S(2)}, u32[]{:S(2)}) collective-permute-start(bf16[1,16,64,128]{3,2,1,0:T(8,128)(2,1)S(1)} %get-tuple-element.32), channel_id=1, source_target_pairs={{0,24},{8,0},{16,8},{24,16},{1,25},{9,1},{17,9},{25,17},{2,26},{10... | collective-permute-start | bytes 786440 | tf_op jit(solution)/shard_map/ppermute | solution.py:272
  14.6 2.5 %collective-permute-done.5.refs_2_ = bf16[1,16,64,128]{3,2,1,0:T(8,128)(2,1)S(1)} collective-permute-done((bf16[1,16,64,128]{3,2,1,0:T(8,128)(2,1)S(1)}, bf16[1,16,64,128]{3,2,1,0:T(8,128)(2,1)S(1)}, u32[]{:S(2)}, u32[]{:S(2)}) %collective-permute-start.5) | collective-permute-done | bytes 262176 | tf_op jit(solution)/shard_map/ppermute | solution.py:269
  17.4 2.7 %collective-permute-start.8 = (bf16[1,16,64,128]{3,2,1,0:T(8,128)(2,1)S(1)}, bf16[1,16,64,128]{3,2,1,0:T(8,128)(2,1)S(1)}, u32[]{:S(2)}, u32[]{:S(2)}) collective-permute-start(bf16[1,16,64,128]{3,2,1,0:T(8,128)(2,1)S(1)} %relay_down.1), channel_id=1, source_target_pairs={{0,24},{8,0},{16,8},{24,16},{1,25},{9,1},{17,9},{25,17},{2,26},{10... | collective-permute-start | bytes 786440 | tf_op jit(solution)/shard_map/ppermute | solution.py:272
  20.3 2.4 %collective-permute-done.2.refs_2_ = bf16[1,16,64,128]{3,2,1,0:T(8,128)(2,1)S(1)} collective-permute-done((bf16[1,16,64,128]{3,2,1,0:T(8,128)(2,1)}, bf16[1,16,64,128]{3,2,1,0:T(8,128)(2,1)S(1)}, u32[]{:S(2)}, u32[]{:S(2)}) %collective-permute-start.2) | collective-permute-done | bytes 262176 | tf_op jit(solution)/shard_map/ppermute | solution.py:269
  22.9 5.4 %collective-permute-done.6.w_up_ref = bf16[1,16,64,128]{3,2,1,0:T(8,128)(2,1)S(1)} collective-permute-done((bf16[1,16,64,128]{3,2,1,0:T(8,128)(2,1)S(1)}, bf16[1,16,64,128]{3,2,1,0:T(8,128)(2,1)S(1)}, u32[]{:S(2)}, u32[]{:S(2)}) %collective-permute-start.6) | collective-permute-done | bytes 262176 | tf_op jit(solution)/shard_map/ppermute | solution.py:269
  28.5 21.7 %all_to_all.10.in_ref = bf16[8,256,128]{2,1,0:T(8,128)(2,1)S(1)} all-to-all(bf16[8,256,128]{2,1,0:T(8,128)(2,1)S(1)} %plane_sum.1), channel_id=1, replica_groups=mesh['z'=8,'y'=4,'core'=2,'mp'=4] {'z'}, dimensions={0} | all-to-all | bytes 1048576 | tf_op jit(solution)/shard_map/all_to_all | solution.py:305
  50.3 3.2 %collective-permute-start.9 = (bf16[256,128]{1,0:T(8,128)(2,1)S(1)}, bf16[256,128]{1,0:T(8,128)(2,1)S(1)}, u32[]{:S(2)}, u32[]{:S(2)}) collective-permute-start(bf16[256,128]{1,0:T(8,128)(2,1)S(1)} %mean_rows.1.mine_ref), channel_id=1, source_target_pairs={{0,4},{4,0},{1,5},{5,1},{2,6},{6,2},{3,7},{7,3},{8,12},{12,8},{9,1... | collective-permute-start | bytes 196616 | tf_op jit(solution)/shard_map/ppermute | solution.py:266
  53.5 0.9 collective-permute-done.9.other_ref
  54.4 0.7 select.11
  55.1 15.6 %all_to_all.11.in_ref = bf16[32,2,16,128]{3,2,1,0:T(8,128)(2,1)S(1)} all-to-all(bf16[32,2,16,128]{3,2,1,0:T(8,128)(2,1)S(1)} %select.11), channel_id=1, replica_groups=mesh['z'=8,'y'=4,'core'=2,'mp'=4] {'z','y'}, dimensions={0} | all-to-all | bytes 524288 | tf_op jit(solution)/shard_map/all_to_all | solution.py:308
  70.7 2.8 %collective-permute-start.11 = (bf16[512,128]{1,0:T(8,128)(2,1)S(1)}, bf16[512,128]{1,0:T(8,128)(2,1)S(1)}, u32[]{:S(2)}, u32[]{:S(2)}) collective-permute-start(bf16[512,128]{1,0:T(8,128)(2,1)S(1)} %get-tuple-element.45.band0_ref), channel_id=1, source_target_pairs={{0,2},{1,3},{2,0},{3,1},{4,6},{5,7},{6,4},{7,5},{8,10},{9,11},{10,... | collective-permute-start | bytes 393224 | tf_op jit(solution)/shard_map/ppermute | solution.py:275
  73.5 0.3 collective-permute-start.12
  73.8 2.4 %collective-permute-start.10 = (bf16[512,128]{1,0:T(8,128)(2,1)S(1)}, bf16[512,128]{1,0:T(8,128)(2,1)S(1)}, u32[]{:S(2)}, u32[]{:S(2)}) collective-permute-start(bf16[512,128]{1,0:T(8,128)(2,1)S(1)} %get-tuple-element.46), channel_id=1, source_target_pairs={{0,3},{1,0},{2,1},{3,2},{4,7},{5,4},{6,5},{7,6},{8,11},{9,8},{10,9... | collective-permute-start | bytes 393224 | tf_op jit(solution)/shard_map/ppermute | solution.py:275
  76.2 3.8 %collective-permute-done.12.band3_ref = bf16[512,128]{1,0:T(8,128)(2,1)S(1)} collective-permute-done((bf16[512,128]{1,0:T(8,128)(2,1)S(1)}, bf16[512,128]{1,0:T(8,128)(2,1)S(1)}, u32[]{:S(2)}, u32[]{:S(2)}) %collective-permute-start.12) | collective-permute-done | bytes 131104 | tf_op jit(solution)/shard_map/ppermute | solution.py:275
  80.0 5.9 %precondition.1 = (bf16[512,128]{1,0:T(8,128)(2,1)S(1)}, bf16[512,128]{1,0:T(8,128)(2,1)S(1)}) custom-call(bf16[512,128]{1,0:T(8,128)(2,1)S(1)} %get-tuple-element.45.band0_ref, bf16[512,128]{1,0:T(8,128)(2,1)S(1)} %collective-permute-done.10.band1_ref, bf16[512,128]{1,0:T(8,128)(2,1)S(1)} %collective-permute-done.11.band2_ref, ...), custom_call_target="tpu_custom_call" | custom-call | tf_op jit(solution)/shard_map/precondition/pallas_call | solution.py:313
  86.0 5.0 %collective-permute-done.13.taken_ref = bf16[512,128]{1,0:T(8,128)(2,1)S(1)} collective-permute-done((bf16[512,128]{1,0:T(8,128)(2,1)S(1)}, bf16[512,128]{1,0:T(8,128)(2,1)S(1)}, u32[]{:S(2)}, u32[]{:S(2)}) %collective-permute-start.13) | collective-permute-done | bytes 131104 | tf_op jit(solution)/shard_map/ppermute | solution.py:275
  91.0 0.7 place.1
  (26 shorter events, 1.4 us)
Async XLA Ops:
  0.0 7.4 %copy-start = (s32[32]{0:T(128)S(1)}, s32[32]{0:T(128)}, u32[]{:S(2)}) copy-start(s32[32]{0:T(128)} %param.3) | copy-start | bytes 388
  1.8 9.3 %collective-permute-start.1 = (bf16[2,32,64,128]{3,2,1,0:T(8,128)(2,1)S(1)}, bf16[2,32,64,128]{3,2,1,0:T(8,128)(2,1)S(1)}, u32[]{:S(2)}, u32[]{:S(2)}) collective-permute-start(bf16[2,32,64,128]{3,2,1,0:T(8,128)(2,1)S(1)} %get-tuple-element.30), channel_id=1, source_target_pairs={{0,4},{4,0},{1,5},{5,1},{2,6},{6,2},{3,7},{7,3},{8,12},{12,8},{9,1... | collective-permute-start | bytes 3145736 | tf_op jit(solution)/shard_map/ppermute | solution.py:266
  5.1 3.0 %collective-permute-start.4 = (bf16[1,32,64,128]{3,2,1,0:T(8,128)(2,1)S(1)}, bf16[1,32,64,128]{3,2,1,0:T(8,128)(2,1)S(1)}, u32[]{:S(2)}, u32[]{:S(2)}) collective-permute-start(bf16[1,32,64,128]{3,2,1,0:T(8,128)(2,1)S(1)} %get-tuple-element.42), channel_id=1, source_target_pairs={{0,4},{4,0},{1,5},{5,1},{2,6},{6,2},{3,7},{7,3},{8,12},{12,8},{9,1... | collective-permute-start | bytes 1572872 | tf_op jit(solution)/shard_map/ppermute | solution.py:266
  5.2 15.1 %collective-permute-start = (bf16[1,32,64,128]{3,2,1,0:T(8,128)(2,1)S(1)}, bf16[1,32,64,128]{3,2,1,0:T(8,128)(2,1)S(1)}, u32[]{:S(2)}, u32[]{:S(2)}) collective-permute-start(bf16[1,32,64,128]{3,2,1,0:T(8,128)(2,1)S(1)} %get-tuple-element.28), channel_id=1, source_target_pairs={{0,4},{4,0},{1,5},{5,1},{2,6},{6,2},{3,7},{7,3},{8,12},{12,8},{9,1... | collective-permute-start | bytes 1572872 | tf_op jit(solution)/shard_map/ppermute | solution.py:266
  8.3 8.8 %collective-permute-start.5 = (bf16[1,16,64,128]{3,2,1,0:T(8,128)(2,1)S(1)}, bf16[1,16,64,128]{3,2,1,0:T(8,128)(2,1)S(1)}, u32[]{:S(2)}, u32[]{:S(2)}) collective-permute-start(bf16[1,16,64,128]{3,2,1,0:T(8,128)(2,1)S(1)} %get-tuple-element.43), channel_id=1, source_target_pairs={{0,8},{8,16},{16,24},{24,0},{1,9},{9,17},{17,25},{25,1},{2,10},{10... | collective-permute-start | bytes 786440 | tf_op jit(solution)/shard_map/ppermute | solution.py:269
  8.4 8.9 %collective-permute-start.7 = (bf16[1,16,64,128]{3,2,1,0:T(8,128)(2,1)S(1)}, bf16[1,16,64,128]{3,2,1,0:T(8,128)(2,1)S(1)}, u32[]{:S(2)}, u32[]{:S(2)}) collective-permute-start(bf16[1,16,64,128]{3,2,1,0:T(8,128)(2,1)S(1)} %get-tuple-element.44), channel_id=1, source_target_pairs={{0,24},{8,0},{16,8},{24,16},{1,25},{9,1},{17,9},{25,17},{2,26},{10... | collective-permute-start | bytes 786440 | tf_op jit(solution)/shard_map/ppermute | solution.py:272
  11.9 10.8 %collective-permute-start.2 = (bf16[1,16,64,128]{3,2,1,0:T(8,128)(2,1)}, bf16[1,16,64,128]{3,2,1,0:T(8,128)(2,1)S(1)}, u32[]{:S(2)}, u32[]{:S(2)}) collective-permute-start(bf16[1,16,64,128]{3,2,1,0:T(8,128)(2,1)} %get-tuple-element.31), channel_id=1, source_target_pairs={{0,8},{8,16},{16,24},{24,0},{1,9},{9,17},{17,25},{25,1},{2,10},{10... | collective-permute-start | bytes 786440 | tf_op jit(solution)/shard_map/ppermute | solution.py:269
  11.9 10.8 %collective-permute-start.3 = (bf16[1,16,64,128]{3,2,1,0:T(8,128)(2,1)S(1)}, bf16[1,16,64,128]{3,2,1,0:T(8,128)(2,1)S(1)}, u32[]{:S(2)}, u32[]{:S(2)}) collective-permute-start(bf16[1,16,64,128]{3,2,1,0:T(8,128)(2,1)S(1)} %get-tuple-element.32), channel_id=1, source_target_pairs={{0,24},{8,0},{16,8},{24,16},{1,25},{9,1},{17,9},{25,17},{2,26},{10... | collective-permute-start | bytes 786440 | tf_op jit(solution)/shard_map/ppermute | solution.py:272
  17.2 11.1 %collective-permute-start.6 = (bf16[1,16,64,128]{3,2,1,0:T(8,128)(2,1)S(1)}, bf16[1,16,64,128]{3,2,1,0:T(8,128)(2,1)S(1)}, u32[]{:S(2)}, u32[]{:S(2)}) collective-permute-start(bf16[1,16,64,128]{3,2,1,0:T(8,128)(2,1)S(1)} %relay_up.1), channel_id=1, source_target_pairs={{0,8},{8,16},{16,24},{24,0},{1,9},{9,17},{17,25},{25,1},{2,10},{10... | collective-permute-start | bytes 786440 | tf_op jit(solution)/shard_map/ppermute | solution.py:269
  17.4 10.9 %collective-permute-start.8 = (bf16[1,16,64,128]{3,2,1,0:T(8,128)(2,1)S(1)}, bf16[1,16,64,128]{3,2,1,0:T(8,128)(2,1)S(1)}, u32[]{:S(2)}, u32[]{:S(2)}) collective-permute-start(bf16[1,16,64,128]{3,2,1,0:T(8,128)(2,1)S(1)} %relay_down.1), channel_id=1, source_target_pairs={{0,24},{8,0},{16,8},{24,16},{1,25},{9,1},{17,9},{25,17},{2,26},{10... | collective-permute-start | bytes 786440 | tf_op jit(solution)/shard_map/ppermute | solution.py:272
  50.3 4.1 %collective-permute-start.9 = (bf16[256,128]{1,0:T(8,128)(2,1)S(1)}, bf16[256,128]{1,0:T(8,128)(2,1)S(1)}, u32[]{:S(2)}, u32[]{:S(2)}) collective-permute-start(bf16[256,128]{1,0:T(8,128)(2,1)S(1)} %mean_rows.1.mine_ref), channel_id=1, source_target_pairs={{0,4},{4,0},{1,5},{5,1},{2,6},{6,2},{3,7},{7,3},{8,12},{12,8},{9,1... | collective-permute-start | bytes 196616 | tf_op jit(solution)/shard_map/ppermute | solution.py:266
  70.7 5.5 %collective-permute-start.11 = (bf16[512,128]{1,0:T(8,128)(2,1)S(1)}, bf16[512,128]{1,0:T(8,128)(2,1)S(1)}, u32[]{:S(2)}, u32[]{:S(2)}) collective-permute-start(bf16[512,128]{1,0:T(8,128)(2,1)S(1)} %get-tuple-element.45.band0_ref), channel_id=1, source_target_pairs={{0,2},{1,3},{2,0},{3,1},{4,6},{5,7},{6,4},{7,5},{8,10},{9,11},{10,... | collective-permute-start | bytes 393224 | tf_op jit(solution)/shard_map/ppermute | solution.py:275
  73.5 6.4 %collective-permute-start.12 = (bf16[512,128]{1,0:T(8,128)(2,1)S(1)}, bf16[512,128]{1,0:T(8,128)(2,1)S(1)}, u32[]{:S(2)}, u32[]{:S(2)}) collective-permute-start(bf16[512,128]{1,0:T(8,128)(2,1)S(1)} %get-tuple-element.46), channel_id=1, source_target_pairs={{0,1},{1,2},{2,3},{3,0},{4,5},{5,6},{6,7},{7,4},{8,9},{9,10},{10,1... | collective-permute-start | bytes 393224 | tf_op jit(solution)/shard_map/ppermute | solution.py:275
  73.8 6.1 %collective-permute-start.10 = (bf16[512,128]{1,0:T(8,128)(2,1)S(1)}, bf16[512,128]{1,0:T(8,128)(2,1)S(1)}, u32[]{:S(2)}, u32[]{:S(2)}) collective-permute-start(bf16[512,128]{1,0:T(8,128)(2,1)S(1)} %get-tuple-element.46), channel_id=1, source_target_pairs={{0,3},{1,0},{2,1},{3,2},{4,7},{5,4},{6,5},{7,6},{8,11},{9,8},{10,9... | collective-permute-start | bytes 393224 | tf_op jit(solution)/shard_map/ppermute | solution.py:275
  85.9 5.1 %collective-permute-start.13 = (bf16[512,128]{1,0:T(8,128)(2,1)S(1)}, bf16[512,128]{1,0:T(8,128)(2,1)S(1)}, u32[]{:S(2)}, u32[]{:S(2)}) collective-permute-start(bf16[512,128]{1,0:T(8,128)(2,1)S(1)} %get-tuple-element.48), channel_id=1, source_target_pairs={{0,1},{1,2},{2,3},{3,0},{4,5},{5,6},{6,7},{7,4},{8,9},{9,10},{10,1... | collective-permute-start | bytes 393224 | tf_op jit(solution)/shard_map/ppermute | solution.py:275

commit v4 on v3

--- a/solution.py
+++ b/solution.py
@@ -18,15 +18,17 @@
 LARGE = pltpu.CompilerParams(vmem_limit_bytes=24 * 1024 * 1024)
 
 
-def block_of_slots(owner, core):
-    blocks = owner.shape[0]
+def selection(owner, core, blocks, stripe):
     positions = jnp.arange(blocks, dtype=jnp.int32)
     earlier = (owner[None, :] == owner[:, None]) & (positions[None, :] < positions[:, None])
     slot_of = owner * MOST + jnp.sum(earlier.astype(jnp.int32), axis=1)
-    local = jnp.arange(Z * Y * MOST, dtype=jnp.int32)
-    wanted = (local // MOST * CORE + core) * MOST + local % MOST
-    found = slot_of[None, :] == wanted[:, None]
-    return jnp.sum(jnp.where(found, positions[None, :] + 1, 0), axis=1) - 1
+    device = slot_of // MOST
+    local = jnp.where(device % CORE == core, device // CORE * MOST + slot_of % MOST, Z * Y * MOST)
+    half = jnp.arange(CORE, dtype=jnp.int32)[:, None, None]
+    row = jnp.arange(stripe, dtype=jnp.int32)[None, None, :]
+    wanted = ((local[None, :, None] * CORE + half) * stripe + row).reshape(1, CORE * blocks * stripe)
+    rows = jnp.arange(Z * Y * MOST * CORE * stripe, dtype=jnp.int32)
+    return (wanted == rows[:, None]).astype(jnp.bfloat16)
 
 
 def dot(a, b):
@@ -100,74 +102,98 @@
     )(*arrays)
 
 
-def plane_kernel(own_a_ref, own_b_ref, w_up_ref, w_down_ref, out_ref):
+def plane_kernel(z_ref, own_a_ref, own_b_ref, w_up_ref, w_down_ref, sent_a_ref, sent_b_ref, kept_ref):
     half, rows = own_a_ref.shape[1:3]
     stripe = rows // Z
-    for first, one, two in ((0, own_a_ref, w_up_ref), (half, own_b_ref, w_down_ref)):
+    even = z_ref[0] % 2 == 0
+    for first, one, two, sent in (
+        (0, own_a_ref, w_up_ref, sent_a_ref),
+        (half, own_b_ref, w_down_ref, sent_b_ref),
+    ):
 
         def add(pair, carry):
             totals = [one[0, b] + two[0, b].astype(jnp.float32) for b in (2 * pair, 2 * pair + 1)]
-            at = pl.multiple_of((first + 2 * pair) * stripe, 2 * stripe)
-            for z in range(Z):
-                both = [total[z * stripe : (z + 1) * stripe] for total in totals]
-                out_ref[z, pl.ds(at, 2 * stripe)] = jnp.concatenate(both, axis=0).astype(jnp.bfloat16)
+            at = pl.multiple_of(2 * pair * stripe, 2 * stripe)
+            for q in range(Z // 2):
+                both = []
+                for z in (2 * q, 2 * q + 1):
+                    both.append(jnp.concatenate([t[z * stripe : (z + 1) * stripe] for t in totals], axis=0))
+                sent[q, pl.ds(at, 2 * stripe)] = jnp.where(even, both[1], both[0]).astype(jnp.bfloat16)
+                kept_ref[q, pl.ds(first * stripe + at, 2 * stripe)] = jnp.where(even, both[0], both[1])
             return carry
 
         lax.fori_loop(0, half // 2, add, 0, unroll=2)
 
 
-def plane_sum(own_a, own_b, w_up, w_down):
+def plane_sum(z, own_a, own_b, w_up, w_down):
     half, rows, columns = own_a.shape[1:]
+    count = half * rows // Z
+    sent = pltpu.VMEM((Z // 2, count, columns), jnp.bfloat16)
     return pl.pallas_call(
         plane_kernel,
-        out_shape=pltpu.VMEM((Z, 2 * half * rows // Z, columns), jnp.bfloat16),
-        in_specs=[IN_VMEM] * 4,
+        out_shape=(sent, sent, pltpu.VMEM((Z // 2, 2 * count, columns), jnp.float32)),
+        in_specs=[IN_SMEM] + [IN_VMEM] * 4,
+        out_specs=[IN_VMEM] * 3,
+        compiler_params=PARAMS,
+        name="plane_sum",
+    )(z, own_a, own_b, w_up, w_down)
+
+
+def parity_kernel(z_ref, kept_ref, a_ref, b_ref, far_ref, up_ref, down_ref, own_ref):
+    count = a_ref.shape[1]
+    for step, out_ref in ((2, far_ref), (1, up_ref), (3, down_ref), (0, own_ref)):
+        q = (z_ref[0] // 2 + step) % (Z // 2)
+        for first, ref in ((0, a_ref), (count, b_ref)):
+            part = pl.ds(first, count)
+            out_ref[part] = (kept_ref[q, part] + ref[q].astype(jnp.float32)).astype(out_ref.dtype)
+
+
+def parity_sum(z, kept, a, b):
+    shape = kept.shape[1:]
+    sent = pltpu.VMEM(shape, jnp.bfloat16)
+    return pl.pallas_call(
+        parity_kernel,
+        out_shape=(sent, sent, sent, pltpu.VMEM(shape, jnp.float32)),
+        in_specs=[IN_SMEM] + [IN_VMEM] * 3,
+        out_specs=[IN_VMEM] * 4,
+        compiler_params=PARAMS,
+        name="parity_sum",
+    )(z, kept, a, b)
+
+
+def mean_rows(own, received, devices):
+    def kernel(own_ref, *refs):
+        total = own_ref[...]
+        for ref in refs[:-1]:
+            total = total + ref[...].astype(jnp.float32)
+        refs[-1][...] = (total / devices).astype(jnp.bfloat16)
+
+    return pl.pallas_call(
+        kernel,
+        out_shape=pltpu.VMEM(own.shape, jnp.bfloat16),
+        in_specs=[IN_VMEM] * (1 + len(received)),
         out_specs=IN_VMEM,
         compiler_params=PARAMS,
-        name="plane_sum",
-    )(own_a, own_b, w_up, w_down)
-
-
-def mean_rows(pieces, devices):
-    def kernel(in_ref, out_ref):
-        out_ref[...] = (jnp.sum(in_ref[...].astype(jnp.float32), axis=0) / devices).astype(jnp.bfloat16)
-
-    return pl.pallas_call(
-        kernel,
-        out_shape=pltpu.VMEM(pieces.shape[1:], pieces.dtype),
-        in_specs=[IN_VMEM],
+        name="mean_rows",
+    )(own, *received)
+
+
+def select_kernel(core_ref, chosen_ref, mine_ref, other_ref, out_ref):
+    first = core_ref[0] == 0
+    mine, other = mine_ref[...], other_ref[...]
+    both = [jnp.where(first, mine, other), jnp.where(first, other, mine)]
+    out_ref[...] = dot16(chosen_ref[...], jnp.concatenate(both, axis=0))
+
+
+def select(core, chosen, mine, other):
+    return pl.pallas_call(
+        select_kernel,
+        out_shape=pltpu.VMEM((chosen.shape[0], mine.shape[1]), mine.dtype),
+        in_specs=[IN_SMEM, IN_VMEM, IN_VMEM, IN_VMEM],
         out_specs=IN_VMEM,
         compiler_params=PARAMS,
-        name="mean_rows",
-    )(pieces)
-
-
-def select_kernel(core_ref, block_ref, mine_ref, other_ref, out_ref, both_ref):
-    blocks, rows, columns = both_ref.shape
-    mine = mine_ref[...].astype(jnp.float32).reshape(blocks, rows // CORE, columns)
-    other = other_ref[...].astype(jnp.float32).reshape(blocks, rows // CORE, columns)
-    first = core_ref[0] == 0
-    halves = [jnp.where(first, mine, other), jnp.where(first, other, mine)]
-    both_ref[...] = jnp.concatenate(halves, axis=1).astype(jnp.bfloat16)
-    for device in range(Z * Y):
-        for slot in range(MOST):
-            block = block_ref[device * MOST + slot]
-            value = both_ref[jnp.maximum(block, 0)]
-            out_ref[device, slot] = jnp.where(block >= 0, value, jnp.zeros_like(value))
-
-
-def select(core, block_of, mine, other, blocks):
-    rows = mine.shape[0] // blocks * CORE
-    columns = mine.shape[1]
-    return pl.pallas_call(
-        select_kernel,
-        out_shape=pltpu.VMEM((Z * Y, MOST, rows, columns), mine.dtype),
-        in_specs=[IN_SMEM, IN_SMEM, IN_VMEM, IN_VMEM],
-        out_specs=IN_VMEM,
-        scratch_shapes=[pltpu.VMEM((blocks, rows, columns), mine.dtype)],
-        compiler_params=PARAMS,
         name="select",
-    )(core, block_of, mine, other)
+    )(core, chosen, mine, other)
 
 
 def bands_kernel(band_ref, in_ref, own_ref, next_ref):
@@ -192,7 +218,7 @@
     )(band, arrived)
 
 
-def precondition_kernel(band0_ref, band1_ref, band2_ref, band3_ref, kept_ref, sent_ref):
+def precondition_kernel(band2_ref, band3_ref, band1_ref, band0_ref, kept_ref, sent_ref):
     extent, columns = kept_ref.shape
     block = jnp.concatenate([band0_ref[...], band1_ref[...], band2_ref[...], band3_ref[...]], axis=1)
     row = lax.broadcasted_iota(jnp.int32, (extent, extent), 0)
@@ -200,14 +226,11 @@
     five = jnp.where(row == col, jnp.float32(5.0), jnp.float32(0.0))
     right = lax.dot_general(block, block, (((0,), (0,)), ((), ())), preferred_element_type=jnp.float32)
     left = lax.dot_general(block, block, (((1,), (1,)), ((), ())), preferred_element_type=jnp.float32)
-    moments, scales = [], []
-    for stat in (right, left):
-        total = jnp.sum(stat * stat, keepdims=True)
-        scaling = 2.5 / jnp.sqrt(total + 1e-06)
-        moments.append((scaling * stat).astype(jnp.bfloat16))
-        scales.append(jnp.sqrt(jnp.sqrt(scaling)).astype(jnp.bfloat16).astype(jnp.float32))
+    scaling = 2.5 / jnp.sqrt(jnp.sum(right * right, keepdims=True) + 1e-06)
+    scale = jnp.sqrt(jnp.sqrt(scaling)).astype(jnp.bfloat16).astype(jnp.float32)
+    moments = [(scaling * stat).astype(jnp.bfloat16) for stat in (right, left)]
     factors = [((five - m.astype(jnp.float32)) * 0.25).astype(jnp.bfloat16) for m in moments]
-    roots = [(s * f.astype(jnp.float32)).astype(jnp.bfloat16) for s, f in zip(scales, factors)]
+    roots = [(scale * f.astype(jnp.float32)).astype(jnp.bfloat16) for f in factors]
     for iteration in range(ITERS - 1):
         squares = [dot16(f, f) for f in factors]
         if iteration > 0:
@@ -233,12 +256,17 @@
 
 def place_kernel(band_ref, kept_ref, taken_ref, out_ref, sems):
     slot = band_ref[0] % MOST
-    one = pltpu.make_async_copy(kept_ref, out_ref.at[slot], sems.at[0])
-    two = pltpu.make_async_copy(taken_ref, out_ref.at[1 - slot], sems.at[1])
-    one.start()
-    two.start()
-    one.wait()
-    two.wait()
+    cuts = sems.shape[1]
+    rows = kept_ref.shape[0] // cuts
+    copies = []
+    for i, (source, to) in enumerate(((taken_ref, 1 - slot), (kept_ref, slot))):
+        for cut in range(cuts):
+            part = pl.ds(cut * rows, rows)
+            copies.append(pltpu.make_async_copy(source.at[part], out_ref.at[to, part], sems.at[i, cut]))
+    for copy in copies:
+        copy.start()
+    for copy in copies:
+        copy.wait()
 
 
 def place(band, kept, taken):
@@ -247,7 +275,7 @@
         out_shape=jax.ShapeDtypeStruct((MOST,) + kept.shape, kept.dtype),
         in_specs=[IN_SMEM, IN_VMEM, IN_VMEM],
         out_specs=IN_HBM,
-        scratch_shapes=[pltpu.SemaphoreType.DMA((2,))],
+        scratch_shapes=[pltpu.SemaphoreType.DMA((MOST, 4))],
         compiler_params=PARAMS,
         name="place",
     )(band, kept, taken)
@@ -259,8 +287,9 @@
     devices = Z * Y * CORE
     core = lax.axis_index("core").reshape(1).astype(jnp.int32)
     y = lax.axis_index("y").reshape(1).astype(jnp.int32)
+    z = lax.axis_index("z").reshape(1).astype(jnp.int32)
     band = lax.axis_index("mp").reshape(1).astype(jnp.int32)
-    block_of = block_of_slots(owner, core)
+    chosen = selection(owner, core, block_count, extent // devices)
 
     def swap(value):
         return lax.ppermute(value, "core", [(0, 1), (1, 0)])
@@ -290,6 +319,7 @@
     (w1a,) = add_parts(
         [[(0, 0, 0, n), (1, 0, 0, n), (2, 0, 0, n)]], (kept_near, near, from_down), jnp.bfloat16, "relay_up"
     )
+    w1a, kept_near = lax.optimization_barrier((w1a, kept_near))
     (w3b,) = add_parts(
         [[(0, 1, n, n), (1, 1, n, n), (2, 0, 0, n)]], (kept_near, near, from_up), jnp.bfloat16, "relay_down"
     )
@@ -300,14 +330,21 @@
         jnp.float32,
         "own_sum",
     )
-    own_a, own_b, block_of, band = lax.optimization_barrier((own_a, own_b, block_of, band))
-    plane = plane_sum(own_a, own_b, w_up, w_down)
-    mine = mean_rows(lax.all_to_all(plane, "z", split_axis=0, concat_axis=0, tiled=True), devices)
-
-    outgoing = select(core, block_of, mine, swap(mine), block_count)
+    own_a, own_b, chosen, band = lax.optimization_barrier((own_a, own_b, chosen, band))
+    sent_a, sent_b, kept = plane_sum(z, own_a, own_b, w_up, w_down)
+    got_a = lax.ppermute(sent_a, "z", [(i, i ^ 1) for i in range(Z)])
+    got_b = lax.ppermute(sent_b, "z", [(i, (i - 1 + 2 * (i % 2)) % Z) for i in range(Z)])
+    far, up_two, down_two, own = parity_sum(z, kept, got_a, got_b)
+    received = [
+        lax.ppermute(value, "z", [(i, (i + shift) % Z) for i in range(Z)])
+        for value, shift in ((far, 4), (up_two, 2), (down_two, 6))
+    ]
+    mine = mean_rows(own, received, devices)
+
+    outgoing = select(core, chosen, mine, swap(mine)).reshape(Z * Y, MOST, -1, columns)
     arrived = lax.all_to_all(outgoing, ("z", "y"), split_axis=0, concat_axis=0, tiled=True)
     own_band, next_band = bands_of(band, arrived)
-    bands = [own_band, along(next_band, 3), along(own_band, 2), along(next_band, 1)]
+    two, one, three = along(own_band, 2), along(next_band, 1), along(next_band, 3)
 
     result = pltpu.VMEM((extent, columns), jnp.bfloat16)
     kept, given = pl.pallas_call(
@@ -317,7 +354,7 @@
         out_specs=[IN_VMEM] * 2,
         compiler_params=LARGE,
         name="precondition",
-    )(*bands)
+    )(two, one, three, own_band)
     return place(band, kept, along(given, 1))
 
 

time: 93.3 us -> 92.3 us (0.989)
  blocking collectives: 37.3 us -> 18.6 us
  starting transfers between devices: 20.8 us -> 32 us
  waiting for transfers between devices: 20.6 us -> 27 us
    all_to_all x1 -> x0, blocking collectives: 21.7 us -> none  [on_device(): lax.all_to_all(plane, 'z', split_axis=0, concat_axis=0, tiled=True)]
    ppermute x0 -> x5, starting transfers between devices: none -> 10.7 us  [the longest x3 5.92 us: on_device(): lax.ppermute(value, 'z', [(i, (i + shift) % Z) for i in range(Z)])]
    ppermute x0 -> x5, waiting for transfers between devices: none -> 7.43 us  [the longest x3 3.32 us: on_device(): lax.ppermute(value, 'z', [(i, (i + shift) % Z) for i in range(Z)])]
    ppermute x3, waiting for transfers between devices: 10.4 us -> 4.94 us  [up(): return lax.ppermute(value, 'y', [(i, (i + 1) % Y) for i in range(Y)])]
    ppermute x3, waiting for transfers between devices: 0.01 us -> 4.35 us  [down(): return lax.ppermute(value, 'y', [(i, (i - 1) % Y) for i in range(Y)])]
    all_to_all x1, blocking collectives: 15.6 us -> 18.6 us  [on_device(): lax.all_to_all(outgoing, ('z', 'y'), split_axis=0, concat_axis=0, tiled=T...]
  transfers between devices with their start and end apart: 14 -> 19, of which waited for: 7 -> 11; matrix products, arithmetic and copies ran while one was open for 0% -> 1% of each run, Pallas kernels for 3% -> 3%
where the time goes in v4:
time: 92.3 us; the launch traced here: 90.9 us
  starting transfers between devices  32 us (35%)
  waiting for transfers between devices  27 us (29%)
  blocking collectives  18.6 us (20%)
  Pallas kernels  12.2 us (13%)
    all_to_all x1, blocking collectives, on_device(): lax.all_to_all(outgoing, ('z', 'y'), split_axis=0, concat_axis=0, tiled=T...  18.6 us
    ppermute x4, waiting for transfers between devices, along(): return lax.ppermute(value, 'mp', [(i, (i + shift) % MP) for i in range(MP)])  8.77 us
    ppermute x4, starting transfers between devices, swap(): return lax.ppermute(value, 'core', [(0, 1), (1, 0)])  7.83 us
    ppermute x3, starting transfers between devices, down(): return lax.ppermute(value, 'y', [(i, (i - 1) % Y) for i in range(Y)])  7.63 us
    ppermute x3, starting transfers between devices, on_device(): lax.ppermute(value, 'z', [(i, (i + shift) % Z) for i in range(Z)])  5.92 us
    pallas_call x1, Pallas kernels, on_device(): pl.pallas_call(precondition_kernel, out_shape=(result, result), in_specs=...  5.87 us
    ppermute x4, starting transfers between devices, along(): return lax.ppermute(value, 'mp', [(i, (i + shift) % MP) for i in range(MP)])  5.78 us
    ppermute x3, waiting for transfers between devices, up(): return lax.ppermute(value, 'y', [(i, (i + 1) % Y) for i in range(Y)])  4.94 us
  transfers between devices with their start and end apart: 19, of which 11 were waited for; matrix products, arithmetic and copies ran while one was open for 1% of the time, Pallas kernels for 3%

profile of v4, /device:TPU:1, one launch (start us, length us, event | category | flops | bytes accessed | tf_op | source)
XLA Modules:
  0.0 90.9 jit_solution(13176800956985670880)
XLA Ops:
  0.0 1.7 %sent.1 = (bf16[1,32,64,128]{3,2,1,0:T(8,128)(2,1)S(1)}, bf16[2,32,64,128]{3,2,1,0:T(8,128)(2,1)S(1)}, bf16[1,32,64,128]{3,2,1,0:T(8,128)(2,1)S(1)}) custom-call(s32[1]{0:T(128)S(6)} %sub.13.core_ref, s32[1]{0:T(128)} %bitcast.1.y_ref, bf16[32,512,128]{2,1,0:T(8,128)(2,1)} %bitcast.7), custom_call_target="tpu_custom_call" | custom-call | tf_op jit(solution)/shard_map/sent/pallas_call | solution.py:66
  1.7 3.3 %collective-permute-start.1 = (bf16[2,32,64,128]{3,2,1,0:T(8,128)(2,1)S(1)}, bf16[2,32,64,128]{3,2,1,0:T(8,128)(2,1)S(1)}, u32[]{:S(2)}, u32[]{:S(2)}) collective-permute-start(bf16[2,32,64,128]{3,2,1,0:T(8,128)(2,1)S(1)} %get-tuple-element.39), channel_id=1, source_target_pairs={{0,4},{4,0},{1,5},{5,1},{2,6},{6,2},{3,7},{7,3},{8,12},{12,8},{9,1... | collective-permute-start | bytes 3145736 | tf_op jit(solution)/shard_map/ppermute | solution.py:295
  5.6 1.7 %kept.1 = (bf16[1,32,64,128]{3,2,1,0:T(8,128)(2,1)S(1)}, bf16[2,32,64,128]{3,2,1,0:T(8,128)(2,1)S(1)}, bf16[1,32,64,128]{3,2,1,0:T(8,128)(2,1)S(1)}) custom-call(s32[1]{0:T(128)} %bitcast.core_ref, s32[1]{0:T(128)} %bitcast.1.y_ref, bf16[32,512,128]{2,1,0:T(8,128)(2,1)} %bitcast.8), custom_call_target="tpu_custom_call" | custom-call | tf_op jit(solution)/shard_map/kept/pallas_call | solution.py:66
  8.4 2.7 %collective-permute-start.7 = (bf16[1,16,64,128]{3,2,1,0:T(8,128)(2,1)S(1)}, bf16[1,16,64,128]{3,2,1,0:T(8,128)(2,1)S(1)}, u32[]{:S(2)}, u32[]{:S(2)}) collective-permute-start(bf16[1,16,64,128]{3,2,1,0:T(8,128)(2,1)S(1)} %get-tuple-element.55), channel_id=1, source_target_pairs={{0,24},{8,0},{16,8},{24,16},{1,25},{9,1},{17,9},{25,17},{2,26},{10... | collective-permute-start | bytes 786440 | tf_op jit(solution)/shard_map/ppermute | solution.py:301
  11.9 2.7 %collective-permute-start.3 = (bf16[1,16,64,128]{3,2,1,0:T(8,128)(2,1)S(1)}, bf16[1,16,64,128]{3,2,1,0:T(8,128)(2,1)S(1)}, u32[]{:S(2)}, u32[]{:S(2)}) collective-permute-start(bf16[1,16,64,128]{3,2,1,0:T(8,128)(2,1)S(1)} %get-tuple-element.41), channel_id=1, source_target_pairs={{0,24},{8,0},{16,8},{24,16},{1,25},{9,1},{17,9},{25,17},{2,26},{10... | collective-permute-start | bytes 786440 | tf_op jit(solution)/shard_map/ppermute | solution.py:301
  14.6 2.5 %collective-permute-done.5.refs_2_ = bf16[1,16,64,128]{3,2,1,0:T(8,128)(2,1)S(1)} collective-permute-done((bf16[1,16,64,128]{3,2,1,0:T(8,128)(2,1)S(1)}, bf16[1,16,64,128]{3,2,1,0:T(8,128)(2,1)S(1)}, u32[]{:S(2)}, u32[]{:S(2)}) %collective-permute-start.5) | collective-permute-done | bytes 262176 | tf_op jit(solution)/shard_map/ppermute | solution.py:298
  17.3 2.3 %collective-permute-start.8 = (bf16[1,16,64,128]{3,2,1,0:T(8,128)(2,1)S(1)}, bf16[1,16,64,128]{3,2,1,0:T(8,128)(2,1)S(1)}, u32[]{:S(2)}, u32[]{:S(2)}) collective-permute-start(bf16[1,16,64,128]{3,2,1,0:T(8,128)(2,1)S(1)} %relay_down.1), channel_id=1, source_target_pairs={{0,24},{8,0},{16,8},{24,16},{1,25},{9,1},{17,9},{25,17},{2,26},{10... | collective-permute-start | bytes 786440 | tf_op jit(solution)/shard_map/ppermute | solution.py:301
  20.2 2.5 %collective-permute-done.2.refs_2_ = bf16[1,16,64,128]{3,2,1,0:T(8,128)(2,1)S(1)} collective-permute-done((bf16[1,16,64,128]{3,2,1,0:T(8,128)(2,1)}, bf16[1,16,64,128]{3,2,1,0:T(8,128)(2,1)S(1)}, u32[]{:S(2)}, u32[]{:S(2)}) %collective-permute-start.2) | collective-permute-done | bytes 262176 | tf_op jit(solution)/shard_map/ppermute | solution.py:298
  22.9 4.3 %collective-permute-done.8.w_down_ref = bf16[1,16,64,128]{3,2,1,0:T(8,128)(2,1)S(1)} collective-permute-done((bf16[1,16,64,128]{3,2,1,0:T(8,128)(2,1)S(1)}, bf16[1,16,64,128]{3,2,1,0:T(8,128)(2,1)S(1)}, u32[]{:S(2)}, u32[]{:S(2)}) %collective-permute-start.8) | collective-permute-done | bytes 262176 | tf_op jit(solution)/shard_map/ppermute | solution.py:301
  27.4 4.7 %collective-permute-start.10 = (bf16[4,128,128]{2,1,0:T(8,128)(2,1)S(1)}, bf16[4,128,128]{2,1,0:T(8,128)(2,1)S(1)}, u32[]{:S(2)}, u32[]{:S(2)}) collective-permute-start(bf16[4,128,128]{2,1,0:T(8,128)(2,1)S(1)} %get-tuple-element.58), channel_id=1, source_target_pairs={{0,224},{32,64},{64,32},{96,128},{128,96},{160,192},{192,160},{224... | collective-permute-start | bytes 393224 | tf_op jit(solution)/shard_map/ppermute | solution.py:336
  32.2 2.4 %collective-permute-done.10.b_ref = bf16[4,128,128]{2,1,0:T(8,128)(2,1)S(1)} collective-permute-done((bf16[4,128,128]{2,1,0:T(8,128)(2,1)S(1)}, bf16[4,128,128]{2,1,0:T(8,128)(2,1)S(1)}, u32[]{:S(2)}, u32[]{:S(2)}) %collective-permute-start.10) | collective-permute-done | bytes 131104 | tf_op jit(solution)/shard_map/ppermute | solution.py:336
  34.5 1.8 %collective-permute-done.9.a_ref = bf16[4,128,128]{2,1,0:T(8,128)(2,1)S(1)} collective-permute-done((bf16[4,128,128]{2,1,0:T(8,128)(2,1)S(1)}, bf16[4,128,128]{2,1,0:T(8,128)(2,1)S(1)}, u32[]{:S(2)}, u32[]{:S(2)}) %collective-permute-start.9) | collective-permute-done | bytes 131104 | tf_op jit(solution)/shard_map/ppermute | solution.py:335
  36.3 2.3 %collective-permute-start.11 = (bf16[256,128]{1,0:T(8,128)(2,1)S(1)}, bf16[256,128]{1,0:T(8,128)(2,1)S(1)}, u32[]{:S(2)}, u32[]{:S(2)}) collective-permute-start(bf16[256,128]{1,0:T(8,128)(2,1)S(1)} %get-tuple-element.60), channel_id=1, source_target_pairs={{0,128},{32,160},{64,192},{96,224},{128,0},{160,32},{192,64},{224,... | collective-permute-start | bytes 196616 | tf_op jit(solution)/shard_map/ppermute | solution.py:339
  39.4 2.9 %collective-permute-start.13 = (bf16[256,128]{1,0:T(8,128)(2,1)S(1)}, bf16[256,128]{1,0:T(8,128)(2,1)S(1)}, u32[]{:S(2)}, u32[]{:S(2)}) collective-permute-start(bf16[256,128]{1,0:T(8,128)(2,1)S(1)} %get-tuple-element.62), channel_id=1, source_target_pairs={{0,192},{32,224},{64,0},{96,32},{128,64},{160,96},{192,128},{224,1... | collective-permute-start | bytes 196616 | tf_op jit(solution)/shard_map/ppermute | solution.py:339
  42.2 2.0 %collective-permute-done.11.refs_0_ = bf16[256,128]{1,0:T(8,128)(2,1)S(1)} collective-permute-done((bf16[256,128]{1,0:T(8,128)(2,1)S(1)}, bf16[256,128]{1,0:T(8,128)(2,1)S(1)}, u32[]{:S(2)}, u32[]{:S(2)}) %collective-permute-start.11) | collective-permute-done | bytes 65568 | tf_op jit(solution)/shard_map/ppermute | solution.py:339
  44.2 1.3 %collective-permute-done.13.refs_2_ = bf16[256,128]{1,0:T(8,128)(2,1)S(1)} collective-permute-done((bf16[256,128]{1,0:T(8,128)(2,1)S(1)}, bf16[256,128]{1,0:T(8,128)(2,1)S(1)}, u32[]{:S(2)}, u32[]{:S(2)}) %collective-permute-start.13) | collective-permute-done | bytes 65568 | tf_op jit(solution)/shard_map/ppermute | solution.py:339
  45.6 4.0 %collective-permute-start.14 = (bf16[256,128]{1,0:T(8,128)(2,1)S(1)}, bf16[256,128]{1,0:T(8,128)(2,1)S(1)}, u32[]{:S(2)}, u32[]{:S(2)}) collective-permute-start(bf16[256,128]{1,0:T(8,128)(2,1)S(1)} %mean_rows.1.mine_ref), channel_id=1, source_target_pairs={{0,4},{4,0},{1,5},{5,1},{2,6},{6,2},{3,7},{7,3},{8,12},{12,8},{9,1... | collective-permute-start | bytes 196616 | tf_op jit(solution)/shard_map/ppermute | solution.py:295
  49.6 0.9 collective-permute-done.14.other_ref
  50.9 18.6 %all_to_all.5.in_ref = bf16[32,2,16,128]{3,2,1,0:T(8,128)(2,1)S(1)} all-to-all(bf16[32,2,16,128]{3,2,1,0:T(8,128)(2,1)S(1)} %bitcast.6), channel_id=1, replica_groups=mesh['z'=8,'y'=4,'core'=2,'mp'=4] {'z','y'}, dimensions={0} | all-to-all | bytes 524288 | tf_op jit(solution)/shard_map/all_to_all | solution.py:345
  69.6 3.0 %collective-permute-start.15 = (bf16[512,128]{1,0:T(8,128)(2,1)S(1)}, bf16[512,128]{1,0:T(8,128)(2,1)S(1)}, u32[]{:S(2)}, u32[]{:S(2)}) collective-permute-start(bf16[512,128]{1,0:T(8,128)(2,1)S(1)} %get-tuple-element.63.band0_ref), channel_id=1, source_target_pairs={{0,2},{1,3},{2,0},{3,1},{4,6},{5,7},{6,4},{7,5},{8,10},{9,11},{10,... | collective-permute-start | bytes 393224 | tf_op jit(solution)/shard_map/ppermute | solution.py:304
  72.9 2.4 %collective-permute-start.17 = (bf16[512,128]{1,0:T(8,128)(2,1)S(1)}, bf16[512,128]{1,0:T(8,128)(2,1)S(1)}, u32[]{:S(2)}, u32[]{:S(2)}) collective-permute-start(bf16[512,128]{1,0:T(8,128)(2,1)S(1)} %get-tuple-element.64), channel_id=1, source_target_pairs={{0,3},{1,0},{2,1},{3,2},{4,7},{5,4},{6,5},{7,6},{8,11},{9,8},{10,9... | collective-permute-start | bytes 393224 | tf_op jit(solution)/shard_map/ppermute | solution.py:304
  75.3 3.8 %collective-permute-done.16.band3_ref = bf16[512,128]{1,0:T(8,128)(2,1)S(1)} collective-permute-done((bf16[512,128]{1,0:T(8,128)(2,1)S(1)}, bf16[512,128]{1,0:T(8,128)(2,1)S(1)}, u32[]{:S(2)}, u32[]{:S(2)}) %collective-permute-start.16) | collective-permute-done | bytes 131104 | tf_op jit(solution)/shard_map/ppermute | solution.py:304
  79.0 5.9 %precondition.1 = (bf16[512,128]{1,0:T(8,128)(2,1)S(1)}, bf16[512,128]{1,0:T(8,128)(2,1)S(1)}) custom-call(bf16[512,128]{1,0:T(8,128)(2,1)S(1)} %collective-permute-done.15.band2_ref, bf16[512,128]{1,0:T(8,128)(2,1)S(1)} %collective-permute-done.16.band3_ref, bf16[512,128]{1,0:T(8,128)(2,1)S(1)} %collective-permute-done.17.band1_ref, ...), custom_call_target="tpu_custom_call" | custom-call | tf_op jit(solution)/shard_map/precondition/pallas_call | solution.py:350
  85.0 5.0 %collective-permute-done.18.taken_ref = bf16[512,128]{1,0:T(8,128)(2,1)S(1)} collective-permute-done((bf16[512,128]{1,0:T(8,128)(2,1)S(1)}, bf16[512,128]{1,0:T(8,128)(2,1)S(1)}, u32[]{:S(2)}, u32[]{:S(2)}) %collective-permute-start.18) | collective-permute-done | bytes 131104 | tf_op jit(solution)/shard_map/ppermute | solution.py:304
  (37 shorter events, 6.0 us)
Async XLA Ops:
  1.7 9.3 %collective-permute-start.1 = (bf16[2,32,64,128]{3,2,1,0:T(8,128)(2,1)S(1)}, bf16[2,32,64,128]{3,2,1,0:T(8,128)(2,1)S(1)}, u32[]{:S(2)}, u32[]{:S(2)}) collective-permute-start(bf16[2,32,64,128]{3,2,1,0:T(8,128)(2,1)S(1)} %get-tuple-element.39), channel_id=1, source_target_pairs={{0,4},{4,0},{1,5},{5,1},{2,6},{6,2},{3,7},{7,3},{8,12},{12,8},{9,1... | collective-permute-start | bytes 3145736 | tf_op jit(solution)/shard_map/ppermute | solution.py:295
  5.1 3.0 %collective-permute-start.4 = (bf16[1,32,64,128]{3,2,1,0:T(8,128)(2,1)S(1)}, bf16[1,32,64,128]{3,2,1,0:T(8,128)(2,1)S(1)}, u32[]{:S(2)}, u32[]{:S(2)}) collective-permute-start(bf16[1,32,64,128]{3,2,1,0:T(8,128)(2,1)S(1)} %get-tuple-element.51), channel_id=1, source_target_pairs={{0,4},{4,0},{1,5},{5,1},{2,6},{6,2},{3,7},{7,3},{8,12},{12,8},{9,1... | collective-permute-start | bytes 1572872 | tf_op jit(solution)/shard_map/ppermute | solution.py:295
  5.2 2.2 %copy-start = (s32[32]{0:T(128)S(1)}, s32[32]{0:T(128)}, u32[]{:S(2)}) copy-start(s32[32]{0:T(128)} %param.3) | copy-start | bytes 388
  5.2 15.1 %collective-permute-start = (bf16[1,32,64,128]{3,2,1,0:T(8,128)(2,1)S(1)}, bf16[1,32,64,128]{3,2,1,0:T(8,128)(2,1)S(1)}, u32[]{:S(2)}, u32[]{:S(2)}) collective-permute-start(bf16[1,32,64,128]{3,2,1,0:T(8,128)(2,1)S(1)} %get-tuple-element.37), channel_id=1, source_target_pairs={{0,4},{4,0},{1,5},{5,1},{2,6},{6,2},{3,7},{7,3},{8,12},{12,8},{9,1... | collective-permute-start | bytes 1572872 | tf_op jit(solution)/shard_map/ppermute | solution.py:295
  8.3 8.8 %collective-permute-start.5 = (bf16[1,16,64,128]{3,2,1,0:T(8,128)(2,1)S(1)}, bf16[1,16,64,128]{3,2,1,0:T(8,128)(2,1)S(1)}, u32[]{:S(2)}, u32[]{:S(2)}) collective-permute-start(bf16[1,16,64,128]{3,2,1,0:T(8,128)(2,1)S(1)} %get-tuple-element.52), channel_id=1, source_target_pairs={{0,8},{8,16},{16,24},{24,0},{1,9},{9,17},{17,25},{25,1},{2,10},{10... | collective-permute-start | bytes 786440 | tf_op jit(solution)/shard_map/ppermute | solution.py:298
  8.4 8.8 %collective-permute-start.7 = (bf16[1,16,64,128]{3,2,1,0:T(8,128)(2,1)S(1)}, bf16[1,16,64,128]{3,2,1,0:T(8,128)(2,1)S(1)}, u32[]{:S(2)}, u32[]{:S(2)}) collective-permute-start(bf16[1,16,64,128]{3,2,1,0:T(8,128)(2,1)S(1)} %get-tuple-element.55), channel_id=1, source_target_pairs={{0,24},{8,0},{16,8},{24,16},{1,25},{9,1},{17,9},{25,17},{2,26},{10... | collective-permute-start | bytes 786440 | tf_op jit(solution)/shard_map/ppermute | solution.py:301
  11.9 10.8 %collective-permute-start.2 = (bf16[1,16,64,128]{3,2,1,0:T(8,128)(2,1)}, bf16[1,16,64,128]{3,2,1,0:T(8,128)(2,1)S(1)}, u32[]{:S(2)}, u32[]{:S(2)}) collective-permute-start(bf16[1,16,64,128]{3,2,1,0:T(8,128)(2,1)} %get-tuple-element.40), channel_id=1, source_target_pairs={{0,8},{8,16},{16,24},{24,0},{1,9},{9,17},{17,25},{25,1},{2,10},{10... | collective-permute-start | bytes 786440 | tf_op jit(solution)/shard_map/ppermute | solution.py:298
  11.9 10.8 %collective-permute-start.3 = (bf16[1,16,64,128]{3,2,1,0:T(8,128)(2,1)S(1)}, bf16[1,16,64,128]{3,2,1,0:T(8,128)(2,1)S(1)}, u32[]{:S(2)}, u32[]{:S(2)}) collective-permute-start(bf16[1,16,64,128]{3,2,1,0:T(8,128)(2,1)S(1)} %get-tuple-element.41), channel_id=1, source_target_pairs={{0,24},{8,0},{16,8},{24,16},{1,25},{9,1},{17,9},{25,17},{2,26},{10... | collective-permute-start | bytes 786440 | tf_op jit(solution)/shard_map/ppermute | solution.py:301
  17.3 9.9 %collective-permute-start.8 = (bf16[1,16,64,128]{3,2,1,0:T(8,128)(2,1)S(1)}, bf16[1,16,64,128]{3,2,1,0:T(8,128)(2,1)S(1)}, u32[]{:S(2)}, u32[]{:S(2)}) collective-permute-start(bf16[1,16,64,128]{3,2,1,0:T(8,128)(2,1)S(1)} %relay_down.1), channel_id=1, source_target_pairs={{0,24},{8,0},{16,8},{24,16},{1,25},{9,1},{17,9},{25,17},{2,26},{10... | collective-permute-start | bytes 786440 | tf_op jit(solution)/shard_map/ppermute | solution.py:301
  19.6 7.6 %collective-permute-start.6 = (bf16[1,16,64,128]{3,2,1,0:T(8,128)(2,1)S(1)}, bf16[1,16,64,128]{3,2,1,0:T(8,128)(2,1)S(1)}, u32[]{:S(2)}, u32[]{:S(2)}) collective-permute-start(bf16[1,16,64,128]{3,2,1,0:T(8,128)(2,1)S(1)} %relay_up.1), channel_id=1, source_target_pairs={{0,8},{8,16},{16,24},{24,0},{1,9},{9,17},{17,25},{25,1},{2,10},{10... | collective-permute-start | bytes 786440 | tf_op jit(solution)/shard_map/ppermute | solution.py:298
  27.4 7.1 %collective-permute-start.10 = (bf16[4,128,128]{2,1,0:T(8,128)(2,1)S(1)}, bf16[4,128,128]{2,1,0:T(8,128)(2,1)S(1)}, u32[]{:S(2)}, u32[]{:S(2)}) collective-permute-start(bf16[4,128,128]{2,1,0:T(8,128)(2,1)S(1)} %get-tuple-element.58), channel_id=1, source_target_pairs={{0,224},{32,64},{64,32},{96,128},{128,96},{160,192},{192,160},{224... | collective-permute-start | bytes 393224 | tf_op jit(solution)/shard_map/ppermute | solution.py:336
  32.2 4.1 %collective-permute-start.9 = (bf16[4,128,128]{2,1,0:T(8,128)(2,1)S(1)}, bf16[4,128,128]{2,1,0:T(8,128)(2,1)S(1)}, u32[]{:S(2)}, u32[]{:S(2)}) collective-permute-start(bf16[4,128,128]{2,1,0:T(8,128)(2,1)S(1)} %get-tuple-element.57), channel_id=1, source_target_pairs={{0,32},{32,0},{64,96},{96,64},{128,160},{160,128},{192,224},{224,1... | collective-permute-start | bytes 393224 | tf_op jit(solution)/shard_map/ppermute | solution.py:335
  36.3 7.9 %collective-permute-start.11 = (bf16[256,128]{1,0:T(8,128)(2,1)S(1)}, bf16[256,128]{1,0:T(8,128)(2,1)S(1)}, u32[]{:S(2)}, u32[]{:S(2)}) collective-permute-start(bf16[256,128]{1,0:T(8,128)(2,1)S(1)} %get-tuple-element.60), channel_id=1, source_target_pairs={{0,128},{32,160},{64,192},{96,224},{128,0},{160,32},{192,64},{224,... | collective-permute-start | bytes 196616 | tf_op jit(solution)/shard_map/ppermute | solution.py:339
  38.7 5.6 %collective-permute-start.12 = (bf16[256,128]{1,0:T(8,128)(2,1)S(1)}, bf16[256,128]{1,0:T(8,128)(2,1)S(1)}, u32[]{:S(2)}, u32[]{:S(2)}) collective-permute-start(bf16[256,128]{1,0:T(8,128)(2,1)S(1)} %get-tuple-element.61), channel_id=1, source_target_pairs={{0,64},{32,96},{64,128},{96,160},{128,192},{160,224},{192,0},{224,... | collective-permute-start | bytes 196616 | tf_op jit(solution)/shard_map/ppermute | solution.py:339
  39.4 6.2 %collective-permute-start.13 = (bf16[256,128]{1,0:T(8,128)(2,1)S(1)}, bf16[256,128]{1,0:T(8,128)(2,1)S(1)}, u32[]{:S(2)}, u32[]{:S(2)}) collective-permute-start(bf16[256,128]{1,0:T(8,128)(2,1)S(1)} %get-tuple-element.62), channel_id=1, source_target_pairs={{0,192},{32,224},{64,0},{96,32},{128,64},{160,96},{192,128},{224,1... | collective-permute-start | bytes 196616 | tf_op jit(solution)/shard_map/ppermute | solution.py:339
  45.6 4.9 %collective-permute-start.14 = (bf16[256,128]{1,0:T(8,128)(2,1)S(1)}, bf16[256,128]{1,0:T(8,128)(2,1)S(1)}, u32[]{:S(2)}, u32[]{:S(2)}) collective-permute-start(bf16[256,128]{1,0:T(8,128)(2,1)S(1)} %mean_rows.1.mine_ref), channel_id=1, source_target_pairs={{0,4},{4,0},{1,5},{5,1},{2,6},{6,2},{3,7},{7,3},{8,12},{12,8},{9,1... | collective-permute-start | bytes 196616 | tf_op jit(solution)/shard_map/ppermute | solution.py:295
  69.6 5.7 %collective-permute-start.15 = (bf16[512,128]{1,0:T(8,128)(2,1)S(1)}, bf16[512,128]{1,0:T(8,128)(2,1)S(1)}, u32[]{:S(2)}, u32[]{:S(2)}) collective-permute-start(bf16[512,128]{1,0:T(8,128)(2,1)S(1)} %get-tuple-element.63.band0_ref), channel_id=1, source_target_pairs={{0,2},{1,3},{2,0},{3,1},{4,6},{5,7},{6,4},{7,5},{8,10},{9,11},{10,... | collective-permute-start | bytes 393224 | tf_op jit(solution)/shard_map/ppermute | solution.py:304
  72.6 6.4 %collective-permute-start.16 = (bf16[512,128]{1,0:T(8,128)(2,1)S(1)}, bf16[512,128]{1,0:T(8,128)(2,1)S(1)}, u32[]{:S(2)}, u32[]{:S(2)}) collective-permute-start(bf16[512,128]{1,0:T(8,128)(2,1)S(1)} %get-tuple-element.64), channel_id=1, source_target_pairs={{0,1},{1,2},{2,3},{3,0},{4,5},{5,6},{6,7},{7,4},{8,9},{9,10},{10,1... | collective-permute-start | bytes 393224 | tf_op jit(solution)/shard_map/ppermute | solution.py:304
  72.9 6.1 %collective-permute-start.17 = (bf16[512,128]{1,0:T(8,128)(2,1)S(1)}, bf16[512,128]{1,0:T(8,128)(2,1)S(1)}, u32[]{:S(2)}, u32[]{:S(2)}) collective-permute-start(bf16[512,128]{1,0:T(8,128)(2,1)S(1)} %get-tuple-element.64), channel_id=1, source_target_pairs={{0,3},{1,0},{2,1},{3,2},{4,7},{5,4},{6,5},{7,6},{8,11},{9,8},{10,9... | collective-permute-start | bytes 393224 | tf_op jit(solution)/shard_map/ppermute | solution.py:304
  84.9 5.1 %collective-permute-start.18 = (bf16[512,128]{1,0:T(8,128)(2,1)S(1)}, bf16[512,128]{1,0:T(8,128)(2,1)S(1)}, u32[]{:S(2)}, u32[]{:S(2)}) collective-permute-start(bf16[512,128]{1,0:T(8,128)(2,1)S(1)} %get-tuple-element.66), channel_id=1, source_target_pairs={{0,1},{1,2},{2,3},{3,0},{4,5},{5,6},{6,7},{7,4},{8,9},{9,10},{10,1... | collective-permute-start | bytes 393224 | tf_op jit(solution)/shard_map/ppermute | solution.py:304

commit v5 on v4

--- a/solution.py
+++ b/solution.py
@@ -39,25 +39,30 @@
     return dot(a, b).astype(jnp.bfloat16)
 
 
-def pieces_of(grads, which_core, y, shifts, name):
+def piece_copies(core, y, in_ref, out_ref, sems, other, shift):
+    blocks, rows = out_ref.shape[1:3]
+    half = rows * Y
+    which = 1 - core if other else core
+    first = pl.multiple_of(which * half + (y + shift) % Y * rows, rows)
+    cuts = sems.shape[0]
+    group = blocks // cuts
+    copies = []
+    for cut in range(cuts):
+        some = pl.ds(cut * group, group)
+        source = in_ref.at[some, pl.ds(first, rows)]
+        copies.append(pltpu.make_async_copy(source, out_ref.at[0, some], sems.at[cut]))
+    return copies
+
+
+def pieces_of(grads, core, y, entries, name):
     blocks, extent, columns = grads.shape
-    half = extent // CORE
-    rows = half // Y
-    cuts = 4
-    group = blocks // cuts
+    rows = extent // CORE // Y
 
     def kernel(core_ref, y_ref, in_ref, *refs):
         outs, sems = refs[:-1], refs[-1]
         copies = []
-        for out_ref, entry in zip(outs, shifts):
-            for i, shift in enumerate(entry):
-                first = pl.multiple_of(core_ref[0] * half + (y_ref[0] + shift) % Y * rows, rows)
-                for cut in range(cuts):
-                    some = pl.ds(cut * group, group)
-                    source = in_ref.at[some, pl.ds(first, rows)]
-                    copies.append(
-                        pltpu.make_async_copy(source, out_ref.at[i, some], sems.at[len(copies)])
-                    )
+        for i, (out_ref, (other, shift)) in enumerate(zip(outs, entries)):
+            copies += piece_copies(core_ref[0], y_ref[0], in_ref, out_ref, sems.at[i], other, shift)
         for copy in copies:
             copy.start()
         for copy in copies:
@@ -65,13 +70,45 @@
 
     return pl.pallas_call(
         kernel,
-        out_shape=[pltpu.VMEM((len(entry), blocks, rows, columns), grads.dtype) for entry in shifts],
+        out_shape=[pltpu.VMEM((1, blocks, rows, columns), grads.dtype)] * len(entries),
         in_specs=[IN_SMEM, IN_SMEM, IN_HBM],
-        out_specs=[IN_VMEM] * len(shifts),
-        scratch_shapes=[pltpu.SemaphoreType.DMA((cuts * sum(len(entry) for entry in shifts),))],
+        out_specs=[IN_VMEM] * len(entries),
+        scratch_shapes=[pltpu.SemaphoreType.DMA((len(entries), 4))],
         compiler_params=PARAMS,
         name=name,
-    )(which_core, y, pltpu.with_memory_space_constraint(grads, pltpu.HBM))
+    )(core, y, pltpu.with_memory_space_constraint(grads, pltpu.HBM))
+
+
+def own_sum_kernel(core_ref, y_ref, grads_ref, got_ref, v_up_ref, v_down_ref, a_ref, b_ref, kept_ref, sems):
+    copies = piece_copies(core_ref[0], y_ref[0], grads_ref, kept_ref, sems, False, 0)
+    for copy in copies:
+        copy.start()
+    for copy in copies:
+        copy.wait()
+    half = a_ref.shape[1]
+    for first, received, out in ((0, v_down_ref, a_ref), (half, v_up_ref, b_ref)):
+
+        def add(b, carry):
+            total = kept_ref[0, first + b].astype(jnp.float32) + got_ref[0, first + b].astype(jnp.float32)
+            out[0, b] = total + received[0, b].astype(jnp.float32)
+            return carry
+
+        lax.fori_loop(0, half, add, 0, unroll=4)
+
+
+def own_sum(grads, core, y, own, v_up, v_down):
+    half, rows, columns = v_up.shape[1:]
+    shape = pltpu.VMEM((1, half, rows, columns), jnp.float32)
+    whole = pltpu.VMEM((1, 2 * half, rows, columns), grads.dtype)
+    return pl.pallas_call(
+        own_sum_kernel,
+        out_shape=(shape, shape),
+        in_specs=[IN_SMEM, IN_SMEM, IN_HBM, IN_VMEM, IN_VMEM, IN_VMEM],
+        out_specs=[IN_VMEM] * 2,
+        scratch_shapes=[whole, pltpu.SemaphoreType.DMA((4,))],
+        compiler_params=PARAMS,
+        name="own_sum",
+    )(core, y, pltpu.with_memory_space_constraint(grads, pltpu.HBM), own, v_up, v_down)
 
 
 def add_parts(parts, arrays, dtype, name):
@@ -139,10 +176,10 @@
     )(z, own_a, own_b, w_up, w_down)
 
 
-def parity_kernel(z_ref, kept_ref, a_ref, b_ref, far_ref, up_ref, down_ref, own_ref):
+def parity_kernel(z_ref, kept_ref, a_ref, b_ref, far_ref, outer_ref, inner_ref, own_ref):
     count = a_ref.shape[1]
-    for step, out_ref in ((2, far_ref), (1, up_ref), (3, down_ref), (0, own_ref)):
-        q = (z_ref[0] // 2 + step) % (Z // 2)
+    for change, out_ref in ((2, far_ref), (3, outer_ref), (1, inner_ref), (0, own_ref)):
+        q = (z_ref[0] // 2) ^ change
         for first, ref in ((0, a_ref), (count, b_ref)):
             part = pl.ds(first, count)
             out_ref[part] = (kept_ref[q, part] + ref[q].astype(jnp.float32)).astype(out_ref.dtype)
@@ -218,9 +255,9 @@
     )(band, arrived)
 
 
-def precondition_kernel(band2_ref, band3_ref, band1_ref, band0_ref, kept_ref, sent_ref):
+def precondition_kernel(same_ref, outer_ref, partner_ref, own_ref, kept_ref, sent_ref):
     extent, columns = kept_ref.shape
-    block = jnp.concatenate([band0_ref[...], band1_ref[...], band2_ref[...], band3_ref[...]], axis=1)
+    block = jnp.concatenate([own_ref[...], partner_ref[...], same_ref[...], outer_ref[...]], axis=1)
     row = lax.broadcasted_iota(jnp.int32, (extent, extent), 0)
     col = lax.broadcasted_iota(jnp.int32, (extent, extent), 1)
     five = jnp.where(row == col, jnp.float32(5.0), jnp.float32(0.0))
@@ -300,51 +337,50 @@
     def down(value):
         return lax.ppermute(value, "y", [(i, (i - 1) % Y) for i in range(Y)])
 
-    def along(value, shift):
-        return lax.ppermute(value, "mp", [(i, (i + shift) % MP) for i in range(MP)])
+    def along(value, to):
+        return lax.ppermute(value, "mp", list(enumerate(to)))
 
     n = block_count // 2
-    shifts = ((2,), (1, 3), (0,))
-    far, near, own = (swap(sent) for sent in pieces_of(local_grads, 1 - core, y, shifts, "sent"))
-    kept_far, kept_near, kept_own = pieces_of(local_grads, core, y, shifts, "kept")
+    sent = pieces_of(local_grads, core, y, [(True, shift) for shift in (2, 1, 3)], "sent")
+    far, near_up, near_down = (swap(piece) for piece in sent)
+    kept_far, kept_up, kept_down = pieces_of(local_grads, core, y, [(False, shift) for shift in (2, 1, 3)], "kept")
     v2a, v2b = add_parts(
         [[(0, 0, 0, n), (1, 0, 0, n)], [(0, 0, n, n), (1, 0, n, n)]], (kept_far, far), jnp.bfloat16, "far_sum"
     )
     from_down, from_up = up(v2a), down(v2b)
-    v1b, v3a = add_parts(
-        [[(0, 0, n, n), (1, 0, n, n)], [(0, 1, 0, n), (1, 1, 0, n)]], (kept_near, near), jnp.bfloat16, "near_sum"
+    (v1b,) = add_parts([[(0, 0, n, n), (1, 0, n, n)]], (kept_up, near_up), jnp.bfloat16, "near_up")
+    (v3a,) = add_parts([[(0, 0, 0, n), (1, 0, 0, n)]], (kept_down, near_down), jnp.bfloat16, "near_down")
+    v_up, v_down = up(v1b), down(v3a)
+    kept_up, kept_down, v1b, v3a, own_grads = lax.optimization_barrier(
+        (kept_up, kept_down, v1b, v3a, local_grads)
     )
-    v_up, v_down = up(v1b), down(v3a)
-    kept_near, near, v1b, v3a = lax.optimization_barrier((kept_near, near, v1b, v3a))
+    (sent_own,) = pieces_of(own_grads, core, y, [(True, 0)], "own_piece")
+    own = swap(sent_own)
     (w1a,) = add_parts(
-        [[(0, 0, 0, n), (1, 0, 0, n), (2, 0, 0, n)]], (kept_near, near, from_down), jnp.bfloat16, "relay_up"
+        [[(0, 0, 0, n), (1, 0, 0, n), (2, 0, 0, n)]], (kept_up, near_up, from_down), jnp.bfloat16, "relay_up"
     )
-    w1a, kept_near = lax.optimization_barrier((w1a, kept_near))
+    w1a, kept_down = lax.optimization_barrier((w1a, kept_down))
     (w3b,) = add_parts(
-        [[(0, 1, n, n), (1, 1, n, n), (2, 0, 0, n)]], (kept_near, near, from_up), jnp.bfloat16, "relay_down"
+        [[(0, 0, n, n), (1, 0, n, n), (2, 0, 0, n)]], (kept_down, near_down, from_up), jnp.bfloat16, "relay_down"
     )
     w_up, w_down = up(w1a), down(w3b)
-    own_a, own_b = add_parts(
-        [[(0, 0, 0, n), (1, 0, 0, n), (3, 0, 0, n)], [(0, 0, n, n), (1, 0, n, n), (2, 0, 0, n)]],
-        (kept_own, own, v_up, v_down),
-        jnp.float32,
-        "own_sum",
-    )
+    own_a, own_b = own_sum(local_grads, core, y, own, v_up, v_down)
     own_a, own_b, chosen, band = lax.optimization_barrier((own_a, own_b, chosen, band))
     sent_a, sent_b, kept = plane_sum(z, own_a, own_b, w_up, w_down)
     got_a = lax.ppermute(sent_a, "z", [(i, i ^ 1) for i in range(Z)])
     got_b = lax.ppermute(sent_b, "z", [(i, (i - 1 + 2 * (i % 2)) % Z) for i in range(Z)])
-    far, up_two, down_two, own = parity_sum(z, kept, got_a, got_b)
+    *sent, own = parity_sum(z, kept, got_a, got_b)
     received = [
-        lax.ppermute(value, "z", [(i, (i + shift) % Z) for i in range(Z)])
-        for value, shift in ((far, 4), (up_two, 2), (down_two, 6))
+        lax.ppermute(value, "z", [(i, i ^ change) for i in range(Z)]) for value, change in zip(sent, (4, 6, 2))
     ]
     mine = mean_rows(own, received, devices)
 
     outgoing = select(core, chosen, mine, swap(mine)).reshape(Z * Y, MOST, -1, columns)
     arrived = lax.all_to_all(outgoing, ("z", "y"), split_axis=0, concat_axis=0, tiled=True)
     own_band, next_band = bands_of(band, arrived)
-    two, one, three = along(own_band, 2), along(next_band, 1), along(next_band, 3)
+    outer = along(next_band, (3, 2, 1, 0))
+    same = along(own_band, (2, 3, 0, 1))
+    partner = along(next_band, (1, 0, 3, 2))
 
     result = pltpu.VMEM((extent, columns), jnp.bfloat16)
     kept, given = pl.pallas_call(
@@ -354,8 +390,8 @@
         out_specs=[IN_VMEM] * 2,
         compiler_params=LARGE,
         name="precondition",
-    )(two, one, three, own_band)
-    return place(band, kept, along(given, 1))
+    )(same, outer, partner, own_band)
+    return place(band, kept, along(given, (1, 0, 3, 2)))
 
 
 def solution(mesh):

time: 92.3 us -> 89.9 us (0.974)
  starting transfers between devices: 32 us -> 29.6 us
  Pallas kernels: 12.2 us -> 13.4 us
    ppermute x3, starting transfers between devices: 7.63 us -> 4.99 us  [down(): return lax.ppermute(value, 'y', [(i, (i - 1) % Y) for i in range(Y)])]
    ppermute x7, waiting for transfers between devices: 12.1 us -> 14.5 us  [the longest x4 9.38 us: along(): return lax.ppermute(value, 'mp', list(enumerate(to)))]
    pallas_call x2 -> x4, Pallas kernels: 3.48 us -> 5.56 us  [the longest x3 4.23 us: pieces_of(): pl.pallas_call(kernel, out_shape=[pltpu.VMEM((1, blocks, rows, columns),...]
    ppermute x7, starting transfers between devices: 11.7 us -> 9.71 us  [the longest x3 5.74 us: on_device(): lax.ppermute(value, 'z', [(i, i ^ change) for i in range(Z)])]
    ppermute x1, waiting for transfers between devices: 1.75 us -> 0.01 us  [on_device(): got_a = lax.ppermute(sent_a, 'z', [(i, i ^ 1) for i in range(Z)])]
    ppermute x3, starting transfers between devices: 0.09 us -> 1.56 us  [up(): return lax.ppermute(value, 'y', [(i, (i + 1) % Y) for i in range(Y)])]
    ppermute x3, waiting for transfers between devices: 4.94 us -> 3.85 us  [up(): return lax.ppermute(value, 'y', [(i, (i + 1) % Y) for i in range(Y)])]
    ppermute x4 -> x5, starting transfers between devices: 7.83 us -> 7.83 us  [swap(): return lax.ppermute(value, 'core', [(0, 1), (1, 0)])]
  transfers between devices with their start and end apart: 19 -> 20, of which waited for: 11 -> 11; matrix products, arithmetic and copies ran while one was open for 1% -> 1% of each run, Pallas kernels for 3% -> 5%
where the time goes in v5:
time: 89.9 us; the launch traced here: 88.4 us
  starting transfers between devices  29.6 us (33%)
  waiting for transfers between devices  26.2 us (29%)
  blocking collectives  18.1 us (20%)
  Pallas kernels  13.4 us (15%)
    all_to_all x1, blocking collectives, on_device(): lax.all_to_all(outgoing, ('z', 'y'), split_axis=0, concat_axis=0, tiled=T...  18.1 us
    ppermute x4, waiting for transfers between devices, along(): return lax.ppermute(value, 'mp', list(enumerate(to)))  9.38 us
    ppermute x5, starting transfers between devices, swap(): return lax.ppermute(value, 'core', [(0, 1), (1, 0)])  7.83 us
    pallas_call x1, Pallas kernels, on_device(): pl.pallas_call(precondition_kernel, out_shape=(result, result), in_specs=...  5.87 us
    ppermute x3, starting transfers between devices, on_device(): lax.ppermute(value, 'z', [(i, i ^ change) for i in range(Z)])  5.74 us
    ppermute x3, waiting for transfers between devices, on_device(): lax.ppermute(value, 'z', [(i, i ^ change) for i in range(Z)])  5.07 us
    ppermute x3, starting transfers between devices, down(): return lax.ppermute(value, 'y', [(i, (i - 1) % Y) for i in range(Y)])  4.99 us
    ppermute x1, starting transfers between devices, on_device(): lax.ppermute(sent_b, 'z', [(i, (i - 1 + 2 * (i % 2)) % Z) for i in range(...  4.67 us
  transfers between devices with their start and end apart: 20, of which 11 were waited for; matrix products, arithmetic and copies ran while one was open for 1% of the time, Pallas kernels for 5%

profile of v5, /device:TPU:1, one launch (start us, length us, event | category | flops | bytes accessed | tf_op | source)
XLA Modules:
  0.0 88.4 jit_solution(7284986599901249411)
XLA Ops:
  0.0 1.5 %sent.1 = (bf16[1,32,64,128]{3,2,1,0:T(8,128)(2,1)S(1)}, bf16[1,32,64,128]{3,2,1,0:T(8,128)(2,1)S(1)}, bf16[1,32,64,128]{3,2,1,0:T(8,128)(2,1)S(1)}) custom-call(s32[1]{0:T(128)} %bitcast.core_ref, s32[1]{0:T(128)} %bitcast.1.y_ref, bf16[32,512,128]{2,1,0:T(8,128)(2,1)} %bitcast.7), custom_call_target="tpu_custom_call" | custom-call | tf_op jit(solution)/shard_map/sent/pallas_call | solution.py:71
  1.6 3.3 %collective-permute-start.5 = (bf16[1,32,64,128]{3,2,1,0:T(8,128)(2,1)S(1)}, bf16[1,32,64,128]{3,2,1,0:T(8,128)(2,1)S(1)}, u32[]{:S(2)}, u32[]{:S(2)}) collective-permute-start(bf16[1,32,64,128]{3,2,1,0:T(8,128)(2,1)S(1)} %get-tuple-element.48), channel_id=1, source_target_pairs={{0,4},{4,0},{1,5},{5,1},{2,6},{6,2},{3,7},{7,3},{8,12},{12,8},{9,1... | collective-permute-start | bytes 1572872 | tf_op jit(solution)/shard_map/ppermute | solution.py:332
  5.4 1.5 %kept.1 = (bf16[1,32,64,128]{3,2,1,0:T(8,128)(2,1)S(1)}, bf16[1,32,64,128]{3,2,1,0:T(8,128)(2,1)S(1)}, bf16[1,32,64,128]{3,2,1,0:T(8,128)(2,1)S(1)}) custom-call(s32[1]{0:T(128)} %bitcast.core_ref, s32[1]{0:T(128)} %bitcast.1.y_ref, bf16[32,512,128]{2,1,0:T(8,128)(2,1)} %bitcast.8), custom_call_target="tpu_custom_call" | custom-call | tf_op jit(solution)/shard_map/kept/pallas_call | solution.py:71
  7.4 2.7 %collective-permute-start.8 = (bf16[1,16,64,128]{3,2,1,0:T(8,128)(2,1)S(1)}, bf16[1,16,64,128]{3,2,1,0:T(8,128)(2,1)S(1)}, u32[]{:S(2)}, u32[]{:S(2)}) collective-permute-start(bf16[1,16,64,128]{3,2,1,0:T(8,128)(2,1)S(1)} %get-tuple-element.53), channel_id=1, source_target_pairs={{0,24},{8,0},{16,8},{24,16},{1,25},{9,1},{17,9},{25,17},{2,26},{10... | collective-permute-start | bytes 786440 | tf_op jit(solution)/shard_map/ppermute | solution.py:338
  10.3 1.1 %own_piece.1 = bf16[1,32,64,128]{3,2,1,0:T(8,128)(2,1)S(1)} custom-call(s32[1]{0:T(128)} %bitcast.core_ref, s32[1]{0:T(128)} %bitcast.1.y_ref, bf16[32,512,128]{2,1,0:T(8,128)(2,1)} %bitcast.9), custom_call_target="tpu_custom_call" | custom-call | tf_op jit(solution)/shard_map/own_piece/pallas_call | solution.py:71
  12.2 1.5 %collective-permute-start.3 = (bf16[1,16,64,128]{3,2,1,0:T(8,128)(2,1)S(1)}, bf16[1,16,64,128]{3,2,1,0:T(8,128)(2,1)S(1)}, u32[]{:S(2)}, u32[]{:S(2)}) collective-permute-start(bf16[1,16,64,128]{3,2,1,0:T(8,128)(2,1)S(1)} %near_up.1), channel_id=1, source_target_pairs={{0,8},{8,16},{16,24},{24,0},{1,9},{9,17},{17,25},{25,1},{2,10},{10... | collective-permute-start | bytes 786440 | tf_op jit(solution)/shard_map/ppermute | solution.py:335
  13.7 2.8 %collective-permute-done.6.refs_2_ = bf16[1,16,64,128]{3,2,1,0:T(8,128)(2,1)S(1)} collective-permute-done((bf16[1,16,64,128]{3,2,1,0:T(8,128)(2,1)S(1)}, bf16[1,16,64,128]{3,2,1,0:T(8,128)(2,1)S(1)}, u32[]{:S(2)}, u32[]{:S(2)}) %collective-permute-start.6) | collective-permute-done | bytes 262176 | tf_op jit(solution)/shard_map/ppermute | solution.py:335
  16.7 2.3 %collective-permute-start.9 = (bf16[1,16,64,128]{3,2,1,0:T(8,128)(2,1)S(1)}, bf16[1,16,64,128]{3,2,1,0:T(8,128)(2,1)S(1)}, u32[]{:S(2)}, u32[]{:S(2)}) collective-permute-start(bf16[1,16,64,128]{3,2,1,0:T(8,128)(2,1)S(1)} %relay_down.1), channel_id=1, source_target_pairs={{0,24},{8,0},{16,8},{24,16},{1,25},{9,1},{17,9},{25,17},{2,26},{10... | collective-permute-start | bytes 786440 | tf_op jit(solution)/shard_map/ppermute | solution.py:338
  19.6 1.4 %collective-permute-done.4.v_down_ref = bf16[1,16,64,128]{3,2,1,0:T(8,128)(2,1)S(1)} collective-permute-done((bf16[1,16,64,128]{3,2,1,0:T(8,128)(2,1)S(1)}, bf16[1,16,64,128]{3,2,1,0:T(8,128)(2,1)S(1)}, u32[]{:S(2)}, u32[]{:S(2)}) %collective-permute-start.4) | collective-permute-done | bytes 262176 | tf_op jit(solution)/shard_map/ppermute | solution.py:338
  22.1 1.3 %own_sum.1 = (f32[1,16,64,128]{3,2,1,0:T(8,128)S(1)}, f32[1,16,64,128]{3,2,1,0:T(8,128)S(1)}) custom-call(s32[1]{0:T(128)} %bitcast.core_ref, s32[1]{0:T(128)} %bitcast.1.y_ref, bf16[32,512,128]{2,1,0:T(8,128)(2,1)} %bitcast.10, bf16[1,32,64,128]{3,2,1,0:T(8,128)(2,1)S(1)} %collective-permute-done.2.got_ref, ...), custom_call_target="tpu_custom_call" | custom-call | tf_op jit(solution)/shard_map/own_sum/pallas_call | solution.py:103
  23.4 3.2 %collective-permute-done.9.w_down_ref = bf16[1,16,64,128]{3,2,1,0:T(8,128)(2,1)S(1)} collective-permute-done((bf16[1,16,64,128]{3,2,1,0:T(8,128)(2,1)S(1)}, bf16[1,16,64,128]{3,2,1,0:T(8,128)(2,1)S(1)}, u32[]{:S(2)}, u32[]{:S(2)}) %collective-permute-start.9) | collective-permute-done | bytes 262176 | tf_op jit(solution)/shard_map/ppermute | solution.py:338
  27.6 4.7 %collective-permute-start.11 = (bf16[4,128,128]{2,1,0:T(8,128)(2,1)S(1)}, bf16[4,128,128]{2,1,0:T(8,128)(2,1)S(1)}, u32[]{:S(2)}, u32[]{:S(2)}) collective-permute-start(bf16[4,128,128]{2,1,0:T(8,128)(2,1)S(1)} %get-tuple-element.56), channel_id=1, source_target_pairs={{0,224},{32,64},{64,32},{96,128},{128,96},{160,192},{192,160},{224... | collective-permute-start | bytes 393224 | tf_op jit(solution)/shard_map/ppermute | solution.py:371
  32.3 2.4 %collective-permute-done.11.b_ref = bf16[4,128,128]{2,1,0:T(8,128)(2,1)S(1)} collective-permute-done((bf16[4,128,128]{2,1,0:T(8,128)(2,1)S(1)}, bf16[4,128,128]{2,1,0:T(8,128)(2,1)S(1)}, u32[]{:S(2)}, u32[]{:S(2)}) %collective-permute-start.11) | collective-permute-done | bytes 131104 | tf_op jit(solution)/shard_map/ppermute | solution.py:371
  34.7 4.1 %collective-permute-start.12 = (bf16[256,128]{1,0:T(8,128)(2,1)S(1)}, bf16[256,128]{1,0:T(8,128)(2,1)S(1)}, u32[]{:S(2)}, u32[]{:S(2)}) collective-permute-start(bf16[256,128]{1,0:T(8,128)(2,1)S(1)} %get-tuple-element.58), channel_id=1, source_target_pairs={{0,128},{32,160},{64,192},{96,224},{128,0},{160,32},{192,64},{224,... | collective-permute-start | bytes 196616 | tf_op jit(solution)/shard_map/ppermute | solution.py:374
  38.8 1.6 %collective-permute-start.14 = (bf16[256,128]{1,0:T(8,128)(2,1)S(1)}, bf16[256,128]{1,0:T(8,128)(2,1)S(1)}, u32[]{:S(2)}, u32[]{:S(2)}) collective-permute-start(bf16[256,128]{1,0:T(8,128)(2,1)S(1)} %get-tuple-element.60), channel_id=1, source_target_pairs={{0,64},{32,96},{64,0},{96,32},{128,192},{160,224},{192,128},{224,1... | collective-permute-start | bytes 196616 | tf_op jit(solution)/shard_map/ppermute | solution.py:374
  40.5 1.4 %collective-permute-done.12.refs_0_ = bf16[256,128]{1,0:T(8,128)(2,1)S(1)} collective-permute-done((bf16[256,128]{1,0:T(8,128)(2,1)S(1)}, bf16[256,128]{1,0:T(8,128)(2,1)S(1)}, u32[]{:S(2)}, u32[]{:S(2)}) %collective-permute-start.12) | collective-permute-done | bytes 65568 | tf_op jit(solution)/shard_map/ppermute | solution.py:374
  41.8 3.7 %collective-permute-done.13.refs_1_ = bf16[256,128]{1,0:T(8,128)(2,1)S(1)} collective-permute-done((bf16[256,128]{1,0:T(8,128)(2,1)S(1)}, bf16[256,128]{1,0:T(8,128)(2,1)S(1)}, u32[]{:S(2)}, u32[]{:S(2)}) %collective-permute-start.13) | collective-permute-done | bytes 65568 | tf_op jit(solution)/shard_map/ppermute | solution.py:374
  45.6 3.3 %collective-permute-start.15 = (bf16[256,128]{1,0:T(8,128)(2,1)S(1)}, bf16[256,128]{1,0:T(8,128)(2,1)S(1)}, u32[]{:S(2)}, u32[]{:S(2)}) collective-permute-start(bf16[256,128]{1,0:T(8,128)(2,1)S(1)} %mean_rows.1.mine_ref), channel_id=1, source_target_pairs={{0,4},{4,0},{1,5},{5,1},{2,6},{6,2},{3,7},{7,3},{8,12},{12,8},{9,1... | collective-permute-start | bytes 196616 | tf_op jit(solution)/shard_map/ppermute | solution.py:332
  50.2 18.1 %all_to_all.5.in_ref = bf16[32,2,16,128]{3,2,1,0:T(8,128)(2,1)S(1)} all-to-all(bf16[32,2,16,128]{3,2,1,0:T(8,128)(2,1)S(1)} %bitcast.6), channel_id=1, replica_groups=mesh['z'=8,'y'=4,'core'=2,'mp'=4] {'z','y'}, dimensions={0} | all-to-all | bytes 524288 | tf_op jit(solution)/shard_map/all_to_all | solution.py:379
  68.3 3.0 %collective-permute-start.16 = (bf16[512,128]{1,0:T(8,128)(2,1)S(1)}, bf16[512,128]{1,0:T(8,128)(2,1)S(1)}, u32[]{:S(2)}, u32[]{:S(2)}) collective-permute-start(bf16[512,128]{1,0:T(8,128)(2,1)S(1)} %get-tuple-element.61.own_ref), channel_id=1, source_target_pairs={{0,2},{1,3},{2,0},{3,1},{4,6},{5,7},{6,4},{7,5},{8,10},{9,11},{10,... | collective-permute-start | bytes 393224 | tf_op jit(solution)/shard_map/ppermute | solution.py:341
  72.2 1.7 %collective-permute-done.16.same_ref = bf16[512,128]{1,0:T(8,128)(2,1)S(1)} collective-permute-done((bf16[512,128]{1,0:T(8,128)(2,1)S(1)}, bf16[512,128]{1,0:T(8,128)(2,1)S(1)}, u32[]{:S(2)}, u32[]{:S(2)}) %collective-permute-start.16) | collective-permute-done | bytes 131104 | tf_op jit(solution)/shard_map/ppermute | solution.py:341
  73.9 3.9 %collective-permute-done.17.outer_ref = bf16[512,128]{1,0:T(8,128)(2,1)S(1)} collective-permute-done((bf16[512,128]{1,0:T(8,128)(2,1)S(1)}, bf16[512,128]{1,0:T(8,128)(2,1)S(1)}, u32[]{:S(2)}, u32[]{:S(2)}) %collective-permute-start.17) | collective-permute-done | bytes 131104 | tf_op jit(solution)/shard_map/ppermute | solution.py:341
  77.7 5.9 %precondition.1 = (bf16[512,128]{1,0:T(8,128)(2,1)S(1)}, bf16[512,128]{1,0:T(8,128)(2,1)S(1)}) custom-call(bf16[512,128]{1,0:T(8,128)(2,1)S(1)} %collective-permute-done.16.same_ref, bf16[512,128]{1,0:T(8,128)(2,1)S(1)} %collective-permute-done.17.outer_ref, bf16[512,128]{1,0:T(8,128)(2,1)S(1)} %collective-permute-done.18.partner_ref, ...), custom_call_target="tpu_custom_call" | custom-call | tf_op jit(solution)/shard_map/precondition/pallas_call | solution.py:386
  83.7 3.8 %collective-permute-done.19.taken_ref = bf16[512,128]{1,0:T(8,128)(2,1)S(1)} collective-permute-done((bf16[512,128]{1,0:T(8,128)(2,1)S(1)}, bf16[512,128]{1,0:T(8,128)(2,1)S(1)}, u32[]{:S(2)}, u32[]{:S(2)}) %collective-permute-start.19) | collective-permute-done | bytes 131104 | tf_op jit(solution)/shard_map/ppermute | solution.py:341
  (41 shorter events, 7.9 us)
Async XLA Ops:
  1.6 5.6 %collective-permute-start.5 = (bf16[1,32,64,128]{3,2,1,0:T(8,128)(2,1)S(1)}, bf16[1,32,64,128]{3,2,1,0:T(8,128)(2,1)S(1)}, u32[]{:S(2)}, u32[]{:S(2)}) collective-permute-start(bf16[1,32,64,128]{3,2,1,0:T(8,128)(2,1)S(1)} %get-tuple-element.48), channel_id=1, source_target_pairs={{0,4},{4,0},{1,5},{5,1},{2,6},{6,2},{3,7},{7,3},{8,12},{12,8},{9,1... | collective-permute-start | bytes 1572872 | tf_op jit(solution)/shard_map/ppermute | solution.py:332
  4.9 5.2 %collective-permute-start.1 = (bf16[1,32,64,128]{3,2,1,0:T(8,128)(2,1)S(1)}, bf16[1,32,64,128]{3,2,1,0:T(8,128)(2,1)S(1)}, u32[]{:S(2)}, u32[]{:S(2)}) collective-permute-start(bf16[1,32,64,128]{3,2,1,0:T(8,128)(2,1)S(1)} %get-tuple-element.38), channel_id=1, source_target_pairs={{0,4},{4,0},{1,5},{5,1},{2,6},{6,2},{3,7},{7,3},{8,12},{12,8},{9,1... | collective-permute-start | bytes 1572872 | tf_op jit(solution)/shard_map/ppermute | solution.py:332
  5.0 2.0 %copy-start = (s32[32]{0:T(128)S(1)}, s32[32]{0:T(128)}, u32[]{:S(2)}) copy-start(s32[32]{0:T(128)} %param.3) | copy-start | bytes 388
  5.0 5.2 %collective-permute-start = (bf16[1,32,64,128]{3,2,1,0:T(8,128)(2,1)S(1)}, bf16[1,32,64,128]{3,2,1,0:T(8,128)(2,1)S(1)}, u32[]{:S(2)}, u32[]{:S(2)}) collective-permute-start(bf16[1,32,64,128]{3,2,1,0:T(8,128)(2,1)S(1)} %get-tuple-element.37), channel_id=1, source_target_pairs={{0,4},{4,0},{1,5},{5,1},{2,6},{6,2},{3,7},{7,3},{8,12},{12,8},{9,1... | collective-permute-start | bytes 1572872 | tf_op jit(solution)/shard_map/ppermute | solution.py:332
  7.3 9.2 %collective-permute-start.6 = (bf16[1,16,64,128]{3,2,1,0:T(8,128)(2,1)S(1)}, bf16[1,16,64,128]{3,2,1,0:T(8,128)(2,1)S(1)}, u32[]{:S(2)}, u32[]{:S(2)}) collective-permute-start(bf16[1,16,64,128]{3,2,1,0:T(8,128)(2,1)S(1)} %get-tuple-element.49), channel_id=1, source_target_pairs={{0,8},{8,16},{16,24},{24,0},{1,9},{9,17},{17,25},{25,1},{2,10},{10... | collective-permute-start | bytes 786440 | tf_op jit(solution)/shard_map/ppermute | solution.py:335
  7.4 9.2 %collective-permute-start.8 = (bf16[1,16,64,128]{3,2,1,0:T(8,128)(2,1)S(1)}, bf16[1,16,64,128]{3,2,1,0:T(8,128)(2,1)S(1)}, u32[]{:S(2)}, u32[]{:S(2)}) collective-permute-start(bf16[1,16,64,128]{3,2,1,0:T(8,128)(2,1)S(1)} %get-tuple-element.53), channel_id=1, source_target_pairs={{0,24},{8,0},{16,8},{24,16},{1,25},{9,1},{17,9},{25,17},{2,26},{10... | collective-permute-start | bytes 786440 | tf_op jit(solution)/shard_map/ppermute | solution.py:338
  11.4 10.6 %collective-permute-start.2 = (bf16[1,32,64,128]{3,2,1,0:T(8,128)(2,1)S(1)}, bf16[1,32,64,128]{3,2,1,0:T(8,128)(2,1)S(1)}, u32[]{:S(2)}, u32[]{:S(2)}) collective-permute-start(bf16[1,32,64,128]{3,2,1,0:T(8,128)(2,1)S(1)} %own_piece.1), channel_id=1, source_target_pairs={{0,4},{4,0},{1,5},{5,1},{2,6},{6,2},{3,7},{7,3},{8,12},{12,8},{9,1... | collective-permute-start | bytes 1572872 | tf_op jit(solution)/shard_map/ppermute | solution.py:332
  12.2 8.8 %collective-permute-start.4 = (bf16[1,16,64,128]{3,2,1,0:T(8,128)(2,1)S(1)}, bf16[1,16,64,128]{3,2,1,0:T(8,128)(2,1)S(1)}, u32[]{:S(2)}, u32[]{:S(2)}) collective-permute-start(bf16[1,16,64,128]{3,2,1,0:T(8,128)(2,1)S(1)} %near_down.1), channel_id=1, source_target_pairs={{0,24},{8,0},{16,8},{24,16},{1,25},{9,1},{17,9},{25,17},{2,26},{10... | collective-permute-start | bytes 786440 | tf_op jit(solution)/shard_map/ppermute | solution.py:338
  12.2 9.9 %collective-permute-start.3 = (bf16[1,16,64,128]{3,2,1,0:T(8,128)(2,1)S(1)}, bf16[1,16,64,128]{3,2,1,0:T(8,128)(2,1)S(1)}, u32[]{:S(2)}, u32[]{:S(2)}) collective-permute-start(bf16[1,16,64,128]{3,2,1,0:T(8,128)(2,1)S(1)} %near_up.1), channel_id=1, source_target_pairs={{0,8},{8,16},{16,24},{24,0},{1,9},{9,17},{17,25},{25,1},{2,10},{10... | collective-permute-start | bytes 786440 | tf_op jit(solution)/shard_map/ppermute | solution.py:335
  16.7 9.9 %collective-permute-start.9 = (bf16[1,16,64,128]{3,2,1,0:T(8,128)(2,1)S(1)}, bf16[1,16,64,128]{3,2,1,0:T(8,128)(2,1)S(1)}, u32[]{:S(2)}, u32[]{:S(2)}) collective-permute-start(bf16[1,16,64,128]{3,2,1,0:T(8,128)(2,1)S(1)} %relay_down.1), channel_id=1, source_target_pairs={{0,24},{8,0},{16,8},{24,16},{1,25},{9,1},{17,9},{25,17},{2,26},{10... | collective-permute-start | bytes 786440 | tf_op jit(solution)/shard_map/ppermute | solution.py:338
  19.0 7.6 %collective-permute-start.7 = (bf16[1,16,64,128]{3,2,1,0:T(8,128)(2,1)S(1)}, bf16[1,16,64,128]{3,2,1,0:T(8,128)(2,1)S(1)}, u32[]{:S(2)}, u32[]{:S(2)}) collective-permute-start(bf16[1,16,64,128]{3,2,1,0:T(8,128)(2,1)S(1)} %relay_up.1), channel_id=1, source_target_pairs={{0,8},{8,16},{16,24},{24,0},{1,9},{9,17},{17,25},{25,1},{2,10},{10... | collective-permute-start | bytes 786440 | tf_op jit(solution)/shard_map/ppermute | solution.py:335
  26.8 5.5 %collective-permute-start.10 = (bf16[4,128,128]{2,1,0:T(8,128)(2,1)S(1)}, bf16[4,128,128]{2,1,0:T(8,128)(2,1)S(1)}, u32[]{:S(2)}, u32[]{:S(2)}) collective-permute-start(bf16[4,128,128]{2,1,0:T(8,128)(2,1)S(1)} %get-tuple-element.55), channel_id=1, source_target_pairs={{0,32},{32,0},{64,96},{96,64},{128,160},{160,128},{192,224},{224,1... | collective-permute-start | bytes 393224 | tf_op jit(solution)/shard_map/ppermute | solution.py:370
  27.6 7.0 %collective-permute-start.11 = (bf16[4,128,128]{2,1,0:T(8,128)(2,1)S(1)}, bf16[4,128,128]{2,1,0:T(8,128)(2,1)S(1)}, u32[]{:S(2)}, u32[]{:S(2)}) collective-permute-start(bf16[4,128,128]{2,1,0:T(8,128)(2,1)S(1)} %get-tuple-element.56), channel_id=1, source_target_pairs={{0,224},{32,64},{64,32},{96,128},{128,96},{160,192},{192,160},{224... | collective-permute-start | bytes 393224 | tf_op jit(solution)/shard_map/ppermute | solution.py:371
  34.7 7.1 %collective-permute-start.12 = (bf16[256,128]{1,0:T(8,128)(2,1)S(1)}, bf16[256,128]{1,0:T(8,128)(2,1)S(1)}, u32[]{:S(2)}, u32[]{:S(2)}) collective-permute-start(bf16[256,128]{1,0:T(8,128)(2,1)S(1)} %get-tuple-element.58), channel_id=1, source_target_pairs={{0,128},{32,160},{64,192},{96,224},{128,0},{160,32},{192,64},{224,... | collective-permute-start | bytes 196616 | tf_op jit(solution)/shard_map/ppermute | solution.py:374
  38.8 6.7 %collective-permute-start.13 = (bf16[256,128]{1,0:T(8,128)(2,1)S(1)}, bf16[256,128]{1,0:T(8,128)(2,1)S(1)}, u32[]{:S(2)}, u32[]{:S(2)}) collective-permute-start(bf16[256,128]{1,0:T(8,128)(2,1)S(1)} %get-tuple-element.59), channel_id=1, source_target_pairs={{0,192},{32,224},{64,128},{96,160},{128,64},{160,96},{192,0},{224,... | collective-permute-start | bytes 196616 | tf_op jit(solution)/shard_map/ppermute | solution.py:374
  38.8 6.7 %collective-permute-start.14 = (bf16[256,128]{1,0:T(8,128)(2,1)S(1)}, bf16[256,128]{1,0:T(8,128)(2,1)S(1)}, u32[]{:S(2)}, u32[]{:S(2)}) collective-permute-start(bf16[256,128]{1,0:T(8,128)(2,1)S(1)} %get-tuple-element.60), channel_id=1, source_target_pairs={{0,64},{32,96},{64,0},{96,32},{128,192},{160,224},{192,128},{224,1... | collective-permute-start | bytes 196616 | tf_op jit(solution)/shard_map/ppermute | solution.py:374
  45.6 4.2 %collective-permute-start.15 = (bf16[256,128]{1,0:T(8,128)(2,1)S(1)}, bf16[256,128]{1,0:T(8,128)(2,1)S(1)}, u32[]{:S(2)}, u32[]{:S(2)}) collective-permute-start(bf16[256,128]{1,0:T(8,128)(2,1)S(1)} %mean_rows.1.mine_ref), channel_id=1, source_target_pairs={{0,4},{4,0},{1,5},{5,1},{2,6},{6,2},{3,7},{7,3},{8,12},{12,8},{9,1... | collective-permute-start | bytes 196616 | tf_op jit(solution)/shard_map/ppermute | solution.py:332
  68.3 5.6 %collective-permute-start.16 = (bf16[512,128]{1,0:T(8,128)(2,1)S(1)}, bf16[512,128]{1,0:T(8,128)(2,1)S(1)}, u32[]{:S(2)}, u32[]{:S(2)}) collective-permute-start(bf16[512,128]{1,0:T(8,128)(2,1)S(1)} %get-tuple-element.61.own_ref), channel_id=1, source_target_pairs={{0,2},{1,3},{2,0},{3,1},{4,6},{5,7},{6,4},{7,5},{8,10},{9,11},{10,... | collective-permute-start | bytes 393224 | tf_op jit(solution)/shard_map/ppermute | solution.py:341
  71.3 6.4 %collective-permute-start.17 = (bf16[512,128]{1,0:T(8,128)(2,1)S(1)}, bf16[512,128]{1,0:T(8,128)(2,1)S(1)}, u32[]{:S(2)}, u32[]{:S(2)}) collective-permute-start(bf16[512,128]{1,0:T(8,128)(2,1)S(1)} %get-tuple-element.62), channel_id=1, source_target_pairs={{0,3},{1,2},{2,1},{3,0},{4,7},{5,6},{6,5},{7,4},{8,11},{9,10},{10,... | collective-permute-start | bytes 393224 | tf_op jit(solution)/shard_map/ppermute | solution.py:341
  72.2 5.6 %collective-permute-start.18 = (bf16[512,128]{1,0:T(8,128)(2,1)S(1)}, bf16[512,128]{1,0:T(8,128)(2,1)S(1)}, u32[]{:S(2)}, u32[]{:S(2)}) collective-permute-start(bf16[512,128]{1,0:T(8,128)(2,1)S(1)} %get-tuple-element.62), channel_id=1, source_target_pairs={{0,1},{1,0},{2,3},{3,2},{4,5},{5,4},{6,7},{7,6},{8,9},{9,8},{10,11... | collective-permute-start | bytes 393224 | tf_op jit(solution)/shard_map/ppermute | solution.py:341
  83.6 3.9 %collective-permute-start.19 = (bf16[512,128]{1,0:T(8,128)(2,1)S(1)}, bf16[512,128]{1,0:T(8,128)(2,1)S(1)}, u32[]{:S(2)}, u32[]{:S(2)}) collective-permute-start(bf16[512,128]{1,0:T(8,128)(2,1)S(1)} %get-tuple-element.64), channel_id=1, source_target_pairs={{0,1},{1,0},{2,3},{3,2},{4,5},{5,4},{6,7},{7,6},{8,9},{9,8},{10,11... | collective-permute-start | bytes 393224 | tf_op jit(solution)/shard_map/ppermute | solution.py:341

commit v6 on v5

--- a/solution.py
+++ b/solution.py
@@ -139,7 +139,7 @@
     )(*arrays)
 
 
-def plane_kernel(z_ref, own_a_ref, own_b_ref, w_up_ref, w_down_ref, sent_a_ref, sent_b_ref, kept_ref):
+def plane_kernel(z_ref, own_a_ref, own_b_ref, w_down_ref, w_up_ref, sent_a_ref, sent_b_ref, kept_ref):
     half, rows = own_a_ref.shape[1:3]
     stripe = rows // Z
     even = z_ref[0] % 2 == 0
@@ -162,7 +162,7 @@
         lax.fori_loop(0, half // 2, add, 0, unroll=2)
 
 
-def plane_sum(z, own_a, own_b, w_up, w_down):
+def plane_sum(z, own_a, own_b, w_down, w_up):
     half, rows, columns = own_a.shape[1:]
     count = half * rows // Z
     sent = pltpu.VMEM((Z // 2, count, columns), jnp.bfloat16)
@@ -173,7 +173,7 @@
         out_specs=[IN_VMEM] * 3,
         compiler_params=PARAMS,
         name="plane_sum",
-    )(z, own_a, own_b, w_up, w_down)
+    )(z, own_a, own_b, w_down, w_up)
 
 
 def parity_kernel(z_ref, kept_ref, a_ref, b_ref, far_ref, outer_ref, inner_ref, own_ref):
@@ -343,7 +343,10 @@
     n = block_count // 2
     sent = pieces_of(local_grads, core, y, [(True, shift) for shift in (2, 1, 3)], "sent")
     far, near_up, near_down = (swap(piece) for piece in sent)
-    kept_far, kept_up, kept_down = pieces_of(local_grads, core, y, [(False, shift) for shift in (2, 1, 3)], "kept")
+    kept_far, kept_up, kept_down, sent_own = pieces_of(
+        local_grads, core, y, [(False, shift) for shift in (2, 1, 3)] + [(True, 0)], "kept"
+    )
+    own = swap(sent_own)
     v2a, v2b = add_parts(
         [[(0, 0, 0, n), (1, 0, 0, n)], [(0, 0, n, n), (1, 0, n, n)]], (kept_far, far), jnp.bfloat16, "far_sum"
     )
@@ -351,22 +354,17 @@
     (v1b,) = add_parts([[(0, 0, n, n), (1, 0, n, n)]], (kept_up, near_up), jnp.bfloat16, "near_up")
     (v3a,) = add_parts([[(0, 0, 0, n), (1, 0, 0, n)]], (kept_down, near_down), jnp.bfloat16, "near_down")
     v_up, v_down = up(v1b), down(v3a)
-    kept_up, kept_down, v1b, v3a, own_grads = lax.optimization_barrier(
-        (kept_up, kept_down, v1b, v3a, local_grads)
-    )
-    (sent_own,) = pieces_of(own_grads, core, y, [(True, 0)], "own_piece")
-    own = swap(sent_own)
+    kept_up, kept_down, v1b, v3a = lax.optimization_barrier((kept_up, kept_down, v1b, v3a))
     (w1a,) = add_parts(
         [[(0, 0, 0, n), (1, 0, 0, n), (2, 0, 0, n)]], (kept_up, near_up, from_down), jnp.bfloat16, "relay_up"
     )
-    w1a, kept_down = lax.optimization_barrier((w1a, kept_down))
     (w3b,) = add_parts(
         [[(0, 0, n, n), (1, 0, n, n), (2, 0, 0, n)]], (kept_down, near_down, from_up), jnp.bfloat16, "relay_down"
     )
     w_up, w_down = up(w1a), down(w3b)
     own_a, own_b = own_sum(local_grads, core, y, own, v_up, v_down)
     own_a, own_b, chosen, band = lax.optimization_barrier((own_a, own_b, chosen, band))
-    sent_a, sent_b, kept = plane_sum(z, own_a, own_b, w_up, w_down)
+    sent_a, sent_b, kept = plane_sum(z, own_a, own_b, w_down, w_up)
     got_a = lax.ppermute(sent_a, "z", [(i, i ^ 1) for i in range(Z)])
     got_b = lax.ppermute(sent_b, "z", [(i, (i - 1 + 2 * (i % 2)) % Z) for i in range(Z)])
     *sent, own = parity_sum(z, kept, got_a, got_b)

time: 89.9 us -> 90.2 us (level)
  starting transfers between devices: 29.6 us -> 30.7 us
    ppermute x3, waiting for transfers between devices: 3.85 us -> 9.18 us  [up(): return lax.ppermute(value, 'y', [(i, (i + 1) % Y) for i in range(Y)])]
    ppermute x3, waiting for transfers between devices: 4.64 us -> 0.01 us  [down(): return lax.ppermute(value, 'y', [(i, (i - 1) % Y) for i in range(Y)])]
    ppermute x3, starting transfers between devices: 4.99 us -> 8.12 us  [down(): return lax.ppermute(value, 'y', [(i, (i - 1) % Y) for i in range(Y)])]
    ppermute x3, starting transfers between devices: 1.56 us -> 0.25 us  [up(): return lax.ppermute(value, 'y', [(i, (i + 1) % Y) for i in range(Y)])]
    ppermute x3, waiting for transfers between devices: 5.07 us -> 3.89 us  [on_device(): lax.ppermute(value, 'z', [(i, i ^ change) for i in range(Z)])]
    pallas_call x3 -> x2, Pallas kernels: 4.23 us -> 3.29 us  [pieces_of(): pl.pallas_call(kernel, out_shape=[pltpu.VMEM((1, blocks, rows, columns),...]
  transfers between devices with their start and end apart: 20 -> 20, of which waited for: 11 -> 10; matrix products, arithmetic and copies ran while one was open for 1% -> 1% of each run, Pallas kernels for 5% -> 4%
where the time goes in v6:
time: 90.2 us; the launch traced here: 88.7 us
  starting transfers between devices  30.7 us (34%)
  waiting for transfers between devices  25.7 us (28%)
  blocking collectives  18.7 us (21%)
  Pallas kernels  12.5 us (14%)
    all_to_all x1, blocking collectives, on_device(): lax.all_to_all(outgoing, ('z', 'y'), split_axis=0, concat_axis=0, tiled=T...  18.7 us
    ppermute x4, waiting for transfers between devices, along(): return lax.ppermute(value, 'mp', list(enumerate(to)))  9.35 us
    ppermute x3, waiting for transfers between devices, up(): return lax.ppermute(value, 'y', [(i, (i + 1) % Y) for i in range(Y)])  9.18 us
    ppermute x3, starting transfers between devices, down(): return lax.ppermute(value, 'y', [(i, (i - 1) % Y) for i in range(Y)])  8.12 us
    ppermute x5, starting transfers between devices, swap(): return lax.ppermute(value, 'core', [(0, 1), (1, 0)])  7.86 us
    pallas_call x1, Pallas kernels, on_device(): pl.pallas_call(precondition_kernel, out_shape=(result, result), in_specs=...  5.87 us
    ppermute x3, starting transfers between devices, on_device(): lax.ppermute(value, 'z', [(i, i ^ change) for i in range(Z)])  5.74 us
    ppermute x1, starting transfers between devices, on_device(): lax.ppermute(sent_b, 'z', [(i, (i - 1 + 2 * (i % 2)) % Z) for i in range(...  4.67 us
  transfers between devices with their start and end apart: 20, of which 10 were waited for; matrix products, arithmetic and copies ran while one was open for 1% of the time, Pallas kernels for 4%

profile of v6, /device:TPU:1, one launch (start us, length us, event | category | flops | bytes accessed | tf_op | source)
XLA Modules:
  0.0 88.7 jit_solution(12521838589554078829)
XLA Ops:
  0.0 1.5 %sent.1 = (bf16[1,32,64,128]{3,2,1,0:T(8,128)(2,1)S(1)}, bf16[1,32,64,128]{3,2,1,0:T(8,128)(2,1)S(1)}, bf16[1,32,64,128]{3,2,1,0:T(8,128)(2,1)S(1)}) custom-call(s32[1]{0:T(128)} %bitcast.core_ref, s32[1]{0:T(128)} %bitcast.1.y_ref, bf16[32,512,128]{2,1,0:T(8,128)(2,1)} %bitcast.7), custom_call_target="tpu_custom_call" | custom-call | tf_op jit(solution)/shard_map/sent/pallas_call | solution.py:71
  1.6 3.3 %collective-permute-start.5 = (bf16[1,32,64,128]{3,2,1,0:T(8,128)(2,1)S(1)}, bf16[1,32,64,128]{3,2,1,0:T(8,128)(2,1)S(1)}, u32[]{:S(2)}, u32[]{:S(2)}) collective-permute-start(bf16[1,32,64,128]{3,2,1,0:T(8,128)(2,1)S(1)} %get-tuple-element.46), channel_id=1, source_target_pairs={{0,4},{4,0},{1,5},{5,1},{2,6},{6,2},{3,7},{7,3},{8,12},{12,8},{9,1... | collective-permute-start | bytes 1572872 | tf_op jit(solution)/shard_map/ppermute | solution.py:332
  5.4 1.7 %kept.1 = (bf16[1,32,64,128]{3,2,1,0:T(8,128)(2,1)S(1)}, bf16[1,32,64,128]{3,2,1,0:T(8,128)(2,1)S(1)}, bf16[1,32,64,128]{3,2,1,0:T(8,128)(2,1)S(1)}, bf16[1,32,64,128]{3,2,1,0:T(8,128)(2,1)S(1)}) custom-call(s32[1]{0:T(128)} %bitcast.core_ref, s32[1]{0:T(128)} %bitcast.1.y_ref, bf16[32,512,128]{2,1,0:T(8,128)(2,1)} %bitcast.8), custom_call_target="tpu_custom_call" | custom-call | tf_op jit(solution)/shard_map/kept/pallas_call | solution.py:71
  7.8 2.7 %collective-permute-start.6 = (bf16[1,16,64,128]{3,2,1,0:T(8,128)(2,1)S(1)}, bf16[1,16,64,128]{3,2,1,0:T(8,128)(2,1)S(1)}, u32[]{:S(2)}, u32[]{:S(2)}) collective-permute-start(bf16[1,16,64,128]{3,2,1,0:T(8,128)(2,1)S(1)} %get-tuple-element.47), channel_id=1, source_target_pairs={{0,24},{8,0},{16,8},{24,16},{1,25},{9,1},{17,9},{25,17},{2,26},{10... | collective-permute-start | bytes 786440 | tf_op jit(solution)/shard_map/ppermute | solution.py:338
  10.8 2.7 %collective-permute-start.4 = (bf16[1,16,64,128]{3,2,1,0:T(8,128)(2,1)S(1)}, bf16[1,16,64,128]{3,2,1,0:T(8,128)(2,1)S(1)}, u32[]{:S(2)}, u32[]{:S(2)}) collective-permute-start(bf16[1,16,64,128]{3,2,1,0:T(8,128)(2,1)S(1)} %near_down.1), channel_id=1, source_target_pairs={{0,24},{8,0},{16,8},{24,16},{1,25},{9,1},{17,9},{25,17},{2,26},{10... | collective-permute-start | bytes 786440 | tf_op jit(solution)/shard_map/ppermute | solution.py:338
  13.5 3.0 %collective-permute-done.8.refs_2_ = bf16[1,16,64,128]{3,2,1,0:T(8,128)(2,1)S(1)} collective-permute-done((bf16[1,16,64,128]{3,2,1,0:T(8,128)(2,1)S(1)}, bf16[1,16,64,128]{3,2,1,0:T(8,128)(2,1)S(1)}, u32[]{:S(2)}, u32[]{:S(2)}) %collective-permute-start.8) | collective-permute-done | bytes 262176 | tf_op jit(solution)/shard_map/ppermute | solution.py:335
  16.8 2.7 %collective-permute-start.7 = (bf16[1,16,64,128]{3,2,1,0:T(8,128)(2,1)S(1)}, bf16[1,16,64,128]{3,2,1,0:T(8,128)(2,1)S(1)}, u32[]{:S(2)}, u32[]{:S(2)}) collective-permute-start(bf16[1,16,64,128]{3,2,1,0:T(8,128)(2,1)S(1)} %relay_down.1), channel_id=1, source_target_pairs={{0,24},{8,0},{16,8},{24,16},{1,25},{9,1},{17,9},{25,17},{2,26},{10... | collective-permute-start | bytes 786440 | tf_op jit(solution)/shard_map/ppermute | solution.py:338
  20.1 1.9 %collective-permute-done.2.v_up_ref = bf16[1,16,64,128]{3,2,1,0:T(8,128)(2,1)S(1)} collective-permute-done((bf16[1,16,64,128]{3,2,1,0:T(8,128)(2,1)S(1)}, bf16[1,16,64,128]{3,2,1,0:T(8,128)(2,1)S(1)}, u32[]{:S(2)}, u32[]{:S(2)}) %collective-permute-start.2) | collective-permute-done | bytes 262176 | tf_op jit(solution)/shard_map/ppermute | solution.py:335
  22.1 1.3 %own_sum.1 = (f32[1,16,64,128]{3,2,1,0:T(8,128)S(1)}, f32[1,16,64,128]{3,2,1,0:T(8,128)S(1)}) custom-call(s32[1]{0:T(128)} %bitcast.core_ref, s32[1]{0:T(128)} %bitcast.1.y_ref, bf16[32,512,128]{2,1,0:T(8,128)(2,1)} %bitcast.9, bf16[1,32,64,128]{3,2,1,0:T(8,128)(2,1)S(1)} %collective-permute-done.got_ref, ...), custom_call_target="tpu_custom_call" | custom-call | tf_op jit(solution)/shard_map/own_sum/pallas_call | solution.py:103
  23.4 4.3 %collective-permute-done.9.w_up_ref = bf16[1,16,64,128]{3,2,1,0:T(8,128)(2,1)S(1)} collective-permute-done((bf16[1,16,64,128]{3,2,1,0:T(8,128)(2,1)S(1)}, bf16[1,16,64,128]{3,2,1,0:T(8,128)(2,1)S(1)}, u32[]{:S(2)}, u32[]{:S(2)}) %collective-permute-start.9) | collective-permute-done | bytes 262176 | tf_op jit(solution)/shard_map/ppermute | solution.py:335
  28.0 4.7 %collective-permute-start.11 = (bf16[4,128,128]{2,1,0:T(8,128)(2,1)S(1)}, bf16[4,128,128]{2,1,0:T(8,128)(2,1)S(1)}, u32[]{:S(2)}, u32[]{:S(2)}) collective-permute-start(bf16[4,128,128]{2,1,0:T(8,128)(2,1)S(1)} %get-tuple-element.52), channel_id=1, source_target_pairs={{0,224},{32,64},{64,32},{96,128},{128,96},{160,192},{192,160},{224... | collective-permute-start | bytes 393224 | tf_op jit(solution)/shard_map/ppermute | solution.py:369
  32.7 2.4 %collective-permute-done.11.b_ref = bf16[4,128,128]{2,1,0:T(8,128)(2,1)S(1)} collective-permute-done((bf16[4,128,128]{2,1,0:T(8,128)(2,1)S(1)}, bf16[4,128,128]{2,1,0:T(8,128)(2,1)S(1)}, u32[]{:S(2)}, u32[]{:S(2)}) %collective-permute-start.11) | collective-permute-done | bytes 131104 | tf_op jit(solution)/shard_map/ppermute | solution.py:369
  35.1 4.1 %collective-permute-start.12 = (bf16[256,128]{1,0:T(8,128)(2,1)S(1)}, bf16[256,128]{1,0:T(8,128)(2,1)S(1)}, u32[]{:S(2)}, u32[]{:S(2)}) collective-permute-start(bf16[256,128]{1,0:T(8,128)(2,1)S(1)} %get-tuple-element.54), channel_id=1, source_target_pairs={{0,128},{32,160},{64,192},{96,224},{128,0},{160,32},{192,64},{224,... | collective-permute-start | bytes 196616 | tf_op jit(solution)/shard_map/ppermute | solution.py:372
  39.2 1.6 %collective-permute-start.14 = (bf16[256,128]{1,0:T(8,128)(2,1)S(1)}, bf16[256,128]{1,0:T(8,128)(2,1)S(1)}, u32[]{:S(2)}, u32[]{:S(2)}) collective-permute-start(bf16[256,128]{1,0:T(8,128)(2,1)S(1)} %get-tuple-element.56), channel_id=1, source_target_pairs={{0,64},{32,96},{64,0},{96,32},{128,192},{160,224},{192,128},{224,1... | collective-permute-start | bytes 196616 | tf_op jit(solution)/shard_map/ppermute | solution.py:372
  40.8 1.4 %collective-permute-done.12.refs_0_ = bf16[256,128]{1,0:T(8,128)(2,1)S(1)} collective-permute-done((bf16[256,128]{1,0:T(8,128)(2,1)S(1)}, bf16[256,128]{1,0:T(8,128)(2,1)S(1)}, u32[]{:S(2)}, u32[]{:S(2)}) %collective-permute-start.12) | collective-permute-done | bytes 65568 | tf_op jit(solution)/shard_map/ppermute | solution.py:372
  42.2 2.5 %collective-permute-done.13.refs_1_ = bf16[256,128]{1,0:T(8,128)(2,1)S(1)} collective-permute-done((bf16[256,128]{1,0:T(8,128)(2,1)S(1)}, bf16[256,128]{1,0:T(8,128)(2,1)S(1)}, u32[]{:S(2)}, u32[]{:S(2)}) %collective-permute-start.13) | collective-permute-done | bytes 65568 | tf_op jit(solution)/shard_map/ppermute | solution.py:372
  44.7 3.8 %collective-permute-start.15 = (bf16[256,128]{1,0:T(8,128)(2,1)S(1)}, bf16[256,128]{1,0:T(8,128)(2,1)S(1)}, u32[]{:S(2)}, u32[]{:S(2)}) collective-permute-start(bf16[256,128]{1,0:T(8,128)(2,1)S(1)} %mean_rows.1.mine_ref), channel_id=1, source_target_pairs={{0,4},{4,0},{1,5},{5,1},{2,6},{6,2},{3,7},{7,3},{8,12},{12,8},{9,1... | collective-permute-start | bytes 196616 | tf_op jit(solution)/shard_map/ppermute | solution.py:332
  48.6 0.9 %collective-permute-done.15.other_ref = bf16[256,128]{1,0:T(8,128)(2,1)S(1)} collective-permute-done((bf16[256,128]{1,0:T(8,128)(2,1)S(1)}, bf16[256,128]{1,0:T(8,128)(2,1)S(1)}, u32[]{:S(2)}, u32[]{:S(2)}) %collective-permute-start.15) | collective-permute-done | bytes 65568 | tf_op jit(solution)/shard_map/ppermute | solution.py:332
  49.9 18.7 %all_to_all.5.in_ref = bf16[32,2,16,128]{3,2,1,0:T(8,128)(2,1)S(1)} all-to-all(bf16[32,2,16,128]{3,2,1,0:T(8,128)(2,1)S(1)} %bitcast.6), channel_id=1, replica_groups=mesh['z'=8,'y'=4,'core'=2,'mp'=4] {'z','y'}, dimensions={0} | all-to-all | bytes 524288 | tf_op jit(solution)/shard_map/all_to_all | solution.py:377
  68.6 3.0 %collective-permute-start.16 = (bf16[512,128]{1,0:T(8,128)(2,1)S(1)}, bf16[512,128]{1,0:T(8,128)(2,1)S(1)}, u32[]{:S(2)}, u32[]{:S(2)}) collective-permute-start(bf16[512,128]{1,0:T(8,128)(2,1)S(1)} %get-tuple-element.57.own_ref), channel_id=1, source_target_pairs={{0,2},{1,3},{2,0},{3,1},{4,6},{5,7},{6,4},{7,5},{8,10},{9,11},{10,... | collective-permute-start | bytes 393224 | tf_op jit(solution)/shard_map/ppermute | solution.py:341
  72.5 1.7 %collective-permute-done.16.same_ref = bf16[512,128]{1,0:T(8,128)(2,1)S(1)} collective-permute-done((bf16[512,128]{1,0:T(8,128)(2,1)S(1)}, bf16[512,128]{1,0:T(8,128)(2,1)S(1)}, u32[]{:S(2)}, u32[]{:S(2)}) %collective-permute-start.16) | collective-permute-done | bytes 131104 | tf_op jit(solution)/shard_map/ppermute | solution.py:341
  74.2 3.8 %collective-permute-done.17.outer_ref = bf16[512,128]{1,0:T(8,128)(2,1)S(1)} collective-permute-done((bf16[512,128]{1,0:T(8,128)(2,1)S(1)}, bf16[512,128]{1,0:T(8,128)(2,1)S(1)}, u32[]{:S(2)}, u32[]{:S(2)}) %collective-permute-start.17) | collective-permute-done | bytes 131104 | tf_op jit(solution)/shard_map/ppermute | solution.py:341
  78.0 5.9 %precondition.1 = (bf16[512,128]{1,0:T(8,128)(2,1)S(1)}, bf16[512,128]{1,0:T(8,128)(2,1)S(1)}) custom-call(bf16[512,128]{1,0:T(8,128)(2,1)S(1)} %collective-permute-done.16.same_ref, bf16[512,128]{1,0:T(8,128)(2,1)S(1)} %collective-permute-done.17.outer_ref, bf16[512,128]{1,0:T(8,128)(2,1)S(1)} %collective-permute-done.18.partner_ref, ...), custom_call_target="tpu_custom_call" | custom-call | tf_op jit(solution)/shard_map/precondition/pallas_call | solution.py:384
  84.0 3.8 %collective-permute-done.19.taken_ref = bf16[512,128]{1,0:T(8,128)(2,1)S(1)} collective-permute-done((bf16[512,128]{1,0:T(8,128)(2,1)S(1)}, bf16[512,128]{1,0:T(8,128)(2,1)S(1)}, u32[]{:S(2)}, u32[]{:S(2)}) %collective-permute-start.19) | collective-permute-done | bytes 131104 | tf_op jit(solution)/shard_map/ppermute | solution.py:341
  (40 shorter events, 4.9 us)
Async XLA Ops:
  1.6 6.0 %collective-permute-start.5 = (bf16[1,32,64,128]{3,2,1,0:T(8,128)(2,1)S(1)}, bf16[1,32,64,128]{3,2,1,0:T(8,128)(2,1)S(1)}, u32[]{:S(2)}, u32[]{:S(2)}) collective-permute-start(bf16[1,32,64,128]{3,2,1,0:T(8,128)(2,1)S(1)} %get-tuple-element.46), channel_id=1, source_target_pairs={{0,4},{4,0},{1,5},{5,1},{2,6},{6,2},{3,7},{7,3},{8,12},{12,8},{9,1... | collective-permute-start | bytes 1572872 | tf_op jit(solution)/shard_map/ppermute | solution.py:332
  4.9 5.6 %collective-permute-start.1 = (bf16[1,32,64,128]{3,2,1,0:T(8,128)(2,1)S(1)}, bf16[1,32,64,128]{3,2,1,0:T(8,128)(2,1)S(1)}, u32[]{:S(2)}, u32[]{:S(2)}) collective-permute-start(bf16[1,32,64,128]{3,2,1,0:T(8,128)(2,1)S(1)} %get-tuple-element.35), channel_id=1, source_target_pairs={{0,4},{4,0},{1,5},{5,1},{2,6},{6,2},{3,7},{7,3},{8,12},{12,8},{9,1... | collective-permute-start | bytes 1572872 | tf_op jit(solution)/shard_map/ppermute | solution.py:332
  5.0 2.4 %copy-start = (s32[32]{0:T(128)S(1)}, s32[32]{0:T(128)}, u32[]{:S(2)}) copy-start(s32[32]{0:T(128)} %param.3) | copy-start | bytes 388
  5.0 5.7 %collective-permute-start.3 = (bf16[1,32,64,128]{3,2,1,0:T(8,128)(2,1)S(1)}, bf16[1,32,64,128]{3,2,1,0:T(8,128)(2,1)S(1)}, u32[]{:S(2)}, u32[]{:S(2)}) collective-permute-start(bf16[1,32,64,128]{3,2,1,0:T(8,128)(2,1)S(1)} %get-tuple-element.37), channel_id=1, source_target_pairs={{0,4},{4,0},{1,5},{5,1},{2,6},{6,2},{3,7},{7,3},{8,12},{12,8},{9,1... | collective-permute-start | bytes 1572872 | tf_op jit(solution)/shard_map/ppermute | solution.py:332
  7.1 13.0 %collective-permute-start = (bf16[1,32,64,128]{3,2,1,0:T(8,128)(2,1)S(1)}, bf16[1,32,64,128]{3,2,1,0:T(8,128)(2,1)S(1)}, u32[]{:S(2)}, u32[]{:S(2)}) collective-permute-start(bf16[1,32,64,128]{3,2,1,0:T(8,128)(2,1)S(1)} %get-tuple-element.33), channel_id=1, source_target_pairs={{0,4},{4,0},{1,5},{5,1},{2,6},{6,2},{3,7},{7,3},{8,12},{12,8},{9,1... | collective-permute-start | bytes 1572872 | tf_op jit(solution)/shard_map/ppermute | solution.py:332
  7.7 8.8 %collective-permute-start.8 = (bf16[1,16,64,128]{3,2,1,0:T(8,128)(2,1)S(1)}, bf16[1,16,64,128]{3,2,1,0:T(8,128)(2,1)S(1)}, u32[]{:S(2)}, u32[]{:S(2)}) collective-permute-start(bf16[1,16,64,128]{3,2,1,0:T(8,128)(2,1)S(1)} %get-tuple-element.49), channel_id=1, source_target_pairs={{0,8},{8,16},{16,24},{24,0},{1,9},{9,17},{17,25},{25,1},{2,10},{10... | collective-permute-start | bytes 786440 | tf_op jit(solution)/shard_map/ppermute | solution.py:335
  7.8 8.9 %collective-permute-start.6 = (bf16[1,16,64,128]{3,2,1,0:T(8,128)(2,1)S(1)}, bf16[1,16,64,128]{3,2,1,0:T(8,128)(2,1)S(1)}, u32[]{:S(2)}, u32[]{:S(2)}) collective-permute-start(bf16[1,16,64,128]{3,2,1,0:T(8,128)(2,1)S(1)} %get-tuple-element.47), channel_id=1, source_target_pairs={{0,24},{8,0},{16,8},{24,16},{1,25},{9,1},{17,9},{25,17},{2,26},{10... | collective-permute-start | bytes 786440 | tf_op jit(solution)/shard_map/ppermute | solution.py:338
  10.6 11.5 %collective-permute-start.2 = (bf16[1,16,64,128]{3,2,1,0:T(8,128)(2,1)S(1)}, bf16[1,16,64,128]{3,2,1,0:T(8,128)(2,1)S(1)}, u32[]{:S(2)}, u32[]{:S(2)}) collective-permute-start(bf16[1,16,64,128]{3,2,1,0:T(8,128)(2,1)S(1)} %near_up.1), channel_id=1, source_target_pairs={{0,8},{8,16},{16,24},{24,0},{1,9},{9,17},{17,25},{25,1},{2,10},{10... | collective-permute-start | bytes 786440 | tf_op jit(solution)/shard_map/ppermute | solution.py:335
  10.8 11.3 %collective-permute-start.4 = (bf16[1,16,64,128]{3,2,1,0:T(8,128)(2,1)S(1)}, bf16[1,16,64,128]{3,2,1,0:T(8,128)(2,1)S(1)}, u32[]{:S(2)}, u32[]{:S(2)}) collective-permute-start(bf16[1,16,64,128]{3,2,1,0:T(8,128)(2,1)S(1)} %near_down.1), channel_id=1, source_target_pairs={{0,24},{8,0},{16,8},{24,16},{1,25},{9,1},{17,9},{25,17},{2,26},{10... | collective-permute-start | bytes 786440 | tf_op jit(solution)/shard_map/ppermute | solution.py:338
  16.6 11.1 %collective-permute-start.9 = (bf16[1,16,64,128]{3,2,1,0:T(8,128)(2,1)S(1)}, bf16[1,16,64,128]{3,2,1,0:T(8,128)(2,1)S(1)}, u32[]{:S(2)}, u32[]{:S(2)}) collective-permute-start(bf16[1,16,64,128]{3,2,1,0:T(8,128)(2,1)S(1)} %relay_up.1), channel_id=1, source_target_pairs={{0,8},{8,16},{16,24},{24,0},{1,9},{9,17},{17,25},{25,1},{2,10},{10... | collective-permute-start | bytes 786440 | tf_op jit(solution)/shard_map/ppermute | solution.py:335
  16.8 10.9 %collective-permute-start.7 = (bf16[1,16,64,128]{3,2,1,0:T(8,128)(2,1)S(1)}, bf16[1,16,64,128]{3,2,1,0:T(8,128)(2,1)S(1)}, u32[]{:S(2)}, u32[]{:S(2)}) collective-permute-start(bf16[1,16,64,128]{3,2,1,0:T(8,128)(2,1)S(1)} %relay_down.1), channel_id=1, source_target_pairs={{0,24},{8,0},{16,8},{24,16},{1,25},{9,1},{17,9},{25,17},{2,26},{10... | collective-permute-start | bytes 786440 | tf_op jit(solution)/shard_map/ppermute | solution.py:338
  27.9 4.8 %collective-permute-start.10 = (bf16[4,128,128]{2,1,0:T(8,128)(2,1)S(1)}, bf16[4,128,128]{2,1,0:T(8,128)(2,1)S(1)}, u32[]{:S(2)}, u32[]{:S(2)}) collective-permute-start(bf16[4,128,128]{2,1,0:T(8,128)(2,1)S(1)} %get-tuple-element.51), channel_id=1, source_target_pairs={{0,32},{32,0},{64,96},{96,64},{128,160},{160,128},{192,224},{224,1... | collective-permute-start | bytes 393224 | tf_op jit(solution)/shard_map/ppermute | solution.py:368
  28.0 7.0 %collective-permute-start.11 = (bf16[4,128,128]{2,1,0:T(8,128)(2,1)S(1)}, bf16[4,128,128]{2,1,0:T(8,128)(2,1)S(1)}, u32[]{:S(2)}, u32[]{:S(2)}) collective-permute-start(bf16[4,128,128]{2,1,0:T(8,128)(2,1)S(1)} %get-tuple-element.52), channel_id=1, source_target_pairs={{0,224},{32,64},{64,32},{96,128},{128,96},{160,192},{192,160},{224... | collective-permute-start | bytes 393224 | tf_op jit(solution)/shard_map/ppermute | solution.py:369
  35.1 7.1 %collective-permute-start.12 = (bf16[256,128]{1,0:T(8,128)(2,1)S(1)}, bf16[256,128]{1,0:T(8,128)(2,1)S(1)}, u32[]{:S(2)}, u32[]{:S(2)}) collective-permute-start(bf16[256,128]{1,0:T(8,128)(2,1)S(1)} %get-tuple-element.54), channel_id=1, source_target_pairs={{0,128},{32,160},{64,192},{96,224},{128,0},{160,32},{192,64},{224,... | collective-permute-start | bytes 196616 | tf_op jit(solution)/shard_map/ppermute | solution.py:372
  39.2 5.5 %collective-permute-start.13 = (bf16[256,128]{1,0:T(8,128)(2,1)S(1)}, bf16[256,128]{1,0:T(8,128)(2,1)S(1)}, u32[]{:S(2)}, u32[]{:S(2)}) collective-permute-start(bf16[256,128]{1,0:T(8,128)(2,1)S(1)} %get-tuple-element.55), channel_id=1, source_target_pairs={{0,192},{32,224},{64,128},{96,160},{128,64},{160,96},{192,0},{224,... | collective-permute-start | bytes 196616 | tf_op jit(solution)/shard_map/ppermute | solution.py:372
  39.2 5.5 %collective-permute-start.14 = (bf16[256,128]{1,0:T(8,128)(2,1)S(1)}, bf16[256,128]{1,0:T(8,128)(2,1)S(1)}, u32[]{:S(2)}, u32[]{:S(2)}) collective-permute-start(bf16[256,128]{1,0:T(8,128)(2,1)S(1)} %get-tuple-element.56), channel_id=1, source_target_pairs={{0,64},{32,96},{64,0},{96,32},{128,192},{160,224},{192,128},{224,1... | collective-permute-start | bytes 196616 | tf_op jit(solution)/shard_map/ppermute | solution.py:372
  44.7 4.7 %collective-permute-start.15 = (bf16[256,128]{1,0:T(8,128)(2,1)S(1)}, bf16[256,128]{1,0:T(8,128)(2,1)S(1)}, u32[]{:S(2)}, u32[]{:S(2)}) collective-permute-start(bf16[256,128]{1,0:T(8,128)(2,1)S(1)} %mean_rows.1.mine_ref), channel_id=1, source_target_pairs={{0,4},{4,0},{1,5},{5,1},{2,6},{6,2},{3,7},{7,3},{8,12},{12,8},{9,1... | collective-permute-start | bytes 196616 | tf_op jit(solution)/shard_map/ppermute | solution.py:332
  68.6 5.6 %collective-permute-start.16 = (bf16[512,128]{1,0:T(8,128)(2,1)S(1)}, bf16[512,128]{1,0:T(8,128)(2,1)S(1)}, u32[]{:S(2)}, u32[]{:S(2)}) collective-permute-start(bf16[512,128]{1,0:T(8,128)(2,1)S(1)} %get-tuple-element.57.own_ref), channel_id=1, source_target_pairs={{0,2},{1,3},{2,0},{3,1},{4,6},{5,7},{6,4},{7,5},{8,10},{9,11},{10,... | collective-permute-start | bytes 393224 | tf_op jit(solution)/shard_map/ppermute | solution.py:341
  71.6 6.4 %collective-permute-start.17 = (bf16[512,128]{1,0:T(8,128)(2,1)S(1)}, bf16[512,128]{1,0:T(8,128)(2,1)S(1)}, u32[]{:S(2)}, u32[]{:S(2)}) collective-permute-start(bf16[512,128]{1,0:T(8,128)(2,1)S(1)} %get-tuple-element.58), channel_id=1, source_target_pairs={{0,3},{1,2},{2,1},{3,0},{4,7},{5,6},{6,5},{7,4},{8,11},{9,10},{10,... | collective-permute-start | bytes 393224 | tf_op jit(solution)/shard_map/ppermute | solution.py:341
  72.5 5.6 %collective-permute-start.18 = (bf16[512,128]{1,0:T(8,128)(2,1)S(1)}, bf16[512,128]{1,0:T(8,128)(2,1)S(1)}, u32[]{:S(2)}, u32[]{:S(2)}) collective-permute-start(bf16[512,128]{1,0:T(8,128)(2,1)S(1)} %get-tuple-element.58), channel_id=1, source_target_pairs={{0,1},{1,0},{2,3},{3,2},{4,5},{5,4},{6,7},{7,6},{8,9},{9,8},{10,11... | collective-permute-start | bytes 393224 | tf_op jit(solution)/shard_map/ppermute | solution.py:341
  83.9 3.9 %collective-permute-start.19 = (bf16[512,128]{1,0:T(8,128)(2,1)S(1)}, bf16[512,128]{1,0:T(8,128)(2,1)S(1)}, u32[]{:S(2)}, u32[]{:S(2)}) collective-permute-start(bf16[512,128]{1,0:T(8,128)(2,1)S(1)} %get-tuple-element.60), channel_id=1, source_target_pairs={{0,1},{1,0},{2,3},{3,2},{4,5},{5,4},{6,7},{7,6},{8,9},{9,8},{10,11... | collective-permute-start | bytes 393224 | tf_op jit(solution)/shard_map/ppermute | solution.py:341

commit v7 on v5

--- a/solution.py
+++ b/solution.py
@@ -139,7 +139,7 @@
     )(*arrays)
 
 
-def plane_kernel(z_ref, own_a_ref, own_b_ref, w_up_ref, w_down_ref, sent_a_ref, sent_b_ref, kept_ref):
+def plane_kernel(z_ref, own_a_ref, own_b_ref, w_down_ref, w_up_ref, sent_a_ref, sent_b_ref, kept_ref):
     half, rows = own_a_ref.shape[1:3]
     stripe = rows // Z
     even = z_ref[0] % 2 == 0
@@ -162,7 +162,7 @@
         lax.fori_loop(0, half // 2, add, 0, unroll=2)
 
 
-def plane_sum(z, own_a, own_b, w_up, w_down):
+def plane_sum(z, own_a, own_b, w_down, w_up):
     half, rows, columns = own_a.shape[1:]
     count = half * rows // Z
     sent = pltpu.VMEM((Z // 2, count, columns), jnp.bfloat16)
@@ -173,7 +173,7 @@
         out_specs=[IN_VMEM] * 3,
         compiler_params=PARAMS,
         name="plane_sum",
-    )(z, own_a, own_b, w_up, w_down)
+    )(z, own_a, own_b, w_down, w_up)
 
 
 def parity_kernel(z_ref, kept_ref, a_ref, b_ref, far_ref, outer_ref, inner_ref, own_ref):
@@ -359,14 +359,13 @@
     (w1a,) = add_parts(
         [[(0, 0, 0, n), (1, 0, 0, n), (2, 0, 0, n)]], (kept_up, near_up, from_down), jnp.bfloat16, "relay_up"
     )
-    w1a, kept_down = lax.optimization_barrier((w1a, kept_down))
     (w3b,) = add_parts(
         [[(0, 0, n, n), (1, 0, n, n), (2, 0, 0, n)]], (kept_down, near_down, from_up), jnp.bfloat16, "relay_down"
     )
     w_up, w_down = up(w1a), down(w3b)
     own_a, own_b = own_sum(local_grads, core, y, own, v_up, v_down)
     own_a, own_b, chosen, band = lax.optimization_barrier((own_a, own_b, chosen, band))
-    sent_a, sent_b, kept = plane_sum(z, own_a, own_b, w_up, w_down)
+    sent_a, sent_b, kept = plane_sum(z, own_a, own_b, w_down, w_up)
     got_a = lax.ppermute(sent_a, "z", [(i, i ^ 1) for i in range(Z)])
     got_b = lax.ppermute(sent_b, "z", [(i, (i - 1 + 2 * (i % 2)) % Z) for i in range(Z)])
     *sent, own = parity_sum(z, kept, got_a, got_b)

time: 89.9 us -> 89.9 us (level)
    ppermute x3, waiting for transfers between devices: 3.85 us -> 8.13 us  [up(): return lax.ppermute(value, 'y', [(i, (i + 1) % Y) for i in range(Y)])]
    ppermute x3, waiting for transfers between devices: 4.64 us -> 0.9 us  [down(): return lax.ppermute(value, 'y', [(i, (i - 1) % Y) for i in range(Y)])]
    ppermute x3, waiting for transfers between devices: 5.07 us -> 3.89 us  [on_device(): lax.ppermute(value, 'z', [(i, i ^ change) for i in range(Z)])]
where the time goes in v7:
time: 89.9 us; the launch traced here: 88.4 us
  starting transfers between devices  30.2 us (34%)
  waiting for transfers between devices  25.6 us (28%)
  blocking collectives  18.1 us (20%)
  Pallas kernels  13.4 us (15%)
    all_to_all x1, blocking collectives, on_device(): lax.all_to_all(outgoing, ('z', 'y'), split_axis=0, concat_axis=0, tiled=T...  18.1 us
    ppermute x4, waiting for transfers between devices, along(): return lax.ppermute(value, 'mp', list(enumerate(to)))  9.39 us
    ppermute x5, starting transfers between devices, swap(): return lax.ppermute(value, 'core', [(0, 1), (1, 0)])  8.4 us
    ppermute x3, waiting for transfers between devices, up(): return lax.ppermute(value, 'y', [(i, (i + 1) % Y) for i in range(Y)])  8.13 us
    pallas_call x1, Pallas kernels, on_device(): pl.pallas_call(precondition_kernel, out_shape=(result, result), in_specs=...  5.87 us
    ppermute x3, starting transfers between devices, on_device(): lax.ppermute(value, 'z', [(i, i ^ change) for i in range(Z)])  5.74 us
    ppermute x3, starting transfers between devices, down(): return lax.ppermute(value, 'y', [(i, (i - 1) % Y) for i in range(Y)])  5.41 us
    ppermute x1, starting transfers between devices, on_device(): lax.ppermute(sent_b, 'z', [(i, (i - 1 + 2 * (i % 2)) % Z) for i in range(...  4.67 us
  transfers between devices with their start and end apart: 20, of which 11 were waited for; matrix products, arithmetic and copies ran while one was open for 1% of the time, Pallas kernels for 5%

profile of v7, /device:TPU:1, one launch (start us, length us, event | category | flops | bytes accessed | tf_op | source)
XLA Modules:
  0.0 88.4 jit_solution(8363285079119814059)
XLA Ops:
  0.0 1.5 %sent.1 = (bf16[1,32,64,128]{3,2,1,0:T(8,128)(2,1)S(1)}, bf16[1,32,64,128]{3,2,1,0:T(8,128)(2,1)S(1)}, bf16[1,32,64,128]{3,2,1,0:T(8,128)(2,1)S(1)}) custom-call(s32[1]{0:T(128)} %bitcast.core_ref, s32[1]{0:T(128)} %bitcast.1.y_ref, bf16[32,512,128]{2,1,0:T(8,128)(2,1)} %bitcast.7), custom_call_target="tpu_custom_call" | custom-call | tf_op jit(solution)/shard_map/sent/pallas_call | solution.py:71
  1.6 3.3 %collective-permute-start.5 = (bf16[1,32,64,128]{3,2,1,0:T(8,128)(2,1)S(1)}, bf16[1,32,64,128]{3,2,1,0:T(8,128)(2,1)S(1)}, u32[]{:S(2)}, u32[]{:S(2)}) collective-permute-start(bf16[1,32,64,128]{3,2,1,0:T(8,128)(2,1)S(1)} %get-tuple-element.46), channel_id=1, source_target_pairs={{0,4},{4,0},{1,5},{5,1},{2,6},{6,2},{3,7},{7,3},{8,12},{12,8},{9,1... | collective-permute-start | bytes 1572872 | tf_op jit(solution)/shard_map/ppermute | solution.py:332
  5.4 1.5 %kept.1 = (bf16[1,32,64,128]{3,2,1,0:T(8,128)(2,1)S(1)}, bf16[1,32,64,128]{3,2,1,0:T(8,128)(2,1)S(1)}, bf16[1,32,64,128]{3,2,1,0:T(8,128)(2,1)S(1)}) custom-call(s32[1]{0:T(128)} %bitcast.core_ref, s32[1]{0:T(128)} %bitcast.1.y_ref, bf16[32,512,128]{2,1,0:T(8,128)(2,1)} %bitcast.8), custom_call_target="tpu_custom_call" | custom-call | tf_op jit(solution)/shard_map/kept/pallas_call | solution.py:71
  7.4 2.7 %collective-permute-start.6 = (bf16[1,16,64,128]{3,2,1,0:T(8,128)(2,1)S(1)}, bf16[1,16,64,128]{3,2,1,0:T(8,128)(2,1)S(1)}, u32[]{:S(2)}, u32[]{:S(2)}) collective-permute-start(bf16[1,16,64,128]{3,2,1,0:T(8,128)(2,1)S(1)} %get-tuple-element.47), channel_id=1, source_target_pairs={{0,24},{8,0},{16,8},{24,16},{1,25},{9,1},{17,9},{25,17},{2,26},{10... | collective-permute-start | bytes 786440 | tf_op jit(solution)/shard_map/ppermute | solution.py:338
  10.3 1.1 %own_piece.1 = bf16[1,32,64,128]{3,2,1,0:T(8,128)(2,1)S(1)} custom-call(s32[1]{0:T(128)} %bitcast.core_ref, s32[1]{0:T(128)} %bitcast.1.y_ref, bf16[32,512,128]{2,1,0:T(8,128)(2,1)} %bitcast.9), custom_call_target="tpu_custom_call" | custom-call | tf_op jit(solution)/shard_map/own_piece/pallas_call | solution.py:71
  12.2 1.5 %collective-permute-start.3 = (bf16[1,16,64,128]{3,2,1,0:T(8,128)(2,1)S(1)}, bf16[1,16,64,128]{3,2,1,0:T(8,128)(2,1)S(1)}, u32[]{:S(2)}, u32[]{:S(2)}) collective-permute-start(bf16[1,16,64,128]{3,2,1,0:T(8,128)(2,1)S(1)} %near_up.1), channel_id=1, source_target_pairs={{0,8},{8,16},{16,24},{24,0},{1,9},{9,17},{17,25},{25,1},{2,10},{10... | collective-permute-start | bytes 786440 | tf_op jit(solution)/shard_map/ppermute | solution.py:335
  13.7 2.8 %collective-permute-done.8.refs_2_ = bf16[1,16,64,128]{3,2,1,0:T(8,128)(2,1)S(1)} collective-permute-done((bf16[1,16,64,128]{3,2,1,0:T(8,128)(2,1)S(1)}, bf16[1,16,64,128]{3,2,1,0:T(8,128)(2,1)S(1)}, u32[]{:S(2)}, u32[]{:S(2)}) %collective-permute-start.8) | collective-permute-done | bytes 262176 | tf_op jit(solution)/shard_map/ppermute | solution.py:335
  16.8 2.7 %collective-permute-start.7 = (bf16[1,16,64,128]{3,2,1,0:T(8,128)(2,1)S(1)}, bf16[1,16,64,128]{3,2,1,0:T(8,128)(2,1)S(1)}, u32[]{:S(2)}, u32[]{:S(2)}) collective-permute-start(bf16[1,16,64,128]{3,2,1,0:T(8,128)(2,1)S(1)} %relay_down.1), channel_id=1, source_target_pairs={{0,24},{8,0},{16,8},{24,16},{1,25},{9,1},{17,9},{25,17},{2,26},{10... | collective-permute-start | bytes 786440 | tf_op jit(solution)/shard_map/ppermute | solution.py:338
  21.0 1.1 %collective-permute-done.3.v_up_ref = bf16[1,16,64,128]{3,2,1,0:T(8,128)(2,1)S(1)} collective-permute-done((bf16[1,16,64,128]{3,2,1,0:T(8,128)(2,1)S(1)}, bf16[1,16,64,128]{3,2,1,0:T(8,128)(2,1)S(1)}, u32[]{:S(2)}, u32[]{:S(2)}) %collective-permute-start.3) | collective-permute-done | bytes 262176 | tf_op jit(solution)/shard_map/ppermute | solution.py:335
  22.1 1.3 %own_sum.1 = (f32[1,16,64,128]{3,2,1,0:T(8,128)S(1)}, f32[1,16,64,128]{3,2,1,0:T(8,128)S(1)}) custom-call(s32[1]{0:T(128)} %bitcast.core_ref, s32[1]{0:T(128)} %bitcast.1.y_ref, bf16[32,512,128]{2,1,0:T(8,128)(2,1)} %bitcast.10, bf16[1,32,64,128]{3,2,1,0:T(8,128)(2,1)S(1)} %collective-permute-done.2.got_ref, ...), custom_call_target="tpu_custom_call" | custom-call | tf_op jit(solution)/shard_map/own_sum/pallas_call | solution.py:103
  23.4 4.3 %collective-permute-done.9.w_up_ref = bf16[1,16,64,128]{3,2,1,0:T(8,128)(2,1)S(1)} collective-permute-done((bf16[1,16,64,128]{3,2,1,0:T(8,128)(2,1)S(1)}, bf16[1,16,64,128]{3,2,1,0:T(8,128)(2,1)S(1)}, u32[]{:S(2)}, u32[]{:S(2)}) %collective-permute-start.9) | collective-permute-done | bytes 262176 | tf_op jit(solution)/shard_map/ppermute | solution.py:335
  28.3 4.7 %collective-permute-start.11 = (bf16[4,128,128]{2,1,0:T(8,128)(2,1)S(1)}, bf16[4,128,128]{2,1,0:T(8,128)(2,1)S(1)}, u32[]{:S(2)}, u32[]{:S(2)}) collective-permute-start(bf16[4,128,128]{2,1,0:T(8,128)(2,1)S(1)} %get-tuple-element.52), channel_id=1, source_target_pairs={{0,224},{32,64},{64,32},{96,128},{128,96},{160,192},{192,160},{224... | collective-permute-start | bytes 393224 | tf_op jit(solution)/shard_map/ppermute | solution.py:370
  32.9 2.4 %collective-permute-done.11.b_ref = bf16[4,128,128]{2,1,0:T(8,128)(2,1)S(1)} collective-permute-done((bf16[4,128,128]{2,1,0:T(8,128)(2,1)S(1)}, bf16[4,128,128]{2,1,0:T(8,128)(2,1)S(1)}, u32[]{:S(2)}, u32[]{:S(2)}) %collective-permute-start.11) | collective-permute-done | bytes 131104 | tf_op jit(solution)/shard_map/ppermute | solution.py:370
  35.3 4.1 %collective-permute-start.12 = (bf16[256,128]{1,0:T(8,128)(2,1)S(1)}, bf16[256,128]{1,0:T(8,128)(2,1)S(1)}, u32[]{:S(2)}, u32[]{:S(2)}) collective-permute-start(bf16[256,128]{1,0:T(8,128)(2,1)S(1)} %get-tuple-element.54), channel_id=1, source_target_pairs={{0,128},{32,160},{64,192},{96,224},{128,0},{160,32},{192,64},{224,... | collective-permute-start | bytes 196616 | tf_op jit(solution)/shard_map/ppermute | solution.py:373
  39.4 1.6 %collective-permute-start.14 = (bf16[256,128]{1,0:T(8,128)(2,1)S(1)}, bf16[256,128]{1,0:T(8,128)(2,1)S(1)}, u32[]{:S(2)}, u32[]{:S(2)}) collective-permute-start(bf16[256,128]{1,0:T(8,128)(2,1)S(1)} %get-tuple-element.56), channel_id=1, source_target_pairs={{0,64},{32,96},{64,0},{96,32},{128,192},{160,224},{192,128},{224,1... | collective-permute-start | bytes 196616 | tf_op jit(solution)/shard_map/ppermute | solution.py:373
  41.1 1.4 %collective-permute-done.12.refs_0_ = bf16[256,128]{1,0:T(8,128)(2,1)S(1)} collective-permute-done((bf16[256,128]{1,0:T(8,128)(2,1)S(1)}, bf16[256,128]{1,0:T(8,128)(2,1)S(1)}, u32[]{:S(2)}, u32[]{:S(2)}) %collective-permute-start.12) | collective-permute-done | bytes 65568 | tf_op jit(solution)/shard_map/ppermute | solution.py:373
  42.4 2.5 %collective-permute-done.13.refs_1_ = bf16[256,128]{1,0:T(8,128)(2,1)S(1)} collective-permute-done((bf16[256,128]{1,0:T(8,128)(2,1)S(1)}, bf16[256,128]{1,0:T(8,128)(2,1)S(1)}, u32[]{:S(2)}, u32[]{:S(2)}) %collective-permute-start.13) | collective-permute-done | bytes 65568 | tf_op jit(solution)/shard_map/ppermute | solution.py:373
  45.0 3.8 %collective-permute-start.15 = (bf16[256,128]{1,0:T(8,128)(2,1)S(1)}, bf16[256,128]{1,0:T(8,128)(2,1)S(1)}, u32[]{:S(2)}, u32[]{:S(2)}) collective-permute-start(bf16[256,128]{1,0:T(8,128)(2,1)S(1)} %mean_rows.1.mine_ref), channel_id=1, source_target_pairs={{0,4},{4,0},{1,5},{5,1},{2,6},{6,2},{3,7},{7,3},{8,12},{12,8},{9,1... | collective-permute-start | bytes 196616 | tf_op jit(solution)/shard_map/ppermute | solution.py:332
  50.2 18.1 %all_to_all.5.in_ref = bf16[32,2,16,128]{3,2,1,0:T(8,128)(2,1)S(1)} all-to-all(bf16[32,2,16,128]{3,2,1,0:T(8,128)(2,1)S(1)} %bitcast.6), channel_id=1, replica_groups=mesh['z'=8,'y'=4,'core'=2,'mp'=4] {'z','y'}, dimensions={0} | all-to-all | bytes 524288 | tf_op jit(solution)/shard_map/all_to_all | solution.py:378
  68.3 3.0 %collective-permute-start.16 = (bf16[512,128]{1,0:T(8,128)(2,1)S(1)}, bf16[512,128]{1,0:T(8,128)(2,1)S(1)}, u32[]{:S(2)}, u32[]{:S(2)}) collective-permute-start(bf16[512,128]{1,0:T(8,128)(2,1)S(1)} %get-tuple-element.57.own_ref), channel_id=1, source_target_pairs={{0,2},{1,3},{2,0},{3,1},{4,6},{5,7},{6,4},{7,5},{8,10},{9,11},{10,... | collective-permute-start | bytes 393224 | tf_op jit(solution)/shard_map/ppermute | solution.py:341
  72.2 1.7 %collective-permute-done.16.same_ref = bf16[512,128]{1,0:T(8,128)(2,1)S(1)} collective-permute-done((bf16[512,128]{1,0:T(8,128)(2,1)S(1)}, bf16[512,128]{1,0:T(8,128)(2,1)S(1)}, u32[]{:S(2)}, u32[]{:S(2)}) %collective-permute-start.16) | collective-permute-done | bytes 131104 | tf_op jit(solution)/shard_map/ppermute | solution.py:341
  73.9 3.8 %collective-permute-done.17.outer_ref = bf16[512,128]{1,0:T(8,128)(2,1)S(1)} collective-permute-done((bf16[512,128]{1,0:T(8,128)(2,1)S(1)}, bf16[512,128]{1,0:T(8,128)(2,1)S(1)}, u32[]{:S(2)}, u32[]{:S(2)}) %collective-permute-start.17) | collective-permute-done | bytes 131104 | tf_op jit(solution)/shard_map/ppermute | solution.py:341
  77.7 5.9 %precondition.1 = (bf16[512,128]{1,0:T(8,128)(2,1)S(1)}, bf16[512,128]{1,0:T(8,128)(2,1)S(1)}) custom-call(bf16[512,128]{1,0:T(8,128)(2,1)S(1)} %collective-permute-done.16.same_ref, bf16[512,128]{1,0:T(8,128)(2,1)S(1)} %collective-permute-done.17.outer_ref, bf16[512,128]{1,0:T(8,128)(2,1)S(1)} %collective-permute-done.18.partner_ref, ...), custom_call_target="tpu_custom_call" | custom-call | tf_op jit(solution)/shard_map/precondition/pallas_call | solution.py:385
  83.7 3.8 %collective-permute-done.19.taken_ref = bf16[512,128]{1,0:T(8,128)(2,1)S(1)} collective-permute-done((bf16[512,128]{1,0:T(8,128)(2,1)S(1)}, bf16[512,128]{1,0:T(8,128)(2,1)S(1)}, u32[]{:S(2)}, u32[]{:S(2)}) %collective-permute-start.19) | collective-permute-done | bytes 131104 | tf_op jit(solution)/shard_map/ppermute | solution.py:341
  (41 shorter events, 7.4 us)
Async XLA Ops:
  1.6 5.6 %collective-permute-start.5 = (bf16[1,32,64,128]{3,2,1,0:T(8,128)(2,1)S(1)}, bf16[1,32,64,128]{3,2,1,0:T(8,128)(2,1)S(1)}, u32[]{:S(2)}, u32[]{:S(2)}) collective-permute-start(bf16[1,32,64,128]{3,2,1,0:T(8,128)(2,1)S(1)} %get-tuple-element.46), channel_id=1, source_target_pairs={{0,4},{4,0},{1,5},{5,1},{2,6},{6,2},{3,7},{7,3},{8,12},{12,8},{9,1... | collective-permute-start | bytes 1572872 | tf_op jit(solution)/shard_map/ppermute | solution.py:332
  4.9 5.2 %collective-permute-start.1 = (bf16[1,32,64,128]{3,2,1,0:T(8,128)(2,1)S(1)}, bf16[1,32,64,128]{3,2,1,0:T(8,128)(2,1)S(1)}, u32[]{:S(2)}, u32[]{:S(2)}) collective-permute-start(bf16[1,32,64,128]{3,2,1,0:T(8,128)(2,1)S(1)} %get-tuple-element.36), channel_id=1, source_target_pairs={{0,4},{4,0},{1,5},{5,1},{2,6},{6,2},{3,7},{7,3},{8,12},{12,8},{9,1... | collective-permute-start | bytes 1572872 | tf_op jit(solution)/shard_map/ppermute | solution.py:332
  5.0 2.0 %copy-start = (s32[32]{0:T(128)S(1)}, s32[32]{0:T(128)}, u32[]{:S(2)}) copy-start(s32[32]{0:T(128)} %param.3) | copy-start | bytes 388
  5.0 5.2 %collective-permute-start = (bf16[1,32,64,128]{3,2,1,0:T(8,128)(2,1)S(1)}, bf16[1,32,64,128]{3,2,1,0:T(8,128)(2,1)S(1)}, u32[]{:S(2)}, u32[]{:S(2)}) collective-permute-start(bf16[1,32,64,128]{3,2,1,0:T(8,128)(2,1)S(1)} %get-tuple-element.35), channel_id=1, source_target_pairs={{0,4},{4,0},{1,5},{5,1},{2,6},{6,2},{3,7},{7,3},{8,12},{12,8},{9,1... | collective-permute-start | bytes 1572872 | tf_op jit(solution)/shard_map/ppermute | solution.py:332
  7.3 9.2 %collective-permute-start.8 = (bf16[1,16,64,128]{3,2,1,0:T(8,128)(2,1)S(1)}, bf16[1,16,64,128]{3,2,1,0:T(8,128)(2,1)S(1)}, u32[]{:S(2)}, u32[]{:S(2)}) collective-permute-start(bf16[1,16,64,128]{3,2,1,0:T(8,128)(2,1)S(1)} %get-tuple-element.49), channel_id=1, source_target_pairs={{0,8},{8,16},{16,24},{24,0},{1,9},{9,17},{17,25},{25,1},{2,10},{10... | collective-permute-start | bytes 786440 | tf_op jit(solution)/shard_map/ppermute | solution.py:335
  7.4 9.3 %collective-permute-start.6 = (bf16[1,16,64,128]{3,2,1,0:T(8,128)(2,1)S(1)}, bf16[1,16,64,128]{3,2,1,0:T(8,128)(2,1)S(1)}, u32[]{:S(2)}, u32[]{:S(2)}) collective-permute-start(bf16[1,16,64,128]{3,2,1,0:T(8,128)(2,1)S(1)} %get-tuple-element.47), channel_id=1, source_target_pairs={{0,24},{8,0},{16,8},{24,16},{1,25},{9,1},{17,9},{25,17},{2,26},{10... | collective-permute-start | bytes 786440 | tf_op jit(solution)/shard_map/ppermute | solution.py:338
  11.4 10.6 %collective-permute-start.2 = (bf16[1,32,64,128]{3,2,1,0:T(8,128)(2,1)S(1)}, bf16[1,32,64,128]{3,2,1,0:T(8,128)(2,1)S(1)}, u32[]{:S(2)}, u32[]{:S(2)}) collective-permute-start(bf16[1,32,64,128]{3,2,1,0:T(8,128)(2,1)S(1)} %own_piece.1), channel_id=1, source_target_pairs={{0,4},{4,0},{1,5},{5,1},{2,6},{6,2},{3,7},{7,3},{8,12},{12,8},{9,1... | collective-permute-start | bytes 1572872 | tf_op jit(solution)/shard_map/ppermute | solution.py:332
  12.2 8.8 %collective-permute-start.4 = (bf16[1,16,64,128]{3,2,1,0:T(8,128)(2,1)S(1)}, bf16[1,16,64,128]{3,2,1,0:T(8,128)(2,1)S(1)}, u32[]{:S(2)}, u32[]{:S(2)}) collective-permute-start(bf16[1,16,64,128]{3,2,1,0:T(8,128)(2,1)S(1)} %near_down.1), channel_id=1, source_target_pairs={{0,24},{8,0},{16,8},{24,16},{1,25},{9,1},{17,9},{25,17},{2,26},{10... | collective-permute-start | bytes 786440 | tf_op jit(solution)/shard_map/ppermute | solution.py:338
  12.2 9.9 %collective-permute-start.3 = (bf16[1,16,64,128]{3,2,1,0:T(8,128)(2,1)S(1)}, bf16[1,16,64,128]{3,2,1,0:T(8,128)(2,1)S(1)}, u32[]{:S(2)}, u32[]{:S(2)}) collective-permute-start(bf16[1,16,64,128]{3,2,1,0:T(8,128)(2,1)S(1)} %near_up.1), channel_id=1, source_target_pairs={{0,8},{8,16},{16,24},{24,0},{1,9},{9,17},{17,25},{25,1},{2,10},{10... | collective-permute-start | bytes 786440 | tf_op jit(solution)/shard_map/ppermute | solution.py:335
  16.6 11.1 %collective-permute-start.9 = (bf16[1,16,64,128]{3,2,1,0:T(8,128)(2,1)S(1)}, bf16[1,16,64,128]{3,2,1,0:T(8,128)(2,1)S(1)}, u32[]{:S(2)}, u32[]{:S(2)}) collective-permute-start(bf16[1,16,64,128]{3,2,1,0:T(8,128)(2,1)S(1)} %relay_up.1), channel_id=1, source_target_pairs={{0,8},{8,16},{16,24},{24,0},{1,9},{9,17},{17,25},{25,1},{2,10},{10... | collective-permute-start | bytes 786440 | tf_op jit(solution)/shard_map/ppermute | solution.py:335
  16.8 10.9 %collective-permute-start.7 = (bf16[1,16,64,128]{3,2,1,0:T(8,128)(2,1)S(1)}, bf16[1,16,64,128]{3,2,1,0:T(8,128)(2,1)S(1)}, u32[]{:S(2)}, u32[]{:S(2)}) collective-permute-start(bf16[1,16,64,128]{3,2,1,0:T(8,128)(2,1)S(1)} %relay_down.1), channel_id=1, source_target_pairs={{0,24},{8,0},{16,8},{24,16},{1,25},{9,1},{17,9},{25,17},{2,26},{10... | collective-permute-start | bytes 786440 | tf_op jit(solution)/shard_map/ppermute | solution.py:338
  27.9 5.0 %collective-permute-start.10 = (bf16[4,128,128]{2,1,0:T(8,128)(2,1)S(1)}, bf16[4,128,128]{2,1,0:T(8,128)(2,1)S(1)}, u32[]{:S(2)}, u32[]{:S(2)}) collective-permute-start(bf16[4,128,128]{2,1,0:T(8,128)(2,1)S(1)} %get-tuple-element.51), channel_id=1, source_target_pairs={{0,32},{32,0},{64,96},{96,64},{128,160},{160,128},{192,224},{224,1... | collective-permute-start | bytes 393224 | tf_op jit(solution)/shard_map/ppermute | solution.py:369
  28.3 7.0 %collective-permute-start.11 = (bf16[4,128,128]{2,1,0:T(8,128)(2,1)S(1)}, bf16[4,128,128]{2,1,0:T(8,128)(2,1)S(1)}, u32[]{:S(2)}, u32[]{:S(2)}) collective-permute-start(bf16[4,128,128]{2,1,0:T(8,128)(2,1)S(1)} %get-tuple-element.52), channel_id=1, source_target_pairs={{0,224},{32,64},{64,32},{96,128},{128,96},{160,192},{192,160},{224... | collective-permute-start | bytes 393224 | tf_op jit(solution)/shard_map/ppermute | solution.py:370
  35.3 7.1 %collective-permute-start.12 = (bf16[256,128]{1,0:T(8,128)(2,1)S(1)}, bf16[256,128]{1,0:T(8,128)(2,1)S(1)}, u32[]{:S(2)}, u32[]{:S(2)}) collective-permute-start(bf16[256,128]{1,0:T(8,128)(2,1)S(1)} %get-tuple-element.54), channel_id=1, source_target_pairs={{0,128},{32,160},{64,192},{96,224},{128,0},{160,32},{192,64},{224,... | collective-permute-start | bytes 196616 | tf_op jit(solution)/shard_map/ppermute | solution.py:373
  39.4 5.5 %collective-permute-start.13 = (bf16[256,128]{1,0:T(8,128)(2,1)S(1)}, bf16[256,128]{1,0:T(8,128)(2,1)S(1)}, u32[]{:S(2)}, u32[]{:S(2)}) collective-permute-start(bf16[256,128]{1,0:T(8,128)(2,1)S(1)} %get-tuple-element.55), channel_id=1, source_target_pairs={{0,192},{32,224},{64,128},{96,160},{128,64},{160,96},{192,0},{224,... | collective-permute-start | bytes 196616 | tf_op jit(solution)/shard_map/ppermute | solution.py:373
  39.4 5.5 %collective-permute-start.14 = (bf16[256,128]{1,0:T(8,128)(2,1)S(1)}, bf16[256,128]{1,0:T(8,128)(2,1)S(1)}, u32[]{:S(2)}, u32[]{:S(2)}) collective-permute-start(bf16[256,128]{1,0:T(8,128)(2,1)S(1)} %get-tuple-element.56), channel_id=1, source_target_pairs={{0,64},{32,96},{64,0},{96,32},{128,192},{160,224},{192,128},{224,1... | collective-permute-start | bytes 196616 | tf_op jit(solution)/shard_map/ppermute | solution.py:373
  45.0 4.7 %collective-permute-start.15 = (bf16[256,128]{1,0:T(8,128)(2,1)S(1)}, bf16[256,128]{1,0:T(8,128)(2,1)S(1)}, u32[]{:S(2)}, u32[]{:S(2)}) collective-permute-start(bf16[256,128]{1,0:T(8,128)(2,1)S(1)} %mean_rows.1.mine_ref), channel_id=1, source_target_pairs={{0,4},{4,0},{1,5},{5,1},{2,6},{6,2},{3,7},{7,3},{8,12},{12,8},{9,1... | collective-permute-start | bytes 196616 | tf_op jit(solution)/shard_map/ppermute | solution.py:332
  68.3 5.6 %collective-permute-start.16 = (bf16[512,128]{1,0:T(8,128)(2,1)S(1)}, bf16[512,128]{1,0:T(8,128)(2,1)S(1)}, u32[]{:S(2)}, u32[]{:S(2)}) collective-permute-start(bf16[512,128]{1,0:T(8,128)(2,1)S(1)} %get-tuple-element.57.own_ref), channel_id=1, source_target_pairs={{0,2},{1,3},{2,0},{3,1},{4,6},{5,7},{6,4},{7,5},{8,10},{9,11},{10,... | collective-permute-start | bytes 393224 | tf_op jit(solution)/shard_map/ppermute | solution.py:341
  71.3 6.4 %collective-permute-start.17 = (bf16[512,128]{1,0:T(8,128)(2,1)S(1)}, bf16[512,128]{1,0:T(8,128)(2,1)S(1)}, u32[]{:S(2)}, u32[]{:S(2)}) collective-permute-start(bf16[512,128]{1,0:T(8,128)(2,1)S(1)} %get-tuple-element.58), channel_id=1, source_target_pairs={{0,3},{1,2},{2,1},{3,0},{4,7},{5,6},{6,5},{7,4},{8,11},{9,10},{10,... | collective-permute-start | bytes 393224 | tf_op jit(solution)/shard_map/ppermute | solution.py:341
  72.1 5.6 %collective-permute-start.18 = (bf16[512,128]{1,0:T(8,128)(2,1)S(1)}, bf16[512,128]{1,0:T(8,128)(2,1)S(1)}, u32[]{:S(2)}, u32[]{:S(2)}) collective-permute-start(bf16[512,128]{1,0:T(8,128)(2,1)S(1)} %get-tuple-element.58), channel_id=1, source_target_pairs={{0,1},{1,0},{2,3},{3,2},{4,5},{5,4},{6,7},{7,6},{8,9},{9,8},{10,11... | collective-permute-start | bytes 393224 | tf_op jit(solution)/shard_map/ppermute | solution.py:341
  83.6 3.9 %collective-permute-start.19 = (bf16[512,128]{1,0:T(8,128)(2,1)S(1)}, bf16[512,128]{1,0:T(8,128)(2,1)S(1)}, u32[]{:S(2)}, u32[]{:S(2)}) collective-permute-start(bf16[512,128]{1,0:T(8,128)(2,1)S(1)} %get-tuple-element.60), channel_id=1, source_target_pairs={{0,1},{1,0},{2,3},{3,2},{4,5},{5,4},{6,7},{7,6},{8,9},{9,8},{10,11... | collective-permute-start | bytes 393224 | tf_op jit(solution)/shard_map/ppermute | solution.py:341
